TPU v7x, 32 devices: a whole 2x2x4 slice. The times are simulated.
32 devices in a mesh: req: 4 (over y, x), kv: 4 (over z), blk: 2 (over core).
Axes of the slice: x: 2, y: 2, z: 4, core: 2. Of those that a mesh axis runs over, the one named last changes fastest.
Arguments:
- x_resid: bfloat16 [4, 256, 5120], P('req', ('kv', 'blk')), may hold values from -54 to 54
- q_new: bfloat16 [4, 256, 2048], P('req', None, 'kv'), may hold values from -36 to 36
- k_new: bfloat16 [4, 256, 512], P('req', None, 'kv'), may hold values from -6 to 12
- v_new: bfloat16 [4, 256, 512], P('req', None, 'kv'), may hold values from -24 to 24
- k_cache: bfloat16 [4, 4, 64, 128, 128], P('req', 'kv', 'blk'), may hold values from -6 to 12
- v_cache: bfloat16 [4, 4, 64, 128, 128], P('req', 'kv', 'blk'), may hold values from -24 to 24
- cache_len: int32 [4], P('req'), may hold values from 1 to 7936, as said below
- page_table: int32 [4, 64], P('req'), may hold values from 0 to 63, as said below
- wo: bfloat16 [2048, 5120], P(('kv', 'blk')), may hold values from -0.125 to 0.125
- norm_gain: bfloat16 [5120], replicated, may hold values from 0.099609375 to 1.8984375
- w_gate: bfloat16 [5120, 7168], P('req', ('kv', 'blk')), may hold values from -0.078125 to 0.078125
- w_up: bfloat16 [5120, 7168], P('req', ('kv', 'blk')), may hold values from -0.078125 to 0.078125
- w_down: bfloat16 [7168, 5120], P(('kv', 'blk'), 'req'), may hold values from -0.0625 to 0.0625
Outputs:
- layer_out: bfloat16 [4, 256, 5120], P('req', ('kv', 'blk'))
- k_cache_out: bfloat16 [4, 4, 64, 128, 128], P('req', 'kv', 'blk')
- v_cache_out: bfloat16 [4, 4, 64, 128, 128], P('req', 'kv', 'blk')
Inputs may be any that keep to these rules, and one draw needn't show every extreme that they name: `cache_len`: at least one request has the largest length. `page_table`: each row is a permutation of 0 to 63.
All inputs are finite; a program needn't handle non-finite values.
Results may differ from a plain program's by a relative error of at most 0.0095.
Values may be sent and summed in bfloat16 or wider, within the bound.
No kernel may reach another device: no remote copies, remote signals or barrier semaphores. Data moves between devices by JAX's collectives and lax.ppermute only.
A program may use at most 128 MiB of HBM per device.

v0:
```python
import math

import jax
import jax.numpy as jnp
from jax import lax
from jax.sharding import PartitionSpec as P


def combined_all(part, axis, combine):
    gathered = jax.tree.map(lambda a: lax.all_gather(a, axis), part)

    def take(source):
        return jax.tree.map(lambda a: lax.dynamic_index_in_dim(a, source, 0, False), gathered)

    return lax.fori_loop(
        1, lax.axis_size(axis), lambda source, state: combine(state, take(source)), take(0)
    )


def rotate(field, positions):
    half_width = field.shape[-1] // 2
    pair_index = jnp.arange(half_width, dtype=jnp.float32)
    frequency = jnp.power(1000000.0, -2.0 * pair_index / field.shape[-1])
    angles = positions.astype(jnp.float32)[:, None] * frequency[None, :]
    cosine = jnp.cos(angles)
    sine_part = jnp.sin(angles)
    lower_half = field[..., :half_width]
    upper_half = field[..., half_width:]
    return jnp.concatenate(
        [
            lower_half * cosine - upper_half * sine_part,
            upper_half * cosine + lower_half * sine_part,
        ],
        axis=-1,
    )


def merge_parts(first_part, second_part):
    max_first, total_first, out_first = first_part
    max_second, total_second, out_second = second_part
    overall = jnp.maximum(max_first, max_second)
    factor_first = jnp.exp(max_first - overall)
    factor_second = jnp.exp(max_second - overall)
    return (
        overall,
        factor_first * total_first + factor_second * total_second,
        factor_first[..., None] * out_first + factor_second[..., None] * out_second,
    )


def fetch_down(w_down):
    return lax.all_gather(w_down, "req", axis=1, tiled=True)


def rms_rows(rows, norm_gain):
    return (
        rows
        * lax.rsqrt(jnp.mean(rows * rows, axis=-1, keepdims=True) + 1e-05)
        * norm_gain.astype(jnp.float32)
    ).astype(jnp.bfloat16)


def on_device(
    x_resid,
    q_new,
    k_new,
    v_new,
    k_cache,
    v_cache,
    cache_len,
    page_table,
    wo,
    norm_gain,
    w_gate,
    w_up,
    w_down,
):
    blk_count = lax.axis_size("blk")
    blk_id = lax.axis_index("blk")
    new_tokens = q_new.shape[1]
    head_dim = k_new.shape[2]
    group_size = q_new.shape[2] // head_dim
    slot_count = k_cache.shape[2]
    page_size = k_cache.shape[3]
    page_total = page_table.shape[1]
    length = cache_len[0]
    positions = length + jnp.arange(new_tokens, dtype=jnp.int32)
    query_heads = rotate(
        q_new[0].reshape(new_tokens, group_size, head_dim).astype(jnp.float32).transpose(1, 0, 2),
        positions,
    ).astype(jnp.bfloat16)
    fresh_keys = rotate(k_new[0].astype(jnp.float32), positions).astype(jnp.bfloat16)
    page_ids = jnp.arange(page_total, dtype=jnp.int32)
    physical = blk_id * slot_count + jnp.arange(slot_count, dtype=jnp.int32)
    logical = jnp.sum(
        jnp.where(page_table[0][None, :] == physical[:, None], page_ids[None, :], 0), axis=1
    )
    slot_position = (
        logical[:, None] * page_size + jnp.arange(page_size, dtype=jnp.int32)[None, :]
    ).reshape(slot_count * page_size)
    new_index = slot_position - length
    is_new = (new_index >= 0) & (new_index < new_tokens)
    chosen = jnp.clip(new_index, 0, new_tokens - 1)
    key_rows = jnp.where(
        is_new[:, None], fresh_keys[chosen], k_cache[0, 0].reshape(slot_count * page_size, head_dim)
    )
    value_rows = jnp.where(
        is_new[:, None], v_new[0][chosen], v_cache[0, 0].reshape(slot_count * page_size, head_dim)
    )
    scores = jnp.einsum(
        "qd,sd->qs",
        query_heads.reshape(group_size * new_tokens, head_dim),
        key_rows,
        preferred_element_type=jnp.float32,
    ) * (1.0 / math.sqrt(head_dim))
    scores = scores.reshape(group_size, new_tokens, slot_count * page_size)
    allowed = slot_position[None, None, :] <= positions[None, :, None]
    masked = jnp.where(allowed, scores, -1e30)
    block_max = jnp.max(masked, axis=-1)
    weights = jnp.where(allowed, jnp.exp(masked - block_max[..., None]), 0.0).astype(jnp.bfloat16)
    block_total = jnp.sum(weights.astype(jnp.float32), axis=-1)
    block_out = jnp.einsum("gcs,sd->gcd", weights, value_rows, preferred_element_type=jnp.float32)
    merged = combined_all((block_max, block_total, block_out), "blk", merge_parts)
    attn = (merged[2] / merged[1][..., None]).astype(jnp.bfloat16)
    per_core = group_size // blk_count
    mine = lax.dynamic_slice_in_dim(attn, blk_id * per_core, per_core, 0)
    mine_rows = mine.transpose(1, 0, 2).reshape(new_tokens, per_core * head_dim)
    token_rows = x_resid.shape[1]
    row_start = lax.axis_index(("kv", "blk")) * token_rows
    partial_value = jnp.dot(mine_rows, wo, preferred_element_type=jnp.float32)
    own_part = lax.dynamic_slice_in_dim(partial_value, row_start, token_rows, 0) + x_resid[
        0
    ].astype(jnp.float32)
    contrib = lax.dynamic_update_slice_in_dim(partial_value, own_part, row_start, 0)
    resid = lax.psum(contrib, ("kv", "blk"))
    normed = rms_rows(resid, norm_gain)
    own_resid = lax.dynamic_slice_in_dim(resid, row_start, token_rows, 0)
    gate_val = jnp.dot(
        normed,
        lax.all_gather(w_gate, "req", axis=0, tiled=True),
        preferred_element_type=jnp.float32,
    )
    up_val = jnp.dot(
        normed, lax.all_gather(w_up, "req", axis=0, tiled=True), preferred_element_type=jnp.float32
    )
    hidden = (jax.nn.silu(gate_val) * up_val).astype(jnp.bfloat16)
    down_full = fetch_down(w_down)
    mlp_rows = lax.psum_scatter(
        jnp.dot(hidden, down_full, preferred_element_type=jnp.float32).astype(jnp.bfloat16),
        ("kv", "blk"),
        scatter_dimension=0,
        tiled=True,
    ).astype(jnp.float32)
    layer_out = (own_resid + mlp_rows).astype(jnp.bfloat16)[None]
    return (layer_out, key_rows.reshape(k_cache.shape), value_rows.reshape(v_cache.shape))


def solution(mesh):
    in_specs = (
        P("req", ("kv", "blk"), None),
        P("req", None, "kv"),
        P("req", None, "kv"),
        P("req", None, "kv"),
        P("req", "kv", "blk", None, None),
        P("req", "kv", "blk", None, None),
        P("req"),
        P("req", None),
        P(("kv", "blk"), None),
        P(),
        P("req", ("kv", "blk")),
        P("req", ("kv", "blk")),
        P(("kv", "blk"), "req"),
    )
    out_specs = (
        P("req", ("kv", "blk"), None),
        P("req", "kv", "blk", None, None),
        P("req", "kv", "blk", None, None),
    )
    return jax.shard_map(
        on_device, mesh=mesh, in_specs=in_specs, out_specs=out_specs, check_vma=False
    )
```

profile of v0, /device:TPU:0, one launch (start us, length us, event | category | flops | bytes accessed | tf_op | source)
XLA Modules:
  0.0 437.2 jit_solution(15610051596787295447)
XLA Ops:
  8.9 0.9 copy.31
  10.3 0.8 select_reduce_fusion
  11.4 1.9 reshape.295
  13.3 1.3 copy.30
  14.8 15.0 %gather_fusion = bf16[4096,128]{1,0:T(8,128)(2,1)} fusion(bf16[256,128]{1,0:T(8,128)(2,1)S(1)} %copy.32, s32[4096]{0:T(1024)S(1)} %broadcast_clamp_fusion), kind=kCustom, calls=%fused_computation | custom fusion | bytes 2113536 | tf_op jit(solution)/shard_map/gather | solution.py:105
  29.8 15.0 %gather_fusion.1 = bf16[4096,128]{1,0:T(8,128)(2,1)} fusion(bf16[256,128]{1,0:T(8,128)(2,1)S(1)} %bitcast.87, s32[4096]{0:T(1024)S(1)} %broadcast_clamp_fusion), kind=kCustom, calls=%fused_computation.1 | custom fusion | bytes 2113536 | tf_op jit(solution)/shard_map/gather | solution.py:108
  44.9 0.6 broadcast_compare_fusion
  45.6 3.6 bitcast_select_fusion.2
  49.2 3.7 fusion.1
  52.9 6.7 %convert_reduce_fusion = (f32[1024]{0:T(1024)S(1)}, bf16[1024,4096]{1,0:T(8,128)(2,1)S(1)}) fusion(f32[1024]{0:T(1024)S(1)} %get-tuple-element.46, f32[1024,4096]{1,0:T(8,128)S(1)} %get-tuple-element.47, pred[256,4096]{1,0:T(8,128)(4,1)S(1)} %broadcast_compare_fusion), kind=kLoop, calls=%fused_computation.5 | loop fusion | flops 29359104 | bytes 26222592 | tf_op jit(solution)/shard_map/reduce_sum | solution.py:121
  59.7 1.5 broadcast_select_fusion
  61.2 1.0 copy-done.7
  62.2 3.2 fusion.29
  65.4 1.9 all_gather.32
  67.4 2.0 all_gather.28
  69.4 7.8 %all-gather.12.cloned.1.call-done = f32[8,256,128]{2,1,0:T(8,128)} async-done(((f32[4,256,128]{2,1,0:T(8,128)}), f32[8,256,128]{2,1,0:T(8,128)}) %all-gather.12.cloned.1.call-update) | async-done | bytes 1048592 | tf_op jit(solution)/shard_map/all_gather | solution.py:10
  77.2 1.3 fusion.28
  78.5 0.8 copy.37
  79.6 1.0 divide_convert_fusion
  80.6 3.2 fusion.30
  83.8 2.0 fusion.3
  85.9 0.5 all-gather.6.cloned.1.call-update
  86.5 0.5 all-gather.10.cloned.1.call-update
  87.1 0.5 all-gather.8.cloned.1.call-update
  87.7 115.8 %all-reduce.2.cloned.1.call-done = f32[256,5120]{1,0:T(8,128)} async-done(((f32[256,5120]{1,0:T(8,128)}), f32[256,5120]{1,0:T(8,128)}) %all-reduce.2.cloned.1.call-update) | async-done | bytes 5242896 | tf_op jit(solution)/shard_map/psum | solution.py:135
  203.5 2.9 multiply_reduce_fusion
  206.5 9.1 %fusion.24 = f32[256,896]{1,0:T(8,128)} fusion(bf16[5120,896]{1,0:T(8,128)(2,1)} %all-gather.6.cloned.1.call-done, f32[256,5120]{1,0:T(8,128)} %all-reduce.2.cloned.1.call-done, f32[5120]{0:T(1024)S(1)} %convert_element_type.69, f32[256]{0:T(256)S(1)} %add_rsqrt_fusion), kind=kOutput, calls=%fused_computation.69 | convolution fusion | flops 2352742400 | bytes 15356928 | tf_op jit(solution)/shard_map/dot_general | solution.py:138
  215.6 63.6 %all-gather.10.cloned.1.call-done = bf16[896,5120]{1,0:T(8,128)(2,1)} async-done(((bf16[896,1280]{1,0:T(8,128)(2,1)}), bf16[896,5120]{1,0:T(8,128)(2,1)}) %all-gather.10.cloned.1.call-update) | async-done | bytes 9175056 | tf_op jit(solution)/shard_map/all_gather | solution.py:52
  279.2 95.7 %all-gather.8.cloned.1.call-done = bf16[5120,896]{1,0:T(8,128)(2,1)} async-done(((bf16[1280,896]{1,0:T(8,128)(2,1)}), bf16[5120,896]{1,0:T(8,128)(2,1)}) %all-gather.8.cloned.1.call-update) | async-done | bytes 9175056 | tf_op jit(solution)/shard_map/all_gather | solution.py:144
  374.9 15.3 %convolution_convert_fusion = bf16[256,5120]{1,0:T(8,128)(2,1)} fusion(bf16[896,5120]{1,0:T(8,128)(2,1)} %all-gather.10.cloned.1.call-done, bf16[5120,896]{1,0:T(8,128)(2,1)} %all-gather.8.cloned.1.call-done, f32[256,896]{1,0:T(8,128)} %fusion.24, f32[256,5120]{1,0:T(8,128)} %all-reduce.2.cloned.1.call-done, f32[5120]{0:T(1024)S(1)} %convert_element_type.69, ...), kind=kOutput, calls=%fused_computation.7 | convolution fusion | flops 4704239616 | bytes 27153408 | tf_op jit(solution)/shard_map/dot_general | solution.py:149
  390.2 37.7 %reduce-scatter.2.cloned.1.call-done = bf16[32,5120]{1,0:T(8,128)(2,1)} async-done(((bf16[256,5120]{1,0:T(8,128)(2,1)}), bf16[32,5120]{1,0:T(8,128)(2,1)}) %reduce-scatter.2.cloned.1.call-update) | async-done | bytes 327696 | tf_op jit(solution)/shard_map/reduce_scatter | solution.py:148
  427.9 2.0 fusion.5
  (56 shorter events, 1.5 us)
Async XLA Ops:
  8.0 72.6 %copy-start = (bf16[256,5120]{1,0:T(8,128)(2,1)S(1)}, bf16[256,5120]{1,0:T(8,128)(2,1)}, u32[]{:S(2)}) copy-start(bf16[256,5120]{1,0:T(8,128)(2,1)} %param.21) | copy-start | bytes 7864324
  8.0 69.2 %all-gather.12.cloned.1.call-start = ((), (), s32[]{:S(2)}) async-start(), calls=%async_computation.6 | async-start | bytes 1572864 | tf_op jit(solution)/shard_map/all_gather | solution.py:10
  14.6 15.2 %copy-start.2 = (bf16[1,256,128]{2,1,0:T(8,128)(2,1)S(1)}, bf16[1,256,128]{2,1,0:T(8,128)(2,1)}, u32[]{:S(2)}) copy-start(bf16[1,256,128]{2,1,0:T(8,128)(2,1)} %param.16) | copy-start | bytes 196612
  52.9 6.8 %copy-start.3 = (bf16[4096,128]{1,0:T(8,128)(2,1)S(1)}, bf16[4096,128]{1,0:T(8,128)(2,1)}, u32[]{:S(2)}) copy-start(bf16[4096,128]{1,0:T(8,128)(2,1)} %gather_fusion) | copy-start | bytes 3145732
  52.9 6.8 %copy-start.4 = (bf16[4096,128]{1,0:T(8,128)(2,1)S(1)}, bf16[4096,128]{1,0:T(8,128)(2,1)}, u32[]{:S(2)}) copy-start(bf16[4096,128]{1,0:T(8,128)(2,1)} %gather_fusion.1) | copy-start | bytes 3145732
  52.9 6.8 %copy-start.5 = (bf16[1,1,32,128,128]{4,3,2,1,0:T(8,128)(2,1)S(1)}, bf16[1,1,32,128,128]{4,3,2,1,0:T(8,128)(2,1)}, u32[]{:S(2)}) copy-start(bf16[1,1,32,128,128]{4,3,2,1,0:T(8,128)(2,1)} %param.17) | copy-start | bytes 3145732
  52.9 6.8 %copy-start.6 = (bf16[1,1,32,128,128]{4,3,2,1,0:T(8,128)(2,1)S(1)}, bf16[1,1,32,128,128]{4,3,2,1,0:T(8,128)(2,1)}, u32[]{:S(2)}) copy-start(bf16[1,1,32,128,128]{4,3,2,1,0:T(8,128)(2,1)} %param.18) | copy-start | bytes 3145732
  61.2 1.0 copy-start.7
  65.3 138.2 %all-reduce.2.cloned.1.call-start = ((), (), s32[]{:S(2)}) async-start(), calls=%async_computation.1 | async-start | bytes 10485760 | tf_op jit(solution)/shard_map/psum | solution.py:135
  79.5 4.3 copy-start.8
  85.9 1.8 copy-start.9
  85.9 120.6 %all-gather.6.cloned.1.call-start = ((), (), s32[]{:S(2)}) async-start(), calls=%async_computation.2 | async-start | bytes 11468800 | tf_op jit(solution)/shard_map/all_gather | solution.py:140
  86.5 192.7 %all-gather.10.cloned.1.call-start = ((), (), s32[]{:S(2)}) async-start(), calls=%async_computation.4 | async-start | bytes 11468800 | tf_op jit(solution)/shard_map/all_gather | solution.py:52
  87.1 287.8 %all-gather.8.cloned.1.call-start = ((), (), s32[]{:S(2)}) async-start(), calls=%async_computation.3 | async-start | bytes 11468800 | tf_op jit(solution)/shard_map/all_gather | solution.py:144
  87.6 340.2 %reduce-scatter.2.cloned.1.call-start = ((), (), s32[]{:S(2)}) async-start(), calls=%async_computation.5 | async-start | bytes 2949120 | tf_op jit(solution)/shard_map/reduce_scatter | solution.py:148
  374.9 55.0 %copy-start.1 = (bf16[256,5120]{1,0:T(8,128)(2,1)S(1)}, bf16[256,5120]{1,0:T(8,128)(2,1)}, u32[]{:S(2)}) copy-start(bf16[256,5120]{1,0:T(8,128)(2,1)} %param.21) | copy-start | bytes 7864324
Sparse Core Ops, SparseCore 0:
  65.5 11.7 all-gather.11
  86.0 117.4 all-reduce.1
  390.3 37.5 reduce-scatter.1
Sparse Core Ops, SparseCore 1:
  88.2 95.1 all-gather.5
  185.1 94.0 all-gather.9
  280.9 94.0 all-gather.7
where the time goes:
time: 438 us; the launch traced here: 437 us
  waiting for transfers between devices  322 us (74%)
  local copies, waits for them, and re-layouts  37.7 us (9%)
  matrix products  34.5 us (8%)
  other arithmetic  22 us (5%)
  between operations  16.6 us (4%)
    psum x1, waiting for transfers between devices, on_device(): resid = lax.psum(contrib, ('kv', 'blk'))  116 us
    all_gather x1, waiting for transfers between devices, on_device(): lax.all_gather(w_up, 'req', axis=0, tiled=True)  95.7 us
    all_gather x1, waiting for transfers between devices, fetch_down(): return lax.all_gather(w_down, 'req', axis=1, tiled=True)  63.6 us
    reduce_scatter x1, waiting for transfers between devices, on_device(): lax.psum_scatter(jnp.dot(hidden, down_full, preferred_element_type=jnp.fl...  37.7 us
    dot_general x1, matrix products, on_device(): jnp.dot(hidden, down_full, preferred_element_type=jnp.float32)  15.3 us
    gather x1, local copies, waits for them, and re-layouts, on_device(): fresh_keys[chosen]  15 us
    gather x1, local copies, waits for them, and re-layouts, on_device(): v_new[0][chosen]  15 us
    dot_general x1, matrix products, on_device(): jnp.dot(normed, lax.all_gather(w_gate, 'req', axis=0, tiled=True), prefer...  9.09 us
  transfers between devices with their start and end apart: 6, of which 5 were waited for; matrix products, arithmetic and copies ran while one was open for 3% of the time, Pallas kernels for 0%

commit v1 on v0

v1 whole, which is shorter than its diff:
```python
import functools
import math

import jax
import jax.numpy as jnp
import numpy as np
from jax import lax
from jax.experimental import pallas as pl
from jax.experimental.pallas import tpu as pltpu
from jax.sharding import PartitionSpec as P

NEG = -1e30
F32 = jnp.float32
BF16 = jnp.bfloat16
VMEM = pl.BlockSpec(memory_space=pltpu.VMEM)
SMEM = pl.BlockSpec(memory_space=pltpu.SMEM)


def swap(a, axis, mask):
    return lax.ppermute(a, axis, [(i, i ^ mask) for i in range(lax.axis_size(axis))])


def reduce_bits(x, axis, order, last=F32):
    count = x.shape[0]
    left = list(range(count.bit_length() - 1))[::-1]
    x = x.reshape((2,) * len(left) + x.shape[1:])
    for bit in order:
        dim = left.index(bit)
        left.remove(bit)
        kept = lax.index_in_dim(x, 0, dim, False).astype(F32)
        came = swap(lax.index_in_dim(x, 1, dim, False), axis, 1 << bit).astype(F32)
        x = (kept + came).astype(BF16 if left else last)
    return x


def gather_bits(x, axis):
    x = x[None]
    for bit in range(lax.axis_size(axis).bit_length() - 1)[::-1]:
        came = swap(x, axis, 1 << bit)
        x = jnp.stack([x, came], 1).reshape((2 * x.shape[0],) + x.shape[1:])
    return x


def trade(pieces, axis):
    return [pieces[0]] + [swap(piece, axis, j) for j, piece in enumerate(pieces) if j]


def attention_body(shape, scal, table, freq, q_ref, kn_ref, vn_ref, kc_ref, vc_ref,
                   ko_ref, vo_ref, ok_ref, os_ref, sk_ref, ss_ref,
                   inverse, key_pos, q_rot):
    kv_count, chunks, rows = shape
    tokens, head_dim = kn_ref.shape
    slots, page = kc_ref.shape[0], kc_ref.shape[1]
    heads = q_ref.shape[1] // head_dim
    pages = table.shape[1]
    length, kv_id, blk_id = scal[0], scal[1], scal[2]
    head = pl.program_id(0)
    scale = 1.0 / math.sqrt(head_dim)

    @pl.when(head == 0)
    def _():
        @pl.loop(0, pages)
        def _(j):
            inverse[table[0, j]] = j

        lane = lax.broadcasted_iota(jnp.int32, (1, page), 1)
        for s in range(slots):
            key_pos[:, s * page:(s + 1) * page] = inverse[blk_id * slots + s] * page + lane

        where_at = (length + lax.broadcasted_iota(jnp.int32, (tokens, head_dim), 0)).astype(F32)
        angle = where_at * freq[...]
        cosine = jnp.cos(angle)
        sine = jnp.sin(angle)
        low = lax.broadcasted_iota(jnp.int32, (tokens, head_dim), 1) < head_dim // 2
        sine = jnp.where(low, -sine, sine)

        def rotate(u):
            u = u.astype(F32)
            return (u * cosine + pltpu.roll(u, head_dim // 2, 1) * sine).astype(BF16)

        for h in range(heads):
            cols = slice(h * head_dim, (h + 1) * head_dim)
            q_rot[:, cols] = rotate(q_ref[:, cols])
        k_rot = rotate(kn_ref[...])

        ko_ref[...] = kc_ref[...]
        vo_ref[...] = vc_ref[...]
        for extra in range(tokens // page + 1):
            logical = length // page + extra
            slot = table[0, jnp.minimum(logical, pages - 1)] - blk_id * slots

            @pl.when((logical < pages) & (slot >= 0) & (slot < slots))
            def _():
                first = logical * page - length
                at = first + lax.broadcasted_iota(jnp.int32, (page, tokens), 0)
                pick = (at == lax.broadcasted_iota(jnp.int32, (page, tokens), 1)).astype(BF16)
                fresh_k = jnp.dot(pick, k_rot, preferred_element_type=F32).astype(BF16)
                fresh_v = jnp.dot(pick, vn_ref[...], preferred_element_type=F32).astype(BF16)
                at = first + lax.broadcasted_iota(jnp.int32, (page, head_dim), 0)
                is_new = (at >= 0) & (at < tokens)
                ko_ref[slot] = jnp.where(is_new, fresh_k, ko_ref[slot])
                vo_ref[slot] = jnp.where(is_new, fresh_v, vo_ref[slot])

    half = tokens // 2
    span = chunks * rows
    hcol = pl.ds(pl.multiple_of(head * head_dim, head_dim), head_dim)
    keys = ko_ref[...].reshape(slots * page, head_dim)
    values = vo_ref[...].reshape(slots * page, head_dim)
    for side in range(2):
        parts = []
        for c in range(chunks):
            for m in range(kv_count):
                start = ((kv_id ^ m) * 2 + (blk_id ^ side)) * span + c * rows
                parts.append(q_rot[pl.ds(pl.multiple_of(start, rows), rows), hcol])
        queries = jnp.concatenate(parts, 0)
        row = lax.broadcasted_iota(jnp.int32, (half, 1), 0)
        group = row // rows
        token = (((group % kv_count) ^ kv_id) * 2 + (blk_id ^ side)) * span
        token = token + (group // kv_count) * rows + row % rows
        scores = lax.dot_general(queries, keys, (((1,), (1,)), ((), ())), preferred_element_type=F32)
        masked = jnp.where(key_pos[...] <= length + token, scores, NEG)
        top = jnp.maximum(jnp.max(masked, 1, keepdims=True), 0.1 * NEG)
        weights = jnp.exp2((masked - top) * (scale * math.log2(math.e))).astype(BF16)
        total = jnp.sum(weights.astype(F32), 1, keepdims=True)
        out = jnp.dot(weights, values, preferred_element_type=F32)
        some = total > 0.0
        safe = jnp.where(some, total, 1.0)
        out = (out / safe).astype(BF16)
        log_sum = jnp.where(some, top * scale + jnp.log(safe), NEG)
        out_ref, stat_ref = ((ok_ref, sk_ref), (os_ref, ss_ref))[side]
        out_ref[:, hcol] = out
        lane = lax.broadcasted_iota(jnp.int32, (half, head_dim), 1)
        before = jnp.where(head == 0, 0.0, stat_ref[...])
        stat_ref[...] = jnp.where(lane == head, log_sum, before)


def attention(scal, table, q, k_new, v_new, k_cache, v_cache, kv_count, chunks, rows):
    tokens, head_dim = k_new.shape
    width = q.shape[1]
    heads = width // head_dim
    slots, page = k_cache.shape[0], k_cache.shape[1]
    half = tokens // 2
    pair = np.arange(head_dim) % (head_dim // 2)
    freq = jnp.asarray((1e6 ** (-2.0 * pair / head_dim)).astype(np.float32)[None])
    whole = lambda *s: pl.BlockSpec(s, lambda h: (0,) * len(s))
    cache = whole(slots, page, head_dim)
    return pl.pallas_call(
        functools.partial(attention_body, (kv_count, chunks, rows)),
        grid=(heads,),
        in_specs=[SMEM, SMEM, whole(1, head_dim), whole(tokens, width), whole(tokens, head_dim),
                  whole(tokens, head_dim), cache, cache],
        out_specs=[cache, cache, whole(half, width), whole(half, width),
                   whole(half, head_dim), whole(half, head_dim)],
        out_shape=[
            jax.ShapeDtypeStruct(k_cache.shape, BF16),
            jax.ShapeDtypeStruct(v_cache.shape, BF16),
            jax.ShapeDtypeStruct((half, width), BF16),
            jax.ShapeDtypeStruct((half, width), BF16),
            jax.ShapeDtypeStruct((half, head_dim), F32),
            jax.ShapeDtypeStruct((half, head_dim), F32),
        ],
        scratch_shapes=[
            pltpu.SMEM((table.shape[1],), jnp.int32),
            pltpu.VMEM((1, slots * page), jnp.int32),
            pltpu.VMEM((tokens, width), BF16),
        ],
        compiler_params=pltpu.CompilerParams(vmem_limit_bytes=48 * 2**20),
        name="attention",
    )(scal, table, freq, q, k_new, v_new, k_cache, v_cache)


def project_body(blk_ref, o1, o2, s1, s2, wa, wb, out_ref, attn):
    head_dim = s1.shape[1]
    heads = o1.shape[1] // head_dim
    depth = wa.shape[0]
    blk_id = blk_ref[0]

    @pl.when(pl.program_id(0) == 0)
    def _():
        for h in range(heads):
            cols = slice(h * head_dim, (h + 1) * head_dim)
            first, second = s1[:, h:h + 1], s2[:, h:h + 1]
            top = jnp.maximum(first, second)
            f1, f2 = jnp.exp(first - top), jnp.exp(second - top)
            mixed = f1 * o1[:, cols].astype(F32) + f2 * o2[:, cols].astype(F32)
            attn[:, cols] = (mixed / (f1 + f2)).astype(BF16)

    mine = attn[:, pl.ds(pl.multiple_of(blk_id * depth, depth), depth)]
    other = attn[:, pl.ds(pl.multiple_of((1 - blk_id) * depth, depth), depth)]
    out_ref[...] = (
        jnp.dot(mine, wa[...], preferred_element_type=F32)
        + jnp.dot(other, wb[...], preferred_element_type=F32)
    ).astype(BF16)


def project(blk, o1, o2, s1, s2, wa, wb):
    rows, width = o1.shape
    model = wa.shape[1]
    step = model // 4
    fixed = lambda a: pl.BlockSpec(a.shape, lambda n: (0, 0))
    weight = pl.BlockSpec((wa.shape[0], step), lambda n: (0, n))
    return pl.pallas_call(
        project_body,
        grid=(model // step,),
        in_specs=[SMEM, fixed(o1), fixed(o2), fixed(s1), fixed(s2), weight, weight],
        out_specs=pl.BlockSpec((rows, step), lambda n: (0, n)),
        out_shape=jax.ShapeDtypeStruct((rows, model), BF16),
        scratch_shapes=[pltpu.VMEM((rows, width), BF16)],
        compiler_params=pltpu.CompilerParams(vmem_limit_bytes=32 * 2**20),
        name="project",
    )(blk, o1, o2, s1, s2, wa, wb)


def on_device(x_resid, q_new, k_new, v_new, k_cache, v_cache, cache_len, page_table,
              wo, norm_gain, w_gate, w_up, w_down):
    reqs, kvs = lax.axis_size("req"), lax.axis_size("kv")
    req_bits = reqs.bit_length() - 1
    kv_bits = kvs.bit_length() - 1
    req_id = lax.axis_index("req")
    blk_id = lax.axis_index("blk")
    span, model = x_resid.shape[1:]
    part = model // reqs
    rows = 16
    chunks = span // rows
    scal = jnp.stack([cache_len[0], lax.axis_index("kv"), blk_id]).astype(jnp.int32)
    blk = blk_id.astype(jnp.int32)[None]

    wo_far, gate_far, up_far, down_far = (swap(w, "blk", 1) for w in (wo, w_gate, w_up, w_down))
    keys_out, values_out, o_keep, o_send, s_keep, s_send = attention(
        scal, page_table, q_new[0], k_new[0], v_new[0], k_cache[0, 0], v_cache[0, 0],
        kvs, chunks, rows)
    o_came, s_came = swap(o_send, "blk", 1), swap(s_send, "blk", 1)

    gain = norm_gain.astype(F32)
    a_order = list(range(req_bits))
    b_order = a_order[req_bits // 2:] + a_order[:req_bits // 2]
    outs = []
    chunk_rows = kvs * rows
    partial_all = project(blk, o_keep, o_came, s_keep, s_came, wo, wo_far)
    for c in range(chunks):
        partial = partial_all[c * chunk_rows:(c + 1) * chunk_rows].reshape(kvs, rows, model)
        summed = reduce_bits(partial, "kv", range(kv_bits))
        resid = x_resid[0, c * rows:(c + 1) * rows].astype(F32) + summed
        normed = (
            resid * lax.rsqrt(jnp.mean(resid * resid, axis=-1, keepdims=True) + 1e-05) * gain
        ).astype(BF16)
        cut = normed.reshape(rows, reqs, part)
        pieces = [lax.dynamic_index_in_dim(cut, req_id ^ j, 1, False) for j in range(reqs)]
        fed = jnp.stack(trade(pieces, "req"))
        fed = gather_bits(fed, "kv")
        flat = fed.reshape(kvs * reqs * rows, part)

        def hidden_of(gate_w, up_w, order):
            both = jnp.concatenate(
                [jnp.dot(flat, w, preferred_element_type=F32).astype(BF16) for w in (gate_w, up_w)], 1)
            both = both.reshape(kvs, reqs, rows, -1).transpose(1, 0, 2, 3)
            both = reduce_bits(both, "req", order)
            gate, up = jnp.split(both, 2, -1)
            return (jax.nn.silu(gate) * up).astype(BF16)

        near = hidden_of(w_gate, w_up, a_order)
        far = hidden_of(gate_far, up_far, b_order)
        near = jnp.stack(trade([near] * reqs, "req"))
        far = jnp.stack(trade([far] * reqs, "req"))
        down = (
            jnp.dot(near.reshape(reqs * kvs * rows, -1), w_down, preferred_element_type=F32)
            + jnp.dot(far.reshape(reqs * kvs * rows, -1), down_far, preferred_element_type=F32)
        ).astype(BF16)
        down = down.reshape(reqs, kvs, rows, part).transpose(1, 0, 2, 3)
        down = reduce_bits(down, "kv", range(kv_bits), BF16)
        came = jnp.stack(trade([down[j] for j in range(reqs)], "req"))
        mlp = [lax.dynamic_index_in_dim(came, req_id ^ j, 0, False) for j in range(reqs)]
        outs.append((resid + jnp.concatenate(mlp, 1).astype(F32)).astype(BF16))
    layer_out = jnp.concatenate(outs, 0)[None]
    return layer_out, keys_out[None, None], values_out[None, None]


def solution(mesh):
    in_specs = (
        P("req", ("kv", "blk"), None),
        P("req", None, "kv"),
        P("req", None, "kv"),
        P("req", None, "kv"),
        P("req", "kv", "blk", None, None),
        P("req", "kv", "blk", None, None),
        P("req"),
        P("req", None),
        P(("kv", "blk"), None),
        P(),
        P("req", ("kv", "blk")),
        P("req", ("kv", "blk")),
        P(("kv", "blk"), "req"),
    )
    out_specs = (
        P("req", ("kv", "blk"), None),
        P("req", "kv", "blk", None, None),
        P("req", "kv", "blk", None, None),
    )
    return jax.shard_map(
        on_device, mesh=mesh, in_specs=in_specs, out_specs=out_specs, check_vma=False
    )
```

time: 438 us -> 194 us (0.44)
  waiting for transfers between devices: 322 us -> 95.2 us
  starting transfers between devices: 0.25 us -> 49.8 us
  matrix products: 34.5 us -> 10.2 us
  local copies, waits for them, and re-layouts: 37.7 us -> 16.7 us
  other arithmetic: 22 us -> 5.4 us
  between operations: 16.6 us -> 2.06 us
  Pallas kernels: 0 us -> 14.2 us
    all_gather x4 -> x0, waiting for transfers between devices: 167 us -> none  [the longest x1 95.7 us: on_device(): lax.all_gather(w_up, 'req', axis=0, tiled=True)]
    psum x1 -> x0, waiting for transfers between devices: 116 us -> none  [on_device(): resid = lax.psum(contrib, ('kv', 'blk'))]
    ppermute x0 -> x50, waiting for transfers between devices: none -> 95.2 us  [swap(): lax.ppermute(a, axis, [(i, i ^ mask) for i in range(lax.axis_size(axis))])]
    ppermute x0 -> x50, starting transfers between devices: none -> 49.8 us  [swap(): lax.ppermute(a, axis, [(i, i ^ mask) for i in range(lax.axis_size(axis))])]
    reduce_scatter x1 -> x0, waiting for transfers between devices: 37.7 us -> none  [on_device(): lax.psum_scatter(jnp.dot(hidden, down_full, preferred_element_type=jnp.fl...]
    gather x2 -> x0, local copies, waits for them, and re-layouts: 30.1 us -> none  [the longest x1 15 us: on_device(): fresh_keys[chosen]]
    dot_general x5 -> x12, matrix products: 34.5 us -> 10.2 us  [the longest x8 6.76 us: hidden_of(): jnp.dot(flat, w, preferred_element_type=F32).astype(BF16)]
    pallas_call x0 -> x2, Pallas kernels: none -> 14.2 us  [the longest x1 11.9 us: attention(): pl.pallas_call(functools.partial(attention_body, (kv_count, chunks, rows)...]
  transfers between devices with their start and end apart: 6 -> 50, of which waited for: 5 -> 23; matrix products, arithmetic and copies ran while one was open for 3% -> 10% of each run, Pallas kernels for 0% -> 6%
where the time goes in v1:
time: 194 us
  waiting for transfers between devices  95.2 us (49%)
  starting transfers between devices  49.8 us (26%)
  local copies, waits for them, and re-layouts  16.7 us (9%)
  Pallas kernels  14.2 us (7%)
  matrix products  10.2 us (5%)
  other arithmetic  5.4 us (3%)
  between operations  2.06 us (1%)
    ppermute x50, waiting for transfers between devices, swap(): lax.ppermute(a, axis, [(i, i ^ mask) for i in range(lax.axis_size(axis))])  95.2 us
    ppermute x50, starting transfers between devices, swap(): lax.ppermute(a, axis, [(i, i ^ mask) for i in range(lax.axis_size(axis))])  49.8 us
    pallas_call x1, Pallas kernels, attention(): pl.pallas_call(functools.partial(attention_body, (kv_count, chunks, rows)...  11.9 us
    unnamed x41, local copies, waits for them, and re-layouts  10.1 us
    dot_general x8, matrix products, hidden_of(): jnp.dot(flat, w, preferred_element_type=F32).astype(BF16)  6.76 us
  transfers between devices with their start and end apart: 50, of which 23 were waited for; matrix products, arithmetic and copies ran while one was open for 10% of the time, Pallas kernels for 6%

profile of v1, /device:TPU:0, one launch (start us, length us, event | category | flops | bytes accessed | tf_op | source)
XLA Modules:
  0.0 193.6 jit_solution(18392349908208456540)
XLA Ops:
  8.3 11.9 %attention.1 = (bf16[32,128,128]{2,1,0:T(8,128)(2,1)}, bf16[32,128,128]{2,1,0:T(8,128)(2,1)}, bf16[128,512]{1,0:T(8,128)(2,1)S(1)}, bf16[128,512]{1,0:T(8,128)(2...) custom-call(s32[3]{0:T(128)S(1)} %pad_add_fusion.scal, s32[1,64]{1,0:T(1,128)S(1)} %copy-done.6, ...), custom_call_target="tpu_custom_call" | custom-call | tf_op jit(solution)/shard_map/attention/pallas_call | solution.py:147
  21.6 1.7 copy-done
  23.3 2.3 %project.1 = bf16[128,5120]{1,0:T(8,128)(2,1)S(1)} custom-call(s32[1]{0:T(128)} %bitcast.1.blk_ref, bf16[128,512]{1,0:T(8,128)(2,1)S(1)} %get-tuple-element.9.o1, bf16[128,512]{1,0:T(8,128)(2,1)S(1)} %collective-permute-done.o2, f32[128,128]{1,0:T(8,128)S(1)} %get-tuple-element.11.s1, f32[128,128]{1,0:T(8,128)S(1)} %collective-permute-done.1.s2, ...), custom_call_target="tpu_custom_call" | custom-call | tf_op jit(solution)/shard_map/project/pallas_call | solution.py:202
  25.8 3.0 %collective-permute-start.28 = (bf16[2,16,5120]{2,1,0:T(8,128)(2,1)S(1)}, bf16[2,16,5120]{2,1,0:T(8,128)(2,1)S(1)}, u32[]{:S(2)}, u32[]{:S(2)}) collective-permute-start(bf16[2,16,5120]{2,1,0:T(8,128)(2,1)S(1)} %slice_bitcast_fusion.1), channel_id=1, source_target_pairs={{0,2},{2,0},{4,6},{6,4},{1,3},{3,1},{5,7},{7,5},{8,10},{10,8},{12,... | collective-permute-start | bytes 983048 | tf_op jit(solution)/shard_map/ppermute | solution.py:20
  28.9 8.4 %collective-permute-done.28 = bf16[2,16,5120]{2,1,0:T(8,128)(2,1)S(1)} collective-permute-done((bf16[2,16,5120]{2,1,0:T(8,128)(2,1)S(1)}, bf16[2,16,5120]{2,1,0:T(8,128)(2,1)S(1)}, u32[]{:S(2)}, u32[]{:S(2)}) %collective-permute-start.28) | collective-permute-done | bytes 327712 | tf_op jit(solution)/shard_map/ppermute | solution.py:20
  37.4 3.1 %collective-permute-start.29 = (bf16[16,5120]{1,0:T(8,128)(2,1)S(1)}, bf16[16,5120]{1,0:T(8,128)(2,1)S(1)}, u32[]{:S(2)}, u32[]{:S(2)}) collective-permute-start(bf16[16,5120]{1,0:T(8,128)(2,1)S(1)} %slice_bitcast_fusion.15), channel_id=1, source_target_pairs={{0,4},{2,6},{4,0},{6,2},{1,5},{3,7},{5,1},{7,3},{8,12},{10,14},{12... | collective-permute-start | bytes 491528 | tf_op jit(solution)/shard_map/ppermute | solution.py:20
  40.5 6.9 %collective-permute-done.3 = bf16[2,16,5120]{2,1,0:T(8,128)(2,1)S(1)} collective-permute-done((bf16[2,16,5120]{2,1,0:T(8,128)(2,1)S(1)}, bf16[2,16,5120]{2,1,0:T(8,128)(2,1)S(1)}, u32[]{:S(2)}, u32[]{:S(2)}) %collective-permute-start.3) | collective-permute-done | bytes 327712 | tf_op jit(solution)/shard_map/ppermute | solution.py:20
  47.5 1.7 collective-permute-start.4
  49.2 8.6 %collective-permute-done.4 = bf16[16,5120]{1,0:T(8,128)(2,1)S(1)} collective-permute-done((bf16[16,5120]{1,0:T(8,128)(2,1)S(1)}, bf16[16,5120]{1,0:T(8,128)(2,1)S(1)}, u32[]{:S(2)}, u32[]{:S(2)}) %collective-permute-start.4) | collective-permute-done | bytes 163872 | tf_op jit(solution)/shard_map/ppermute | solution.py:20
  59.6 1.6 constant_dynamic-slice_fusion.3
  66.6 1.7 reshape.121
  68.3 1.6 constant_dynamic-slice_fusion.7
  75.5 2.5 %collective-permute-done.7 = bf16[16,1280]{1,0:T(8,128)(2,1)S(1)} collective-permute-done((bf16[16,1280]{1,0:T(8,128)(2,1)S(1)}, bf16[16,1280]{1,0:T(8,128)(2,1)S(1)}, u32[]{:S(2)}, u32[]{:S(2)}) %collective-permute-start.7) | collective-permute-done | bytes 40992 | tf_op jit(solution)/shard_map/ppermute | solution.py:20
  78.0 9.2 %collective-permute-done.33 = bf16[1,4,16,1280]{3,2,1,0:T(8,128)(2,1)S(1)} collective-permute-done((bf16[1,4,16,1280]{3,2,1,0:T(8,128)(2,1)S(1)}, bf16[1,4,16,1280]{3,2,1,0:T(8,128)(2,1)S(1)}, u32[]{:S(2)}, u32[]{:S(2)}) %collective-permute-start.33) | collective-permute-done | bytes 163872 | tf_op jit(solution)/shard_map/ppermute | solution.py:20
  88.0 1.9 collective-permute-done.8
  90.1 7.9 %collective-permute-done.34 = bf16[2,4,16,1280]{3,2,1,0:T(8,128)(2,1)S(1)} collective-permute-done((bf16[2,4,16,1280]{3,2,1,0:T(8,128)(2,1)S(1)}, bf16[2,4,16,1280]{3,2,1,0:T(8,128)(2,1)S(1)}, u32[]{:S(2)}, u32[]{:S(2)}) %collective-permute-start.34) | collective-permute-done | bytes 327712 | tf_op jit(solution)/shard_map/ppermute | solution.py:20
  101.6 2.3 %collective-permute-done.9 = bf16[2,4,16,1280]{3,2,1,0:T(8,128)(2,1)S(1)} collective-permute-done((bf16[2,4,16,1280]{3,2,1,0:T(8,128)(2,1)S(1)}, bf16[2,4,16,1280]{3,2,1,0:T(8,128)(2,1)S(1)}, u32[]{:S(2)}, u32[]{:S(2)}) %collective-permute-start.9) | collective-permute-done | bytes 327712 | tf_op jit(solution)/shard_map/ppermute | solution.py:20
  114.8 6.4 %collective-permute-done.40 = bf16[2,4,16,1792]{3,2,1,0:T(8,128)(2,1)S(1)} collective-permute-done((bf16[2,4,16,1792]{3,2,1,0:T(8,128)(2,1)S(1)}, bf16[2,4,16,1792]{3,2,1,0:T(8,128)(2,1)S(1)}, u32[]{:S(2)}, u32[]{:S(2)}) %collective-permute-start.40) | collective-permute-done | bytes 458784 | tf_op jit(solution)/shard_map/ppermute | solution.py:20
  124.2 6.8 %collective-permute-done.17 = bf16[2,4,16,1792]{3,2,1,0:T(8,128)(2,1)S(1)} collective-permute-done((bf16[2,4,16,1792]{3,2,1,0:T(8,128)(2,1)S(1)}, bf16[2,4,16,1792]{3,2,1,0:T(8,128)(2,1)S(1)}, u32[]{:S(2)}, u32[]{:S(2)}) %collective-permute-start.17) | collective-permute-done | bytes 458784 | tf_op jit(solution)/shard_map/ppermute | solution.py:20
  132.3 3.6 %collective-permute-done.36 = bf16[4,16,1792]{2,1,0:T(8,128)(2,1)S(1)} collective-permute-done((bf16[4,16,1792]{2,1,0:T(8,128)(2,1)S(1)}, bf16[4,16,1792]{2,1,0:T(8,128)(2,1)S(1)}, u32[]{:S(2)}, u32[]{:S(2)}) %collective-permute-start.36) | collective-permute-done | bytes 229408 | tf_op jit(solution)/shard_map/ppermute | solution.py:20
  139.9 1.7 collective-permute-start.39
  144.0 2.2 %collective-permute-done.38 = bf16[4,16,896]{2,1,0:T(8,128)(2,1)S(1)} collective-permute-done((bf16[4,16,896]{2,1,0:T(8,128)(2,1)S(1)}, bf16[4,16,896]{2,1,0:T(8,128)(2,1)S(1)}, u32[]{:S(2)}, u32[]{:S(2)}) %collective-permute-start.38) | collective-permute-done | bytes 114720 | tf_op jit(solution)/shard_map/ppermute | solution.py:20
  150.9 2.1 %collective-permute-done.44 = bf16[4,16,896]{2,1,0:T(8,128)(2,1)S(1)} collective-permute-done((bf16[4,16,896]{2,1,0:T(8,128)(2,1)S(1)}, bf16[4,16,896]{2,1,0:T(8,128)(2,1)S(1)}, u32[]{:S(2)}, u32[]{:S(2)}) %collective-permute-start.44) | collective-permute-done | bytes 114720 | tf_op jit(solution)/shard_map/ppermute | solution.py:20
  153.1 1.7 collective-permute-start.20
  156.7 1.9 collective-permute-start.21
  158.7 3.7 %collective-permute-done.21 = bf16[4,16,896]{2,1,0:T(8,128)(2,1)S(1)} collective-permute-done((bf16[4,16,896]{2,1,0:T(8,128)(2,1)S(1)}, bf16[4,16,896]{2,1,0:T(8,128)(2,1)S(1)}, u32[]{:S(2)}, u32[]{:S(2)}) %collective-permute-start.21) | collective-permute-done | bytes 114720 | tf_op jit(solution)/shard_map/ppermute | solution.py:20
  164.4 6.4 %collective-permute-done.45 = bf16[2,4,16,1280]{3,2,1,0:T(8,128)(2,1)S(1)} collective-permute-done((bf16[2,4,16,1280]{3,2,1,0:T(8,128)(2,1)S(1)}, bf16[2,4,16,1280]{3,2,1,0:T(8,128)(2,1)S(1)}, u32[]{:S(2)}, u32[]{:S(2)}) %collective-permute-start.45) | collective-permute-done | bytes 327712 | tf_op jit(solution)/shard_map/ppermute | solution.py:20
  171.0 3.3 %collective-permute-done.23 = bf16[2,4,16,1280]{3,2,1,0:T(8,128)(2,1)S(1)} collective-permute-done((bf16[2,4,16,1280]{3,2,1,0:T(8,128)(2,1)S(1)}, bf16[2,4,16,1280]{3,2,1,0:T(8,128)(2,1)S(1)}, u32[]{:S(2)}, u32[]{:S(2)}) %collective-permute-start.23) | collective-permute-done | bytes 327712 | tf_op jit(solution)/shard_map/ppermute | solution.py:20
  174.9 7.7 %collective-permute-done.46 = bf16[4,16,1280]{2,1,0:T(8,128)(2,1)S(1)} collective-permute-done((bf16[4,16,1280]{2,1,0:T(8,128)(2,1)S(1)}, bf16[4,16,1280]{2,1,0:T(8,128)(2,1)S(1)}, u32[]{:S(2)}, u32[]{:S(2)}) %collective-permute-start.46) | collective-permute-done | bytes 163872 | tf_op jit(solution)/shard_map/ppermute | solution.py:20
  184.1 2.1 %collective-permute-start.49 = (bf16[16,1280]{1,0:T(8,128)(2,1)S(1)}, bf16[16,1280]{1,0:T(8,128)(2,1)S(1)}, u32[]{:S(2)}, u32[]{:S(2)}) collective-permute-start(bf16[16,1280]{1,0:T(8,128)(2,1)S(1)} %get-tuple-element.52), channel_id=1, source_target_pairs={{0,24},{8,16},{16,8},{24,0},{1,25},{9,17},{17,9},{25,1},{2,26},{10... | collective-permute-start | bytes 122888 | tf_op jit(solution)/shard_map/ppermute | solution.py:20
  187.7 2.1 %collective-permute-start.27 = (bf16[16,1280]{1,0:T(8,128)(2,1)S(1)}, bf16[16,1280]{1,0:T(8,128)(2,1)S(1)}, u32[]{:S(2)}, u32[]{:S(2)}) collective-permute-start(bf16[16,1280]{1,0:T(8,128)(2,1)S(1)} %get-tuple-element.38), channel_id=1, source_target_pairs={{0,24},{8,16},{16,8},{24,0},{1,25},{9,17},{17,9},{25,1},{2,26},{10... | collective-permute-start | bytes 122888 | tf_op jit(solution)/shard_map/ppermute | solution.py:20
  190.5 2.1 %collective-permute-done.27 = bf16[16,1280]{1,0:T(8,128)(2,1)S(1)} collective-permute-done((bf16[16,1280]{1,0:T(8,128)(2,1)S(1)}, bf16[16,1280]{1,0:T(8,128)(2,1)S(1)}, u32[]{:S(2)}, u32[]{:S(2)}) %collective-permute-start.27) | collective-permute-done | bytes 40992 | tf_op jit(solution)/shard_map/ppermute | solution.py:20
  (198 shorter events, 61.4 us)
Async XLA Ops:
  0.6 21.0 %collective-permute-start.2 = (bf16[256,5120]{1,0:T(8,128)(2,1)}, bf16[256,5120]{1,0:T(8,128)(2,1)S(1)}, u32[]{:S(2)}, u32[]{:S(2)}) collective-permute-start(bf16[256,5120]{1,0:T(8,128)(2,1)} %wa.1), channel_id=1, source_target_pairs={{0,1},{1,0},{2,3},{3,2},{4,5},{5,4},{6,7},{7,6},{8,9},{9,8},{10,11... | collective-permute-start | bytes 7864328 | tf_op jit(solution)/shard_map/ppermute | solution.py:20
  25.8 11.5 %collective-permute-start.28 = (bf16[2,16,5120]{2,1,0:T(8,128)(2,1)S(1)}, bf16[2,16,5120]{2,1,0:T(8,128)(2,1)S(1)}, u32[]{:S(2)}, u32[]{:S(2)}) collective-permute-start(bf16[2,16,5120]{2,1,0:T(8,128)(2,1)S(1)} %slice_bitcast_fusion.1), channel_id=1, source_target_pairs={{0,2},{2,0},{4,6},{6,4},{1,3},{3,1},{5,7},{7,5},{8,10},{10,8},{12,... | collective-permute-start | bytes 983048 | tf_op jit(solution)/shard_map/ppermute | solution.py:20
  28.8 18.6 %collective-permute-start.3 = (bf16[2,16,5120]{2,1,0:T(8,128)(2,1)S(1)}, bf16[2,16,5120]{2,1,0:T(8,128)(2,1)S(1)}, u32[]{:S(2)}, u32[]{:S(2)}) collective-permute-start(bf16[2,16,5120]{2,1,0:T(8,128)(2,1)S(1)} %slice_bitcast_fusion.3), channel_id=1, source_target_pairs={{0,2},{2,0},{4,6},{6,4},{1,3},{3,1},{5,7},{7,5},{8,10},{10,8},{12,... | collective-permute-start | bytes 983048 | tf_op jit(solution)/shard_map/ppermute | solution.py:20
  37.4 11.8 %collective-permute-start.29 = (bf16[16,5120]{1,0:T(8,128)(2,1)S(1)}, bf16[16,5120]{1,0:T(8,128)(2,1)S(1)}, u32[]{:S(2)}, u32[]{:S(2)}) collective-permute-start(bf16[16,5120]{1,0:T(8,128)(2,1)S(1)} %slice_bitcast_fusion.15), channel_id=1, source_target_pairs={{0,4},{2,6},{4,0},{6,2},{1,5},{3,7},{5,1},{7,3},{8,12},{10,14},{12... | collective-permute-start | bytes 491528 | tf_op jit(solution)/shard_map/ppermute | solution.py:20
  47.5 10.3 %collective-permute-start.4 = (bf16[16,5120]{1,0:T(8,128)(2,1)S(1)}, bf16[16,5120]{1,0:T(8,128)(2,1)S(1)}, u32[]{:S(2)}, u32[]{:S(2)}) collective-permute-start(bf16[16,5120]{1,0:T(8,128)(2,1)S(1)} %slice_bitcast_fusion.19), channel_id=1, source_target_pairs={{0,4},{2,6},{4,0},{6,2},{1,5},{3,7},{5,1},{7,3},{8,12},{10,14},{12... | collective-permute-start | bytes 491528 | tf_op jit(solution)/shard_map/ppermute | solution.py:20
  61.9 11.0 %collective-permute-start.30 = (bf16[16,1280]{1,0:T(8,128)(2,1)}, bf16[16,1280]{1,0:T(8,128)(2,1)}, u32[]{:S(2)}, u32[]{:S(2)}) collective-permute-start(bf16[16,1280]{1,0:T(8,128)(2,1)} %bitcast.311), channel_id=1, source_target_pairs={{0,8},{8,0},{16,24},{24,16},{1,9},{9,1},{17,25},{25,17},{2,10},{10... | collective-permute-start | bytes 122888 | tf_op jit(solution)/shard_map/ppermute | solution.py:20
  63.9 9.8 %collective-permute-start.31 = (bf16[16,1280]{1,0:T(8,128)(2,1)}, bf16[16,1280]{1,0:T(8,128)(2,1)}, u32[]{:S(2)}, u32[]{:S(2)}) collective-permute-start(bf16[16,1280]{1,0:T(8,128)(2,1)} %bitcast.310), channel_id=1, source_target_pairs={{0,16},{8,24},{16,0},{24,8},{1,17},{9,25},{17,1},{25,9},{2,18},{10... | collective-permute-start | bytes 122888 | tf_op jit(solution)/shard_map/ppermute | solution.py:20
  66.0 7.7 %collective-permute-start.32 = (bf16[16,1280]{1,0:T(8,128)(2,1)}, bf16[16,1280]{1,0:T(8,128)(2,1)}, u32[]{:S(2)}, u32[]{:S(2)}) collective-permute-start(bf16[16,1280]{1,0:T(8,128)(2,1)} %bitcast.309), channel_id=1, source_target_pairs={{0,24},{8,16},{16,8},{24,0},{1,25},{9,17},{17,9},{25,1},{2,26},{10... | collective-permute-start | bytes 122888 | tf_op jit(solution)/shard_map/ppermute | solution.py:20
  74.5 12.7 %collective-permute-start.33 = (bf16[1,4,16,1280]{3,2,1,0:T(8,128)(2,1)S(1)}, bf16[1,4,16,1280]{3,2,1,0:T(8,128)(2,1)S(1)}, u32[]{:S(2)}, u32[]{:S(2)}) collective-permute-start(bf16[1,4,16,1280]{3,2,1,0:T(8,128)(2,1)S(1)} %get-tuple-element.56), channel_id=1, source_target_pairs={{0,4},{2,6},{4,0},{6,2},{1,5},{3,7},{5,1},{7,3},{8,12},{10,14},{12... | collective-permute-start | bytes 491528 | tf_op jit(solution)/shard_map/ppermute | solution.py:20
  78.0 12.0 %collective-permute-start.8 = (bf16[1,4,16,1280]{3,2,1,0:T(8,128)(2,1)S(1)}, bf16[1,4,16,1280]{3,2,1,0:T(8,128)(2,1)S(1)}, u32[]{:S(2)}, u32[]{:S(2)}) collective-permute-start(bf16[1,4,16,1280]{3,2,1,0:T(8,128)(2,1)S(1)} %get-tuple-element.42), channel_id=1, source_target_pairs={{0,4},{2,6},{4,0},{6,2},{1,5},{3,7},{5,1},{7,3},{8,12},{10,14},{12... | collective-permute-start | bytes 491528 | tf_op jit(solution)/shard_map/ppermute | solution.py:20
  87.3 10.7 %collective-permute-start.34 = (bf16[2,4,16,1280]{3,2,1,0:T(8,128)(2,1)S(1)}, bf16[2,4,16,1280]{3,2,1,0:T(8,128)(2,1)S(1)}, u32[]{:S(2)}, u32[]{:S(2)}) collective-permute-start(bf16[2,4,16,1280]{3,2,1,0:T(8,128)(2,1)S(1)} %get-tuple-element.32), channel_id=1, source_target_pairs={{0,2},{2,0},{4,6},{6,4},{1,3},{3,1},{5,7},{7,5},{8,10},{10,8},{12,... | collective-permute-start | bytes 983048 | tf_op jit(solution)/shard_map/ppermute | solution.py:20
  87.4 18.3 %collective-permute-start.15 = (bf16[1280,896]{1,0:T(8,128)(2,1)S(1)}, bf16[1280,896]{1,0:T(8,128)(2,1)S(1)}, u32[]{:S(2)}, u32[]{:S(2)}) collective-permute-start(bf16[1280,896]{1,0:T(8,128)(2,1)S(1)} %copy-done.13), channel_id=1, source_target_pairs={{0,1},{1,0},{2,3},{3,2},{4,5},{5,4},{6,7},{7,6},{8,9},{9,8},{10,11... | collective-permute-start | bytes 6881288 | tf_op jit(solution)/shard_map/ppermute | solution.py:20
  87.5 19.1 %collective-permute-start.16 = (bf16[1280,896]{1,0:T(8,128)(2,1)}, bf16[1280,896]{1,0:T(8,128)(2,1)S(1)}, u32[]{:S(2)}, u32[]{:S(2)}) collective-permute-start(bf16[1280,896]{1,0:T(8,128)(2,1)} %param.25), channel_id=1, source_target_pairs={{0,1},{1,0},{2,3},{3,2},{4,5},{5,4},{6,7},{7,6},{8,9},{9,8},{10,11... | collective-permute-start | bytes 6881288 | tf_op jit(solution)/shard_map/ppermute | solution.py:20
  88.0 65.1 %collective-permute-start.22 = (bf16[896,1280]{1,0:T(8,128)(2,1)S(1)}, bf16[896,1280]{1,0:T(8,128)(2,1)S(1)}, u32[]{:S(2)}, u32[]{:S(2)}) collective-permute-start(bf16[896,1280]{1,0:T(8,128)(2,1)S(1)} %copy-done.8), channel_id=1, source_target_pairs={{0,1},{1,0},{2,3},{3,2},{4,5},{5,4},{6,7},{7,6},{8,9},{9,8},{10,11... | collective-permute-start | bytes 6881288 | tf_op jit(solution)/shard_map/ppermute | solution.py:20
  90.0 13.9 %collective-permute-start.9 = (bf16[2,4,16,1280]{3,2,1,0:T(8,128)(2,1)S(1)}, bf16[2,4,16,1280]{3,2,1,0:T(8,128)(2,1)S(1)}, u32[]{:S(2)}, u32[]{:S(2)}) collective-permute-start(bf16[2,4,16,1280]{3,2,1,0:T(8,128)(2,1)S(1)} %get-tuple-element.30), channel_id=1, source_target_pairs={{0,2},{2,0},{4,6},{6,4},{1,3},{3,1},{5,7},{7,5},{8,10},{10,8},{12,... | collective-permute-start | bytes 983048 | tf_op jit(solution)/shard_map/ppermute | solution.py:20
  100.0 13.0 %collective-permute-start.35 = (bf16[2,4,16,1792]{3,2,1,0:T(8,128)(2,1)S(1)}, bf16[2,4,16,1792]{3,2,1,0:T(8,128)(2,1)S(1)}, u32[]{:S(2)}, u32[]{:S(2)}) collective-permute-start(bf16[2,4,16,1792]{3,2,1,0:T(8,128)(2,1)S(1)} %bitcast.350), channel_id=1, source_target_pairs={{0,8},{8,0},{16,24},{24,16},{1,9},{9,1},{17,25},{25,17},{2,10},{10... | collective-permute-start | bytes 1376264 | tf_op jit(solution)/shard_map/ppermute | solution.py:20
  107.6 13.5 %collective-permute-start.40 = (bf16[2,4,16,1792]{3,2,1,0:T(8,128)(2,1)S(1)}, bf16[2,4,16,1792]{3,2,1,0:T(8,128)(2,1)S(1)}, u32[]{:S(2)}, u32[]{:S(2)}) collective-permute-start(bf16[2,4,16,1792]{3,2,1,0:T(8,128)(2,1)S(1)} %slice.211), channel_id=1, source_target_pairs={{0,16},{8,24},{16,0},{24,8},{1,17},{9,25},{17,1},{25,9},{2,18},{10... | collective-permute-start | bytes 1376264 | tf_op jit(solution)/shard_map/ppermute | solution.py:20
  109.1 13.4 %collective-permute-start.10 = (bf16[2,4,16,1792]{3,2,1,0:T(8,128)(2,1)S(1)}, bf16[2,4,16,1792]{3,2,1,0:T(8,128)(2,1)S(1)}, u32[]{:S(2)}, u32[]{:S(2)}) collective-permute-start(bf16[2,4,16,1792]{3,2,1,0:T(8,128)(2,1)S(1)} %slice_bitcast_fusion), channel_id=1, source_target_pairs={{0,8},{8,0},{16,24},{24,16},{1,9},{9,1},{17,25},{25,17},{2,10},{10... | collective-permute-start | bytes 1376264 | tf_op jit(solution)/shard_map/ppermute | solution.py:20
  112.5 18.5 %collective-permute-start.17 = (bf16[2,4,16,1792]{3,2,1,0:T(8,128)(2,1)S(1)}, bf16[2,4,16,1792]{3,2,1,0:T(8,128)(2,1)S(1)}, u32[]{:S(2)}, u32[]{:S(2)}) collective-permute-start(bf16[2,4,16,1792]{3,2,1,0:T(8,128)(2,1)S(1)} %slice.190), channel_id=1, source_target_pairs={{0,16},{8,24},{16,0},{24,8},{1,17},{9,25},{17,1},{25,9},{2,18},{10... | collective-permute-start | bytes 1376264 | tf_op jit(solution)/shard_map/ppermute | solution.py:20
  113.2 22.7 %collective-permute-start.36 = (bf16[4,16,1792]{2,1,0:T(8,128)(2,1)S(1)}, bf16[4,16,1792]{2,1,0:T(8,128)(2,1)S(1)}, u32[]{:S(2)}, u32[]{:S(2)}) collective-permute-start(bf16[4,16,1792]{2,1,0:T(8,128)(2,1)S(1)} %slice_bitcast_fusion.7), channel_id=1, source_target_pairs={{0,16},{8,24},{16,0},{24,8},{1,17},{9,25},{17,1},{25,9},{2,18},{10... | collective-permute-start | bytes 688136 | tf_op jit(solution)/shard_map/ppermute | solution.py:20
  121.3 16.0 %collective-permute-start.41 = (bf16[4,16,1792]{2,1,0:T(8,128)(2,1)S(1)}, bf16[4,16,1792]{2,1,0:T(8,128)(2,1)S(1)}, u32[]{:S(2)}, u32[]{:S(2)}) collective-permute-start(bf16[4,16,1792]{2,1,0:T(8,128)(2,1)S(1)} %slice_bitcast_fusion.5), channel_id=1, source_target_pairs={{0,8},{8,0},{16,24},{24,16},{1,9},{9,1},{17,25},{25,17},{2,10},{10... | collective-permute-start | bytes 688136 | tf_op jit(solution)/shard_map/ppermute | solution.py:20
  122.6 17.3 %collective-permute-start.11 = (bf16[4,16,1792]{2,1,0:T(8,128)(2,1)S(1)}, bf16[4,16,1792]{2,1,0:T(8,128)(2,1)S(1)}, u32[]{:S(2)}, u32[]{:S(2)}) collective-permute-start(bf16[4,16,1792]{2,1,0:T(8,128)(2,1)S(1)} %slice_bitcast_fusion.11), channel_id=1, source_target_pairs={{0,16},{8,24},{16,0},{24,8},{1,17},{9,25},{17,1},{25,9},{2,18},{10... | collective-permute-start | bytes 688136 | tf_op jit(solution)/shard_map/ppermute | solution.py:20
  131.1 10.8 %collective-permute-start.18 = (bf16[4,16,1792]{2,1,0:T(8,128)(2,1)S(1)}, bf16[4,16,1792]{2,1,0:T(8,128)(2,1)S(1)}, u32[]{:S(2)}, u32[]{:S(2)}) collective-permute-start(bf16[4,16,1792]{2,1,0:T(8,128)(2,1)S(1)} %slice_bitcast_fusion.9), channel_id=1, source_target_pairs={{0,8},{8,0},{16,24},{24,16},{1,9},{9,1},{17,25},{25,17},{2,10},{10... | collective-permute-start | bytes 688136 | tf_op jit(solution)/shard_map/ppermute | solution.py:20
  137.3 8.8 %collective-permute-start.38 = (bf16[4,16,896]{2,1,0:T(8,128)(2,1)S(1)}, bf16[4,16,896]{2,1,0:T(8,128)(2,1)S(1)}, u32[]{:S(2)}, u32[]{:S(2)}) collective-permute-start(bf16[4,16,896]{2,1,0:T(8,128)(2,1)S(1)} %fusion.13), channel_id=1, source_target_pairs={{0,16},{8,24},{16,0},{24,8},{1,17},{9,25},{17,1},{25,9},{2,18},{10... | collective-permute-start | bytes 344072 | tf_op jit(solution)/shard_map/ppermute | solution.py:20
  139.9 7.3 %collective-permute-start.39 = (bf16[4,16,896]{2,1,0:T(8,128)(2,1)S(1)}, bf16[4,16,896]{2,1,0:T(8,128)(2,1)S(1)}, u32[]{:S(2)}, u32[]{:S(2)}) collective-permute-start(bf16[4,16,896]{2,1,0:T(8,128)(2,1)S(1)} %fusion.13), channel_id=1, source_target_pairs={{0,24},{8,16},{16,8},{24,0},{1,25},{9,17},{17,9},{25,1},{2,26},{10... | collective-permute-start | bytes 344072 | tf_op jit(solution)/shard_map/ppermute | solution.py:20
  147.2 9.4 %collective-permute-start.12 = (bf16[4,16,896]{2,1,0:T(8,128)(2,1)S(1)}, bf16[4,16,896]{2,1,0:T(8,128)(2,1)S(1)}, u32[]{:S(2)}, u32[]{:S(2)}) collective-permute-start(bf16[4,16,896]{2,1,0:T(8,128)(2,1)S(1)} %fusion.15), channel_id=1, source_target_pairs={{0,8},{8,0},{16,24},{24,16},{1,9},{9,1},{17,25},{25,17},{2,10},{10... | collective-permute-start | bytes 344072 | tf_op jit(solution)/shard_map/ppermute | solution.py:20
  149.0 9.6 %collective-permute-start.13 = (bf16[4,16,896]{2,1,0:T(8,128)(2,1)S(1)}, bf16[4,16,896]{2,1,0:T(8,128)(2,1)S(1)}, u32[]{:S(2)}, u32[]{:S(2)}) collective-permute-start(bf16[4,16,896]{2,1,0:T(8,128)(2,1)S(1)} %fusion.15), channel_id=1, source_target_pairs={{0,16},{8,24},{16,0},{24,8},{1,17},{9,25},{17,1},{25,9},{2,18},{10... | collective-permute-start | bytes 344072 | tf_op jit(solution)/shard_map/ppermute | solution.py:20
  149.8 8.8 %collective-permute-start.14 = (bf16[4,16,896]{2,1,0:T(8,128)(2,1)S(1)}, bf16[4,16,896]{2,1,0:T(8,128)(2,1)S(1)}, u32[]{:S(2)}, u32[]{:S(2)}) collective-permute-start(bf16[4,16,896]{2,1,0:T(8,128)(2,1)S(1)} %fusion.15), channel_id=1, source_target_pairs={{0,24},{8,16},{16,8},{24,0},{1,25},{9,17},{17,9},{25,1},{2,26},{10... | collective-permute-start | bytes 344072 | tf_op jit(solution)/shard_map/ppermute | solution.py:20
  158.6 12.2 %collective-permute-start.45 = (bf16[2,4,16,1280]{3,2,1,0:T(8,128)(2,1)S(1)}, bf16[2,4,16,1280]{3,2,1,0:T(8,128)(2,1)S(1)}, u32[]{:S(2)}, u32[]{:S(2)}) collective-permute-start(bf16[2,4,16,1280]{3,2,1,0:T(8,128)(2,1)S(1)} %bitcast.353), channel_id=1, source_target_pairs={{0,2},{2,0},{4,6},{6,4},{1,3},{3,1},{5,7},{7,5},{8,10},{10,8},{12,... | collective-permute-start | bytes 983048 | tf_op jit(solution)/shard_map/ppermute | solution.py:20
  164.3 10.0 %collective-permute-start.23 = (bf16[2,4,16,1280]{3,2,1,0:T(8,128)(2,1)S(1)}, bf16[2,4,16,1280]{3,2,1,0:T(8,128)(2,1)S(1)}, u32[]{:S(2)}, u32[]{:S(2)}) collective-permute-start(bf16[2,4,16,1280]{3,2,1,0:T(8,128)(2,1)S(1)} %bitcast.354), channel_id=1, source_target_pairs={{0,2},{2,0},{4,6},{6,4},{1,3},{3,1},{5,7},{7,5},{8,10},{10,8},{12,... | collective-permute-start | bytes 983048 | tf_op jit(solution)/shard_map/ppermute | solution.py:20
  170.9 11.7 %collective-permute-start.46 = (bf16[4,16,1280]{2,1,0:T(8,128)(2,1)S(1)}, bf16[4,16,1280]{2,1,0:T(8,128)(2,1)S(1)}, u32[]{:S(2)}, u32[]{:S(2)}) collective-permute-start(bf16[4,16,1280]{2,1,0:T(8,128)(2,1)S(1)} %slice_bitcast_fusion.13), channel_id=1, source_target_pairs={{0,4},{2,6},{4,0},{6,2},{1,5},{3,7},{5,1},{7,3},{8,12},{10,14},{12... | collective-permute-start | bytes 491528 | tf_op jit(solution)/shard_map/ppermute | solution.py:20
  174.4 11.8 %collective-permute-start.24 = (bf16[4,16,1280]{2,1,0:T(8,128)(2,1)S(1)}, bf16[4,16,1280]{2,1,0:T(8,128)(2,1)S(1)}, u32[]{:S(2)}, u32[]{:S(2)}) collective-permute-start(bf16[4,16,1280]{2,1,0:T(8,128)(2,1)S(1)} %slice_bitcast_fusion.17), channel_id=1, source_target_pairs={{0,4},{2,6},{4,0},{6,2},{1,5},{3,7},{5,1},{7,3},{8,12},{10,14},{12... | collective-permute-start | bytes 491528 | tf_op jit(solution)/shard_map/ppermute | solution.py:20
  (33 other events, 236.4 us)

commit v2 on v1

v2 whole, which is shorter than its diff:
```python
import functools
import math

import jax
import jax.numpy as jnp
import numpy as np
from jax import lax
from jax.experimental import pallas as pl
from jax.experimental.pallas import tpu as pltpu
from jax.sharding import PartitionSpec as P

NEG = -1e30
F32 = jnp.float32
BF16 = jnp.bfloat16
VMEM = pl.BlockSpec(memory_space=pltpu.VMEM)
SMEM = pl.BlockSpec(memory_space=pltpu.SMEM)


def swap(a, axis, mask):
    return lax.ppermute(a, axis, [(i, i ^ mask) for i in range(lax.axis_size(axis))])


def reduce_bits(x, axis, order, last=F32):
    first = None
    count = x.shape[0]
    left = list(range(count.bit_length() - 1))[::-1]
    x = x.reshape((2,) * len(left) + x.shape[1:])
    for bit in order:
        dim = left.index(bit)
        left.remove(bit)
        kept = lax.index_in_dim(x, 0, dim, False).astype(F32)
        came = swap(lax.index_in_dim(x, 1, dim, False), axis, 1 << bit)
        if first is None:
            first = came
        x = (kept + came.astype(F32)).astype(BF16 if left else last)
    return x, first


def gather_bits(x, axis):
    x = x[None]
    for bit in range(lax.axis_size(axis).bit_length() - 1)[::-1]:
        came = swap(x, axis, 1 << bit)
        x = jnp.stack([x, came], 1).reshape((2 * x.shape[0],) + x.shape[1:])
    return x


def trade(pieces, axis):
    return [pieces[0]] + [swap(piece, axis, j) for j, piece in enumerate(pieces) if j]


def attention_body(shape, first, *refs):
    kv_count, rows, chunk, span = shape
    if first:
        (scal, table, freq, q_ref, kn_ref, vn_ref, kc_ref, vc_ref,
         ko_ref, vo_ref, q_rot, key_pos, ok_ref, os_ref, sk_ref, ss_ref, inverse) = refs
        tokens, head_dim = kn_ref.shape
        pages = table.shape[1]
    else:
        scal, ko_ref, vo_ref, q_rot, key_pos, ok_ref, os_ref, sk_ref, ss_ref = refs
        tokens, head_dim = q_rot.shape[0], ko_ref.shape[2]
    slots, page = ko_ref.shape[0], ko_ref.shape[1]
    heads = q_rot.shape[1] // head_dim
    length, kv_id, blk_id = scal[0], scal[1], scal[2]
    scale = 1.0 / math.sqrt(head_dim)

    if first:
        @pl.loop(0, pages)
        def _(j):
            inverse[table[0, j]] = j

        lane = lax.broadcasted_iota(jnp.int32, (1, page), 1)
        for s in range(slots):
            key_pos[:, s * page:(s + 1) * page] = inverse[blk_id * slots + s] * page + lane

        where_at = (length + lax.broadcasted_iota(jnp.int32, (tokens, head_dim), 0)).astype(F32)
        angle = where_at * freq[...]
        cosine = jnp.cos(angle)
        sine = jnp.sin(angle)
        low = lax.broadcasted_iota(jnp.int32, (tokens, head_dim), 1) < head_dim // 2
        sine = jnp.where(low, -sine, sine)

        def rotate(u):
            u = u.astype(F32)
            return (u * cosine + pltpu.roll(u, head_dim // 2, 1) * sine).astype(BF16)

        for h in range(heads):
            cols = slice(h * head_dim, (h + 1) * head_dim)
            q_rot[:, cols] = rotate(q_ref[:, cols])
        k_rot = rotate(kn_ref[...])

        ko_ref[...] = kc_ref[...]
        vo_ref[...] = vc_ref[...]
        for extra in range(tokens // page + 1):
            logical = length // page + extra
            slot = table[0, jnp.minimum(logical, pages - 1)] - blk_id * slots

            @pl.when((logical < pages) & (slot >= 0) & (slot < slots))
            def _():
                begin = logical * page - length
                at = begin + lax.broadcasted_iota(jnp.int32, (page, tokens), 0)
                pick = (at == lax.broadcasted_iota(jnp.int32, (page, tokens), 1)).astype(BF16)
                fresh_k = jnp.dot(pick, k_rot, preferred_element_type=F32).astype(BF16)
                fresh_v = jnp.dot(pick, vn_ref[...], preferred_element_type=F32).astype(BF16)
                at = begin + lax.broadcasted_iota(jnp.int32, (page, head_dim), 0)
                is_new = (at >= 0) & (at < tokens)
                ko_ref[slot] = jnp.where(is_new, fresh_k, ko_ref[slot])
                vo_ref[slot] = jnp.where(is_new, fresh_v, vo_ref[slot])

    keys = ko_ref[...].reshape(slots * page, head_dim)
    values = vo_ref[...].reshape(slots * page, head_dim)
    side_rows = kv_count * rows
    head_rows = 2 * side_rows
    together = 2
    row = lax.broadcasted_iota(jnp.int32, (together * head_rows, 1), 0) % head_rows
    side = row // side_rows
    group = (row % side_rows) // rows
    token = ((group ^ kv_id) * 2 + (blk_id ^ side)) * span + chunk * rows + row % rows
    lane = lax.broadcasted_iota(jnp.int32, (side_rows, head_dim), 1)
    stats = [jnp.zeros((side_rows, head_dim), F32)] * 2
    for pair in range(heads // together):
        parts = []
        for h in range(pair * together, (pair + 1) * together):
            cols = slice(h * head_dim, (h + 1) * head_dim)
            for s in range(2):
                for m in range(kv_count):
                    start = ((kv_id ^ m) * 2 + (blk_id ^ s)) * span + chunk * rows
                    parts.append(q_rot[pl.ds(pl.multiple_of(start, rows), rows), cols])
        queries = jnp.concatenate(parts, 0)
        scores = lax.dot_general(queries, keys, (((1,), (1,)), ((), ())), preferred_element_type=F32)
        masked = jnp.where(key_pos[...] <= length + token, scores, NEG)
        top = jnp.maximum(jnp.max(masked, 1, keepdims=True), 0.1 * NEG)
        weights = jnp.exp2((masked - top) * (scale * math.log2(math.e))).astype(BF16)
        total = jnp.sum(weights.astype(F32), 1, keepdims=True)
        out = jnp.dot(weights, values, preferred_element_type=F32)
        some = total > 0.0
        safe = jnp.where(some, total, 1.0)
        out = (out / safe).astype(BF16)
        log_sum = jnp.where(some, top * scale + jnp.log(safe), NEG)
        for i in range(together):
            h = pair * together + i
            cols = slice(h * head_dim, (h + 1) * head_dim)
            for s, out_ref in enumerate((ok_ref, os_ref)):
                at = i * head_rows + s * side_rows
                out_ref[:, cols] = out[at:at + side_rows]
                stats[s] = jnp.where(lane == h, log_sum[at:at + side_rows], stats[s])
    sk_ref[...] = stats[0]
    ss_ref[...] = stats[1]


def attend_first(scal, table, q, k_new, v_new, k_cache, v_cache, kv_count, rows, span):
    tokens, head_dim = k_new.shape
    width = q.shape[1]
    slots, page = k_cache.shape[0], k_cache.shape[1]
    side = kv_count * rows
    pair = np.arange(head_dim) % (head_dim // 2)
    freq = jnp.asarray((1e6 ** (-2.0 * pair / head_dim)).astype(np.float32)[None])
    return pl.pallas_call(
        functools.partial(attention_body, (kv_count, rows, 0, span), True),
        in_specs=[SMEM, SMEM] + [VMEM] * 6,
        out_specs=[VMEM] * 8,
        out_shape=[
            jax.ShapeDtypeStruct(k_cache.shape, BF16),
            jax.ShapeDtypeStruct(v_cache.shape, BF16),
            jax.ShapeDtypeStruct((tokens, width), BF16),
            jax.ShapeDtypeStruct((1, slots * page), jnp.int32),
            jax.ShapeDtypeStruct((side, width), BF16),
            jax.ShapeDtypeStruct((side, width), BF16),
            jax.ShapeDtypeStruct((side, head_dim), F32),
            jax.ShapeDtypeStruct((side, head_dim), F32),
        ],
        scratch_shapes=[pltpu.SMEM((table.shape[1],), jnp.int32)],
        compiler_params=pltpu.CompilerParams(vmem_limit_bytes=60 * 2**20),
        name="attend_first",
    )(scal, table, freq, q, k_new, v_new, k_cache, v_cache)


def attend_next(scal, keys, values, q_rot, key_pos, kv_count, rows, chunk, span):
    width, head_dim = q_rot.shape[1], keys.shape[2]
    side = kv_count * rows
    return pl.pallas_call(
        functools.partial(attention_body, (kv_count, rows, chunk, span), False),
        in_specs=[SMEM] + [VMEM] * 4,
        out_specs=[VMEM] * 4,
        out_shape=[
            jax.ShapeDtypeStruct((side, width), BF16),
            jax.ShapeDtypeStruct((side, width), BF16),
            jax.ShapeDtypeStruct((side, head_dim), F32),
            jax.ShapeDtypeStruct((side, head_dim), F32),
        ],
        compiler_params=pltpu.CompilerParams(vmem_limit_bytes=40 * 2**20),
        name="attend_next",
    )(scal, keys, values, q_rot, key_pos)


def project_body(blk_ref, o1, o2, s1, s2, wa, wb, out_ref, attn):
    head_dim = s1.shape[1]
    heads = o1.shape[1] // head_dim
    depth = wa.shape[0]
    blk_id = blk_ref[0]

    @pl.when(pl.program_id(0) == 0)
    def _():
        for h in range(heads):
            cols = slice(h * head_dim, (h + 1) * head_dim)
            first, second = s1[:, h:h + 1], s2[:, h:h + 1]
            top = jnp.maximum(first, second)
            f1, f2 = jnp.exp(first - top), jnp.exp(second - top)
            mixed = f1 * o1[:, cols].astype(F32) + f2 * o2[:, cols].astype(F32)
            attn[:, cols] = (mixed / (f1 + f2)).astype(BF16)

    mine = attn[:, pl.ds(pl.multiple_of(blk_id * depth, depth), depth)]
    other = attn[:, pl.ds(pl.multiple_of((1 - blk_id) * depth, depth), depth)]
    out_ref[...] = (
        jnp.dot(mine, wa[...], preferred_element_type=F32)
        + jnp.dot(other, wb[...], preferred_element_type=F32)
    ).astype(BF16)


def project(blk, o1, o2, s1, s2, wa, wb):
    rows, width = o1.shape
    model = wa.shape[1]
    step = model // 4
    fixed = lambda a: pl.BlockSpec(a.shape, lambda n: (0, 0))
    weight = pl.BlockSpec((wa.shape[0], step), lambda n: (0, n))
    return pl.pallas_call(
        project_body,
        grid=(model // step,),
        in_specs=[SMEM, fixed(o1), fixed(o2), fixed(s1), fixed(s2), weight, weight],
        out_specs=pl.BlockSpec((rows, step), lambda n: (0, n)),
        out_shape=jax.ShapeDtypeStruct((rows, model), BF16),
        scratch_shapes=[pltpu.VMEM((rows, width), BF16)],
        compiler_params=pltpu.CompilerParams(vmem_limit_bytes=32 * 2**20),
        name="project",
    )(blk, o1, o2, s1, s2, wa, wb)


def norm_body(row0, req_ref, x_ref, kept, came, gain_ref, resid_ref, *rest):
    pieces, held = rest[:-1], rest[-1]
    part = pieces[0].shape[1]
    rows = resid_ref.shape[0]
    resid = x_ref[row0:row0 + rows].astype(F32) + (kept[...].astype(F32) + came[...].astype(F32))
    resid_ref[...] = resid
    scale = lax.rsqrt(jnp.mean(resid * resid, axis=-1, keepdims=True) + 1e-05)
    held[...] = (resid * scale * gain_ref[...].astype(F32)).astype(BF16)
    for j, piece in enumerate(pieces):
        start = pl.multiple_of((req_ref[0] ^ j) * part, part)
        piece[...] = held[:, pl.ds(start, part)]


def norm_cut(req, x, kept, came, gain, reqs, row0):
    rows, model = kept.shape
    part = model // reqs
    if part % 128:
        resid = x[row0:row0 + rows].astype(F32) + kept.astype(F32) + came.astype(F32)
        scale = lax.rsqrt(jnp.mean(resid * resid, axis=-1, keepdims=True) + 1e-05)
        cut = (resid * scale * gain.astype(F32)).astype(BF16).reshape(rows, reqs, part)
        return resid, [lax.dynamic_index_in_dim(cut, req[0] ^ j, 1, False) for j in range(reqs)]
    resid, *pieces = pl.pallas_call(
        functools.partial(norm_body, row0),
        in_specs=[SMEM] + [VMEM] * 4,
        out_specs=[VMEM] * (reqs + 1),
        out_shape=[jax.ShapeDtypeStruct((rows, model), F32)]
        + [jax.ShapeDtypeStruct((rows, part), BF16)] * reqs,
        scratch_shapes=[pltpu.VMEM((rows, model), BF16)],
        compiler_params=pltpu.CompilerParams(vmem_limit_bytes=8 * 2**20),
        name="norm_cut",
    )(req, x, kept, came, gain)
    return resid, pieces


def finish_body(req_ref, *refs):
    out_ref = refs[-1]
    at = 0
    chunks = out_ref.shape[0] // refs[0].shape[0]
    count = (len(refs) - 1) // chunks - 1
    for c in range(chunks):
        resid, pieces = refs[at], refs[at + 1:at + 1 + count]
        at += 1 + count
        rows = resid.shape[0]
        for j, piece in enumerate(pieces):
            part = piece.shape[1]
            cols = pl.ds(pl.multiple_of((req_ref[0] ^ j) * part, part), part)
            out_ref[c * rows:(c + 1) * rows, cols] = (
                resid[:, cols] + piece[...].astype(F32)
            ).astype(BF16)


def finish(req, parts):
    part = parts[0][1][0].shape[1]
    if part % 128:
        outs = []
        for resid, pieces in parts:
            came = jnp.stack(pieces)
            mlp = [lax.dynamic_index_in_dim(came, req[0] ^ j, 0, False) for j in range(len(pieces))]
            outs.append((resid + jnp.concatenate(mlp, 1).astype(F32)).astype(BF16))
        return jnp.concatenate(outs, 0)
    flat = [a for resid, pieces in parts for a in [resid] + list(pieces)]
    rows, model = parts[0][0].shape
    return pl.pallas_call(
        finish_body,
        in_specs=[SMEM] + [VMEM] * len(flat),
        out_specs=VMEM,
        out_shape=jax.ShapeDtypeStruct((len(parts) * rows, model), BF16),
        compiler_params=pltpu.CompilerParams(vmem_limit_bytes=8 * 2**20),
        name="finish",
    )(req, *flat)


def after(a, *others):
    return lax.optimization_barrier((a,) + others)[0]


def on_device(x_resid, q_new, k_new, v_new, k_cache, v_cache, cache_len, page_table,
              wo, norm_gain, w_gate, w_up, w_down):
    reqs, kvs = lax.axis_size("req"), lax.axis_size("kv")
    req_bits = reqs.bit_length() - 1
    kv_bits = kvs.bit_length() - 1
    req_id = lax.axis_index("req").astype(jnp.int32)
    blk_id = lax.axis_index("blk").astype(jnp.int32)
    span, model = x_resid.shape[1:]
    part = model // reqs
    rows = 16
    chunks = span // rows
    scal = jnp.stack([cache_len[0], lax.axis_index("kv"), blk_id]).astype(jnp.int32)
    blk, req = blk_id[None], req_id[None]
    near_masks = [0]
    far_masks = list(range(reqs))

    wo_far, gate_far, up_far = (swap(w, "blk", 1) for w in (wo, w_gate, w_up))
    early, late = [], []
    if len(near_masks) > 1:
        quarter = w_down.shape[0] // 4
        late = [w_down[i * quarter:(i + 1) * quarter] for i in range(4)]
        early = [swap(late.pop(0), "req", 1) for _ in range(3)]

    keys_out, values_out, q_rot, key_pos, *got = attend_first(
        scal, page_table, q_new[0], k_new[0], v_new[0], k_cache[0, 0], v_cache[0, 0],
        kvs, rows, span)
    attended = [got] + [
        attend_next(scal, keys_out, values_out, after(q_rot, *early[:1]), key_pos, kvs, rows, c, span)
        for c in range(1, chunks)
    ]
    a_order = list(range(req_bits))
    b_order = a_order[req_bits // 2:] + a_order[:req_bits // 2]

    kept, came = [], []
    last = None
    for o_keep, o_send, s_keep, s_send in attended:
        o_came, s_came = swap(o_send, "blk", 1), swap(s_send, "blk", 1)
        x = project(blk, o_keep, o_came, s_keep, s_came, wo, wo_far).reshape(kvs, rows, model)
        if last is not None:
            x = after(x, last, *early[1:2])
        for bit in range(kv_bits):
            x = x.reshape((-1, 2) + x.shape[1:])
            moved = swap(x[:, 1], "kv", 1 << bit)
            if bit == 0:
                last = moved
            if bit < kv_bits - 1:
                x = (x[:, 0].astype(F32) + moved.astype(F32)).astype(BF16)
        kept.append(x[0, 0])
        came.append(moved[0])

    resids, fed = [], []
    last = None
    for c in range(chunks):
        ready = after(kept[c], *early[2:]) if c == 0 else kept[c]
        resid, pieces = norm_cut(req, x_resid[0], ready, came[c], norm_gain[None], reqs, c * rows)
        resids.append(resid)
        got = jnp.stack(trade(pieces, "req"))
        if c == chunks - 1:
            late = [swap(after(w, got), "req", 1) for w in late]
        if last is not None:
            got = after(got, last)
        x = got[None]
        for bit in range(kv_bits)[::-1]:
            moved = swap(x, "kv", 1 << bit)
            if bit == kv_bits - 1:
                last = moved
            x = jnp.stack([x, moved], 1).reshape((2 * x.shape[0],) + x.shape[1:])
        fed.append(x.reshape(kvs * reqs * rows, part))

    downs = [w_down] + ([jnp.concatenate(early + late)] if early else [])
    downs = [(w, swap(w, "blk", 1)) for w in downs]
    parts = []
    last = None
    for c in range(chunks):
        flat = fed[c]

        def partials(gate_w, up_w):
            both = jnp.concatenate(
                [jnp.dot(flat, w, preferred_element_type=F32).astype(BF16) for w in (gate_w, up_w)], 1)
            return both.reshape(kvs, reqs, rows, -1).transpose(1, 0, 2, 3)

        def hidden_of(both):
            gate, up = jnp.split(both, 2, -1)
            return (jax.nn.silu(gate) * up).astype(BF16)

        near, far = partials(w_gate, w_up), partials(gate_far, up_far)
        if last is not None:
            near, far = after(near, *last), after(far, *last)
        near, near_first = reduce_bits(near, "req", a_order)
        far, far_first = reduce_bits(far, "req", b_order)
        last = near_first, far_first
        near, far = hidden_of(near), hidden_of(far)
        hidden = jnp.concatenate([near, far], -1)
        every = jnp.stack([swap(hidden, "req", h) if h else hidden for h in far_masks])
        every = every.reshape(len(far_masks) * kvs * rows, -1)
        depth = w_down.shape[0]
        down = jnp.stack([
            (
                jnp.dot(every[:, :depth], w, preferred_element_type=F32)
                + jnp.dot(every[:, depth:], w_far, preferred_element_type=F32)
            ).astype(BF16).reshape(len(far_masks), kvs, rows, part).transpose(1, 0, 2, 3)
            for w, w_far in downs
        ], 1)
        down, _ = reduce_bits(down, "kv", range(kv_bits), BF16)
        final = [None] * reqs
        for i, h in enumerate(far_masks):
            block = down[:, i]
            block = swap(block, "req", h) if h else block
            for k, g in enumerate(near_masks):
                final[h ^ g] = block[k]
        parts.append((resids[c], final))
    layer_out = finish(req, parts)[None]
    return layer_out, keys_out[None, None], values_out[None, None]


def solution(mesh):
    in_specs = (
        P("req", ("kv", "blk"), None),
        P("req", None, "kv"),
        P("req", None, "kv"),
        P("req", None, "kv"),
        P("req", "kv", "blk", None, None),
        P("req", "kv", "blk", None, None),
        P("req"),
        P("req", None),
        P(("kv", "blk"), None),
        P(),
        P("req", ("kv", "blk")),
        P("req", ("kv", "blk")),
        P(("kv", "blk"), "req"),
    )
    out_specs = (
        P("req", ("kv", "blk"), None),
        P("req", "kv", "blk", None, None),
        P("req", "kv", "blk", None, None),
    )
    return jax.shard_map(
        on_device, mesh=mesh, in_specs=in_specs, out_specs=out_specs, check_vma=False
    )
```

time: 194 us -> 164 us (0.85)
  waiting for transfers between devices: 95.2 us -> 78.7 us
  local copies, waits for them, and re-layouts: 16.7 us -> 5.61 us
  Pallas kernels: 14.2 us -> 18.4 us
  other arithmetic: 5.4 us -> 2.79 us
  starting transfers between devices: 49.8 us -> 47.2 us
    ppermute x50 -> x46, waiting for transfers between devices: 95.2 us -> 78.7 us  [swap(): lax.ppermute(a, axis, [(i, i ^ mask) for i in range(lax.axis_size(axis))])]
    unnamed x41 -> x28, local copies, waits for them, and re-layouts: 10.1 us -> 4.11 us
    dynamic_slice x2 -> x0, local copies, waits for them, and re-layouts: 3.28 us -> none  [on_device(): lax.dynamic_index_in_dim(cut, req_id ^ j, 1, False)]
    ppermute x50 -> x46, starting transfers between devices: 49.8 us -> 47.2 us  [swap(): lax.ppermute(a, axis, [(i, i ^ mask) for i in range(lax.axis_size(axis))])]
    reshape x5 -> x6, local copies, waits for them, and re-layouts: 2.65 us -> 0.35 us  [the longest x4 0.26 us: partials(): return both.reshape(kvs, reqs, rows, -1).transpose(1, 0, 2, 3)]
    pallas_call x1 -> x5, Pallas kernels: 11.9 us -> 14.1 us  [the longest x1 8.11 us: attend_first(): pl.pallas_call(functools.partial(attention_body, (kv_count, rows, 0, span...]
    pallas_call x1 -> x2, Pallas kernels: 2.32 us -> 4.24 us  [project(): pl.pallas_call(project_body, grid=(model // step,), in_specs=[SMEM, fixed...]
  transfers between devices with their start and end apart: 50 -> 46, of which waited for: 23 -> 25; matrix products, arithmetic and copies ran while one was open for 10% -> 9% of each run, Pallas kernels for 6% -> 9%
where the time goes in v2:
time: 164 us; the launch traced here: 165 us
  waiting for transfers between devices  78.7 us (48%)
  starting transfers between devices  47.2 us (29%)
  Pallas kernels  18.4 us (11%)
  matrix products  10.1 us (6%)
  local copies, waits for them, and re-layouts  5.61 us (3%)
  other arithmetic  2.79 us (2%)
  between operations  1.96 us (1%)
    ppermute x46, waiting for transfers between devices, swap(): lax.ppermute(a, axis, [(i, i ^ mask) for i in range(lax.axis_size(axis))])  78.7 us
    ppermute x46, starting transfers between devices, swap(): lax.ppermute(a, axis, [(i, i ^ mask) for i in range(lax.axis_size(axis))])  47.2 us
    pallas_call x1, Pallas kernels, attend_first(): pl.pallas_call(functools.partial(attention_body, (kv_count, rows, 0, span...  8.11 us
    dot_general x8, matrix products, partials(): jnp.dot(flat, w, preferred_element_type=F32).astype(BF16)  6.75 us
    pallas_call x1, Pallas kernels, attend_next(): pl.pallas_call(functools.partial(attention_body, (kv_count, rows, chunk,...  4.75 us
    pallas_call x2, Pallas kernels, project(): pl.pallas_call(project_body, grid=(model // step,), in_specs=[SMEM, fixed...  4.24 us
    unnamed x28, local copies, waits for them, and re-layouts  4.11 us
  transfers between devices with their start and end apart: 46, of which 25 were waited for; matrix products, arithmetic and copies ran while one was open for 9% of the time, Pallas kernels for 9%

profile of v2, /device:TPU:0, one launch (start us, length us, event | category | flops | bytes accessed | tf_op | source)
XLA Modules:
  0.0 164.8 jit_solution(3808366505086197822)
XLA Ops:
  2.5 8.1 %attend_first.1 = (bf16[32,128,128]{2,1,0:T(8,128)(2,1)}, bf16[32,128,128]{2,1,0:T(8,128)(2,1)}, bf16[256,512]{1,0:T(8,128)(2,1)}, s32[1,4096]{1,0:T(1,128)}, bf...) custom-call(s32[3]{0:T(128)} %pad_add_fusion.refs_0_, ...), custom_call_target="tpu_custom_call" | custom-call | tf_op jit(solution)/shard_map/attend_first/pallas_call | solution.py:157
  12.1 1.7 %copy-done = bf16[256,5120]{1,0:T(8,128)(2,1)S(1)} copy-done((bf16[256,5120]{1,0:T(8,128)(2,1)S(1)}, bf16[256,5120]{1,0:T(8,128)(2,1)}, u32[]{:S(2)}) %copy-start) | copy-done | bytes 2621464
  15.5 2.0 %project.2 = bf16[64,5120]{1,0:T(8,128)(2,1)S(1)} custom-call(s32[1]{0:T(128)} %bitcast.2.blk_ref, bf16[64,512]{1,0:T(8,128)(2,1)S(1)} %copy-done.6, bf16[64,512]{1,0:T(8,128)(2,1)S(1)} %collective-permute-done.o2, f32[64,128]{1,0:T(8,128)S(1)} %copy-done.7, f32[64,128]{1,0:T(8,128)S(1)} %collective-permute-done.1.s2, bf16[256,5120]{1,0:T(8,128)(2,1)S(1)} %copy-done, ...), custom_call_target="tpu_custom_call" | custom-call | tf_op jit(solution)/shard_map/project/pallas_call | solution.py:225
  17.6 2.8 %collective-permute-start.3 = (bf16[2,16,5120]{2,1,0:T(8,128)(2,1)S(1)}, bf16[2,16,5120]{2,1,0:T(8,128)(2,1)S(1)}, u32[]{:S(2)}, u32[]{:S(2)}) collective-permute-start(bf16[2,16,5120]{2,1,0:T(8,128)(2,1)S(1)} %slice_bitcast_fusion.9), channel_id=1, source_target_pairs={{0,2},{2,0},{4,6},{6,4},{1,3},{3,1},{5,7},{7,5},{8,10},{10,8},{12,... | collective-permute-start | bytes 983048 | tf_op jit(solution)/shard_map/ppermute | solution.py:20
  20.4 4.8 %attend_next.1 = (bf16[64,512]{1,0:T(8,128)(2,1)S(1)}, bf16[64,512]{1,0:T(8,128)(2,1)S(1)}, f32[64,128]{1,0:T(8,128)S(1)}, f32[64,128]{1,0:T(8,128)S(1)}) custom-call(s32[3]{0:T(128)S(1)} %copy-done.9, bf16[32,128,128]{2,1,0:T(8,128)(2,1)S(1)} %copy-done.3, bf16[32,128,128]{2,1,0:T(8,128)(2,1)S(1)} %copy-done.4, bf16[256,512]{1,0:T(8,128)(2,1)S(1)} %copy-done.5, ...), custom_call_target="tpu_custom_call" | custom-call | tf_op jit(solution)/shard_map/attend_next/pallas_call | solution.py:180
  26.6 2.2 %project.3 = bf16[64,5120]{1,0:T(8,128)(2,1)S(1)} custom-call(s32[1]{0:T(128)} %bitcast.2.blk_ref, bf16[64,512]{1,0:T(8,128)(2,1)S(1)} %get-tuple-element.42.o1, bf16[64,512]{1,0:T(8,128)(2,1)S(1)} %collective-permute-done.25.o2, f32[64,128]{1,0:T(8,128)S(1)} %get-tuple-element.44.s1, f32[64,128]{1,0:T(8,128)S(1)} %collective-permute-done.26.s2, ...), custom_call_target="tpu_custom_call" | custom-call | tf_op jit(solution)/shard_map/project/pallas_call | solution.py:225
  31.1 2.6 %collective-permute-start.4 = (bf16[1,16,5120]{2,1,0:T(8,128)(2,1)}, bf16[1,16,5120]{2,1,0:T(8,128)(2,1)S(1)}, u32[]{:S(2)}, u32[]{:S(2)}) collective-permute-start(bf16[1,16,5120]{2,1,0:T(8,128)(2,1)} %get-tuple-element.61), channel_id=1, source_target_pairs={{0,4},{2,6},{4,0},{6,2},{1,5},{3,7},{5,1},{7,3},{8,12},{10,14},{12... | collective-permute-start | bytes 491528 | tf_op jit(solution)/shard_map/ppermute | solution.py:20
  33.7 8.8 %collective-permute-done.27 = bf16[2,16,5120]{2,1,0:T(8,128)(2,1)S(1)} collective-permute-done((bf16[2,16,5120]{2,1,0:T(8,128)(2,1)S(1)}, bf16[2,16,5120]{2,1,0:T(8,128)(2,1)S(1)}, u32[]{:S(2)}, u32[]{:S(2)}) %collective-permute-start.27) | collective-permute-done | bytes 327712 | tf_op jit(solution)/shard_map/ppermute | solution.py:20
  45.0 1.7 %collective-permute-start.6 = (bf16[16,1280]{1,0:T(8,128)(2,1)S(1)}, bf16[16,1280]{1,0:T(8,128)(2,1)S(1)}, u32[]{:S(2)}, u32[]{:S(2)}) collective-permute-start(bf16[16,1280]{1,0:T(8,128)(2,1)S(1)} %get-tuple-element.36), channel_id=1, source_target_pairs={{0,16},{8,24},{16,0},{24,8},{1,17},{9,25},{17,1},{25,9},{2,18},{10... | collective-permute-start | bytes 122888 | tf_op jit(solution)/shard_map/ppermute | solution.py:20
  47.0 4.6 %collective-permute-done.28 = bf16[1,16,5120]{2,1,0:T(8,128)(2,1)S(1)} collective-permute-done((bf16[1,16,5120]{2,1,0:T(8,128)(2,1)S(1)}, bf16[1,16,5120]{2,1,0:T(8,128)(2,1)S(1)}, u32[]{:S(2)}, u32[]{:S(2)}) %collective-permute-start.28) | collective-permute-done | bytes 163872 | tf_op jit(solution)/shard_map/ppermute | solution.py:20
  53.5 1.7 %collective-permute-start.30 = (bf16[16,1280]{1,0:T(8,128)(2,1)S(1)}, bf16[16,1280]{1,0:T(8,128)(2,1)S(1)}, u32[]{:S(2)}, u32[]{:S(2)}) collective-permute-start(bf16[16,1280]{1,0:T(8,128)(2,1)S(1)} %get-tuple-element.50), channel_id=1, source_target_pairs={{0,16},{8,24},{16,0},{24,8},{1,17},{9,25},{17,1},{25,9},{2,18},{10... | collective-permute-start | bytes 122888 | tf_op jit(solution)/shard_map/ppermute | solution.py:20
  57.5 2.6 %collective-permute-done.31 = bf16[16,1280]{1,0:T(8,128)(2,1)S(1)} collective-permute-done((bf16[16,1280]{1,0:T(8,128)(2,1)S(1)}, bf16[16,1280]{1,0:T(8,128)(2,1)S(1)}, u32[]{:S(2)}, u32[]{:S(2)}) %collective-permute-start.31) | collective-permute-done | bytes 40992 | tf_op jit(solution)/shard_map/ppermute | solution.py:20
  60.1 5.3 %collective-permute-done.8 = bf16[1,4,16,1280]{3,2,1,0:T(8,128)(2,1)S(1)} collective-permute-done((bf16[1,4,16,1280]{3,2,1,0:T(8,128)(2,1)S(1)}, bf16[1,4,16,1280]{3,2,1,0:T(8,128)(2,1)S(1)}, u32[]{:S(2)}, u32[]{:S(2)}) %collective-permute-start.8) | collective-permute-done | bytes 163872 | tf_op jit(solution)/shard_map/ppermute | solution.py:20
  65.5 2.2 %collective-permute-start.9 = (bf16[2,4,16,1280]{3,2,1,0:T(8,128)(2,1)S(1)}, bf16[2,4,16,1280]{3,2,1,0:T(8,128)(2,1)S(1)}, u32[]{:S(2)}, u32[]{:S(2)}) collective-permute-start(bf16[2,4,16,1280]{3,2,1,0:T(8,128)(2,1)S(1)} %get-tuple-element.60), channel_id=1, source_target_pairs={{0,2},{2,0},{4,6},{6,4},{1,3},{3,1},{5,7},{7,5},{8,10},{10,8},{12,... | collective-permute-start | bytes 983048 | tf_op jit(solution)/shard_map/ppermute | solution.py:20
  67.7 7.3 %collective-permute-done.32 = bf16[1,4,16,1280]{3,2,1,0:T(8,128)(2,1)S(1)} collective-permute-done((bf16[1,4,16,1280]{3,2,1,0:T(8,128)(2,1)S(1)}, bf16[1,4,16,1280]{3,2,1,0:T(8,128)(2,1)S(1)}, u32[]{:S(2)}, u32[]{:S(2)}) %collective-permute-start.32) | collective-permute-done | bytes 163872 | tf_op jit(solution)/shard_map/ppermute | solution.py:20
  75.2 4.6 %collective-permute-done.9 = bf16[2,4,16,1280]{3,2,1,0:T(8,128)(2,1)S(1)} collective-permute-done((bf16[2,4,16,1280]{3,2,1,0:T(8,128)(2,1)S(1)}, bf16[2,4,16,1280]{3,2,1,0:T(8,128)(2,1)S(1)}, u32[]{:S(2)}, u32[]{:S(2)}) %collective-permute-start.9) | collective-permute-done | bytes 327712 | tf_op jit(solution)/shard_map/ppermute | solution.py:20
  86.0 1.8 %collective-permute-start.14 = (bf16[2,4,16,1792]{3,2,1,0:T(8,128)(2,1)S(1)}, bf16[2,4,16,1792]{3,2,1,0:T(8,128)(2,1)S(1)}, u32[]{:S(2)}, u32[]{:S(2)}) collective-permute-start(bf16[2,4,16,1792]{3,2,1,0:T(8,128)(2,1)S(1)} %slice.189), channel_id=1, source_target_pairs={{0,16},{8,24},{16,0},{24,8},{1,17},{9,25},{17,1},{25,9},{2,18},{10... | collective-permute-start | bytes 1376264 | tf_op jit(solution)/shard_map/ppermute | solution.py:20
  91.6 1.7 %collective-permute-done.10 = bf16[2,4,16,1792]{3,2,1,0:T(8,128)(2,1)S(1)} collective-permute-done((bf16[2,4,16,1792]{3,2,1,0:T(8,128)(2,1)S(1)}, bf16[2,4,16,1792]{3,2,1,0:T(8,128)(2,1)S(1)}, u32[]{:S(2)}, u32[]{:S(2)}) %collective-permute-start.10) | collective-permute-done | bytes 458784 | tf_op jit(solution)/shard_map/ppermute | solution.py:20
  93.3 3.2 %collective-permute-done.14 = bf16[2,4,16,1792]{3,2,1,0:T(8,128)(2,1)S(1)} collective-permute-done((bf16[2,4,16,1792]{3,2,1,0:T(8,128)(2,1)S(1)}, bf16[2,4,16,1792]{3,2,1,0:T(8,128)(2,1)S(1)}, u32[]{:S(2)}, u32[]{:S(2)}) %collective-permute-start.14) | collective-permute-done | bytes 458784 | tf_op jit(solution)/shard_map/ppermute | solution.py:20
  101.1 10.2 %collective-permute-done.11 = bf16[4,16,1792]{2,1,0:T(8,128)(2,1)S(1)} collective-permute-done((bf16[4,16,1792]{2,1,0:T(8,128)(2,1)S(1)}, bf16[4,16,1792]{2,1,0:T(8,128)(2,1)S(1)}, u32[]{:S(2)}, u32[]{:S(2)}) %collective-permute-start.11) | collective-permute-done | bytes 229408 | tf_op jit(solution)/shard_map/ppermute | solution.py:20
  111.9 2.2 %collective-permute-start.16 = (bf16[4,16,1792]{2,1,0:T(8,128)(2,1)S(1)}, bf16[4,16,1792]{2,1,0:T(8,128)(2,1)S(1)}, u32[]{:S(2)}, u32[]{:S(2)}) collective-permute-start(bf16[4,16,1792]{2,1,0:T(8,128)(2,1)S(1)} %get-tuple-element.66), channel_id=1, source_target_pairs={{0,8},{8,0},{16,24},{24,16},{1,9},{9,1},{17,25},{25,17},{2,10},{10... | collective-permute-start | bytes 688136 | tf_op jit(solution)/shard_map/ppermute | solution.py:20
  114.0 1.8 %collective-permute-start.17 = (bf16[4,16,1792]{2,1,0:T(8,128)(2,1)S(1)}, bf16[4,16,1792]{2,1,0:T(8,128)(2,1)S(1)}, u32[]{:S(2)}, u32[]{:S(2)}) collective-permute-start(bf16[4,16,1792]{2,1,0:T(8,128)(2,1)S(1)} %get-tuple-element.66), channel_id=1, source_target_pairs={{0,16},{8,24},{16,0},{24,8},{1,17},{9,25},{17,1},{25,9},{2,18},{10... | collective-permute-start | bytes 688136 | tf_op jit(solution)/shard_map/ppermute | solution.py:20
  117.7 2.8 %collective-permute-done.16 = bf16[4,16,1792]{2,1,0:T(8,128)(2,1)S(1)} collective-permute-done((bf16[4,16,1792]{2,1,0:T(8,128)(2,1)S(1)}, bf16[4,16,1792]{2,1,0:T(8,128)(2,1)S(1)}, u32[]{:S(2)}, u32[]{:S(2)}) %collective-permute-start.16) | collective-permute-done | bytes 229408 | tf_op jit(solution)/shard_map/ppermute | solution.py:20
  123.0 1.6 collective-permute-done.18
  129.7 1.6 collective-permute-start.40
  131.4 4.0 %collective-permute-done.20 = bf16[2,1,4,16,1280]{4,3,2,1,0:T(8,128)(2,1)S(1)} collective-permute-done((bf16[2,1,4,16,1280]{4,3,2,1,0:T(8,128)(2,1)S(1)}, bf16[2,1,4,16,1280]{4,3,2,1,0:T(8,128)(2,1)S(1)}, u32[]{:S(2)}, u32[]{:S(2)}) %collective-permute-start.20) | collective-permute-done | bytes 327712 | tf_op jit(solution)/shard_map/ppermute | solution.py:20
  141.2 2.3 %collective-permute-done.21 = bf16[1,4,16,1280]{3,2,1,0:T(8,128)(2,1)S(1)} collective-permute-done((bf16[1,4,16,1280]{3,2,1,0:T(8,128)(2,1)S(1)}, bf16[1,4,16,1280]{3,2,1,0:T(8,128)(2,1)S(1)}, u32[]{:S(2)}, u32[]{:S(2)}) %collective-permute-start.21) | collective-permute-done | bytes 163872 | tf_op jit(solution)/shard_map/ppermute | solution.py:20
  143.5 5.2 %collective-permute-done.41 = bf16[2,1,4,16,1280]{4,3,2,1,0:T(8,128)(2,1)S(1)} collective-permute-done((bf16[2,1,4,16,1280]{4,3,2,1,0:T(8,128)(2,1)S(1)}, bf16[2,1,4,16,1280]{4,3,2,1,0:T(8,128)(2,1)S(1)}, u32[]{:S(2)}, u32[]{:S(2)}) %collective-permute-start.41) | collective-permute-done | bytes 327712 | tf_op jit(solution)/shard_map/ppermute | solution.py:20
  148.8 1.6 collective-permute-start.22
  152.8 3.9 %collective-permute-done.42 = bf16[1,4,16,1280]{3,2,1,0:T(8,128)(2,1)S(1)} collective-permute-done((bf16[1,4,16,1280]{3,2,1,0:T(8,128)(2,1)S(1)}, bf16[1,4,16,1280]{3,2,1,0:T(8,128)(2,1)S(1)}, u32[]{:S(2)}, u32[]{:S(2)}) %collective-permute-start.42) | collective-permute-done | bytes 163872 | tf_op jit(solution)/shard_map/ppermute | solution.py:20
  157.0 2.0 %collective-permute-start.44 = (bf16[1,16,1280]{2,1,0:T(8,128)(2,1)S(1)}, bf16[1,16,1280]{2,1,0:T(8,128)(2,1)S(1)}, u32[]{:S(2)}, u32[]{:S(2)}) collective-permute-start(bf16[1,16,1280]{2,1,0:T(8,128)(2,1)S(1)} %get-tuple-element.68), channel_id=1, source_target_pairs={{0,16},{8,24},{16,0},{24,8},{1,17},{9,25},{17,1},{25,9},{2,18},{10... | collective-permute-start | bytes 122888 | tf_op jit(solution)/shard_map/ppermute | solution.py:20
  161.0 2.9 %collective-permute-done.45 = bf16[1,16,1280]{2,1,0:T(8,128)(2,1)S(1)} collective-permute-done((bf16[1,16,1280]{2,1,0:T(8,128)(2,1)S(1)}, bf16[1,16,1280]{2,1,0:T(8,128)(2,1)S(1)}, u32[]{:S(2)}, u32[]{:S(2)}) %collective-permute-start.45) | collective-permute-done | bytes 40992 | tf_op jit(solution)/shard_map/ppermute | solution.py:20
  (167 shorter events, 50.7 us)
Async XLA Ops:
  0.6 11.5 %collective-permute-start.2 = (bf16[256,5120]{1,0:T(8,128)(2,1)}, bf16[256,5120]{1,0:T(8,128)(2,1)S(1)}, u32[]{:S(2)}, u32[]{:S(2)}) collective-permute-start(bf16[256,5120]{1,0:T(8,128)(2,1)} %wa.3), channel_id=1, source_target_pairs={{0,1},{1,0},{2,3},{3,2},{4,5},{5,4},{6,7},{7,6},{8,9},{9,8},{10,11... | collective-permute-start | bytes 7864328 | tf_op jit(solution)/shard_map/ppermute | solution.py:20
  17.6 11.3 %collective-permute-start.3 = (bf16[2,16,5120]{2,1,0:T(8,128)(2,1)S(1)}, bf16[2,16,5120]{2,1,0:T(8,128)(2,1)S(1)}, u32[]{:S(2)}, u32[]{:S(2)}) collective-permute-start(bf16[2,16,5120]{2,1,0:T(8,128)(2,1)S(1)} %slice_bitcast_fusion.9), channel_id=1, source_target_pairs={{0,2},{2,0},{4,6},{6,4},{1,3},{3,1},{5,7},{7,5},{8,10},{10,8},{12,... | collective-permute-start | bytes 983048 | tf_op jit(solution)/shard_map/ppermute | solution.py:20
  28.9 13.5 %collective-permute-start.27 = (bf16[2,16,5120]{2,1,0:T(8,128)(2,1)S(1)}, bf16[2,16,5120]{2,1,0:T(8,128)(2,1)S(1)}, u32[]{:S(2)}, u32[]{:S(2)}) collective-permute-start(bf16[2,16,5120]{2,1,0:T(8,128)(2,1)S(1)} %slice_bitcast_fusion.5), channel_id=1, source_target_pairs={{0,2},{2,0},{4,6},{6,4},{1,3},{3,1},{5,7},{7,5},{8,10},{10,8},{12,... | collective-permute-start | bytes 983048 | tf_op jit(solution)/shard_map/ppermute | solution.py:20
  31.1 12.1 %collective-permute-start.4 = (bf16[1,16,5120]{2,1,0:T(8,128)(2,1)}, bf16[1,16,5120]{2,1,0:T(8,128)(2,1)S(1)}, u32[]{:S(2)}, u32[]{:S(2)}) collective-permute-start(bf16[1,16,5120]{2,1,0:T(8,128)(2,1)} %get-tuple-element.61), channel_id=1, source_target_pairs={{0,4},{2,6},{4,0},{6,2},{1,5},{3,7},{5,1},{7,3},{8,12},{10,14},{12... | collective-permute-start | bytes 491528 | tf_op jit(solution)/shard_map/ppermute | solution.py:20
  42.6 9.1 %collective-permute-start.28 = (bf16[1,16,5120]{2,1,0:T(8,128)(2,1)S(1)}, bf16[1,16,5120]{2,1,0:T(8,128)(2,1)S(1)}, u32[]{:S(2)}, u32[]{:S(2)}) collective-permute-start(bf16[1,16,5120]{2,1,0:T(8,128)(2,1)S(1)} %get-tuple-element.57), channel_id=1, source_target_pairs={{0,4},{2,6},{4,0},{6,2},{1,5},{3,7},{5,1},{7,3},{8,12},{10,14},{12... | collective-permute-start | bytes 491528 | tf_op jit(solution)/shard_map/ppermute | solution.py:20
  43.5 8.4 %collective-permute-start.5 = (bf16[16,1280]{1,0:T(8,128)(2,1)S(1)}, bf16[16,1280]{1,0:T(8,128)(2,1)S(1)}, u32[]{:S(2)}, u32[]{:S(2)}) collective-permute-start(bf16[16,1280]{1,0:T(8,128)(2,1)S(1)} %get-tuple-element.35), channel_id=1, source_target_pairs={{0,8},{8,0},{16,24},{24,16},{1,9},{9,1},{17,25},{25,17},{2,10},{10... | collective-permute-start | bytes 122888 | tf_op jit(solution)/shard_map/ppermute | solution.py:20
  45.0 8.5 %collective-permute-start.6 = (bf16[16,1280]{1,0:T(8,128)(2,1)S(1)}, bf16[16,1280]{1,0:T(8,128)(2,1)S(1)}, u32[]{:S(2)}, u32[]{:S(2)}) collective-permute-start(bf16[16,1280]{1,0:T(8,128)(2,1)S(1)} %get-tuple-element.36), channel_id=1, source_target_pairs={{0,16},{8,24},{16,0},{24,8},{1,17},{9,25},{17,1},{25,9},{2,18},{10... | collective-permute-start | bytes 122888 | tf_op jit(solution)/shard_map/ppermute | solution.py:20
  46.7 8.5 %collective-permute-start.7 = (bf16[16,1280]{1,0:T(8,128)(2,1)S(1)}, bf16[16,1280]{1,0:T(8,128)(2,1)S(1)}, u32[]{:S(2)}, u32[]{:S(2)}) collective-permute-start(bf16[16,1280]{1,0:T(8,128)(2,1)S(1)} %get-tuple-element.37), channel_id=1, source_target_pairs={{0,24},{8,16},{16,8},{24,0},{1,25},{9,17},{17,9},{25,1},{2,26},{10... | collective-permute-start | bytes 122888 | tf_op jit(solution)/shard_map/ppermute | solution.py:20
  47.0 37.0 %collective-permute-start.13 = (bf16[1280,896]{1,0:T(8,128)(2,1)}, bf16[1280,896]{1,0:T(8,128)(2,1)S(1)}, u32[]{:S(2)}, u32[]{:S(2)}) collective-permute-start(bf16[1280,896]{1,0:T(8,128)(2,1)} %param.25), channel_id=1, source_target_pairs={{0,1},{1,0},{2,3},{3,2},{4,5},{5,4},{6,7},{7,6},{8,9},{9,8},{10,11... | collective-permute-start | bytes 6881288 | tf_op jit(solution)/shard_map/ppermute | solution.py:20
  51.7 33.3 %collective-permute-start.12 = (bf16[1280,896]{1,0:T(8,128)(2,1)}, bf16[1280,896]{1,0:T(8,128)(2,1)S(1)}, u32[]{:S(2)}, u32[]{:S(2)}) collective-permute-start(bf16[1280,896]{1,0:T(8,128)(2,1)} %param.24), channel_id=1, source_target_pairs={{0,1},{1,0},{2,3},{3,2},{4,5},{5,4},{6,7},{7,6},{8,9},{9,8},{10,11... | collective-permute-start | bytes 6881288 | tf_op jit(solution)/shard_map/ppermute | solution.py:20
  56.0 9.4 %collective-permute-start.8 = (bf16[1,4,16,1280]{3,2,1,0:T(8,128)(2,1)S(1)}, bf16[1,4,16,1280]{3,2,1,0:T(8,128)(2,1)S(1)}, u32[]{:S(2)}, u32[]{:S(2)}) collective-permute-start(bf16[1,4,16,1280]{3,2,1,0:T(8,128)(2,1)S(1)} %get-tuple-element.76), channel_id=1, source_target_pairs={{0,4},{2,6},{4,0},{6,2},{1,5},{3,7},{5,1},{7,3},{8,12},{10,14},{12... | collective-permute-start | bytes 491528 | tf_op jit(solution)/shard_map/ppermute | solution.py:20
  65.4 9.6 %collective-permute-start.32 = (bf16[1,4,16,1280]{3,2,1,0:T(8,128)(2,1)S(1)}, bf16[1,4,16,1280]{3,2,1,0:T(8,128)(2,1)S(1)}, u32[]{:S(2)}, u32[]{:S(2)}) collective-permute-start(bf16[1,4,16,1280]{3,2,1,0:T(8,128)(2,1)S(1)} %bitcast.292), channel_id=1, source_target_pairs={{0,4},{2,6},{4,0},{6,2},{1,5},{3,7},{5,1},{7,3},{8,12},{10,14},{12... | collective-permute-start | bytes 491528 | tf_op jit(solution)/shard_map/ppermute | solution.py:20
  65.5 14.3 %collective-permute-start.9 = (bf16[2,4,16,1280]{3,2,1,0:T(8,128)(2,1)S(1)}, bf16[2,4,16,1280]{3,2,1,0:T(8,128)(2,1)S(1)}, u32[]{:S(2)}, u32[]{:S(2)}) collective-permute-start(bf16[2,4,16,1280]{3,2,1,0:T(8,128)(2,1)S(1)} %get-tuple-element.60), channel_id=1, source_target_pairs={{0,2},{2,0},{4,6},{6,4},{1,3},{3,1},{5,7},{7,5},{8,10},{10,8},{12,... | collective-permute-start | bytes 983048 | tf_op jit(solution)/shard_map/ppermute | solution.py:20
  67.7 57.8 %collective-permute-start.19 = (bf16[896,1280]{1,0:T(8,128)(2,1)S(1)}, bf16[896,1280]{1,0:T(8,128)(2,1)S(1)}, u32[]{:S(2)}, u32[]{:S(2)}) collective-permute-start(bf16[896,1280]{1,0:T(8,128)(2,1)S(1)} %copy-done.10), channel_id=1, source_target_pairs={{0,1},{1,0},{2,3},{3,2},{4,5},{5,4},{6,7},{7,6},{8,9},{9,8},{10,11... | collective-permute-start | bytes 6881288 | tf_op jit(solution)/shard_map/ppermute | solution.py:20
  75.1 12.6 %collective-permute-start.33 = (bf16[2,4,16,1280]{3,2,1,0:T(8,128)(2,1)S(1)}, bf16[2,4,16,1280]{3,2,1,0:T(8,128)(2,1)S(1)}, u32[]{:S(2)}, u32[]{:S(2)}) collective-permute-start(bf16[2,4,16,1280]{3,2,1,0:T(8,128)(2,1)S(1)} %get-tuple-element.56), channel_id=1, source_target_pairs={{0,2},{2,0},{4,6},{6,4},{1,3},{3,1},{5,7},{7,5},{8,10},{10,8},{12,... | collective-permute-start | bytes 983048 | tf_op jit(solution)/shard_map/ppermute | solution.py:20
  82.5 10.8 %collective-permute-start.10 = (bf16[2,4,16,1792]{3,2,1,0:T(8,128)(2,1)S(1)}, bf16[2,4,16,1792]{3,2,1,0:T(8,128)(2,1)S(1)}, u32[]{:S(2)}, u32[]{:S(2)}) collective-permute-start(bf16[2,4,16,1792]{3,2,1,0:T(8,128)(2,1)S(1)} %slice_bitcast_fusion.2), channel_id=1, source_target_pairs={{0,8},{8,0},{16,24},{24,16},{1,9},{9,1},{17,25},{25,17},{2,10},{10... | collective-permute-start | bytes 1376264 | tf_op jit(solution)/shard_map/ppermute | solution.py:20
  86.0 10.5 %collective-permute-start.14 = (bf16[2,4,16,1792]{3,2,1,0:T(8,128)(2,1)S(1)}, bf16[2,4,16,1792]{3,2,1,0:T(8,128)(2,1)S(1)}, u32[]{:S(2)}, u32[]{:S(2)}) collective-permute-start(bf16[2,4,16,1792]{3,2,1,0:T(8,128)(2,1)S(1)} %slice.189), channel_id=1, source_target_pairs={{0,16},{8,24},{16,0},{24,8},{1,17},{9,25},{17,1},{25,9},{2,18},{10... | collective-permute-start | bytes 1376264 | tf_op jit(solution)/shard_map/ppermute | solution.py:20
  96.5 19.3 %collective-permute-start.34 = (bf16[2,4,16,1792]{3,2,1,0:T(8,128)(2,1)S(1)}, bf16[2,4,16,1792]{3,2,1,0:T(8,128)(2,1)S(1)}, u32[]{:S(2)}, u32[]{:S(2)}) collective-permute-start(bf16[2,4,16,1792]{3,2,1,0:T(8,128)(2,1)S(1)} %slice_bitcast_fusion), channel_id=1, source_target_pairs={{0,8},{8,0},{16,24},{24,16},{1,9},{9,1},{17,25},{25,17},{2,10},{10... | collective-permute-start | bytes 1376264 | tf_op jit(solution)/shard_map/ppermute | solution.py:20
  97.2 18.8 %collective-permute-start.36 = (bf16[2,4,16,1792]{3,2,1,0:T(8,128)(2,1)S(1)}, bf16[2,4,16,1792]{3,2,1,0:T(8,128)(2,1)S(1)}, u32[]{:S(2)}, u32[]{:S(2)}) collective-permute-start(bf16[2,4,16,1792]{3,2,1,0:T(8,128)(2,1)S(1)} %slice.167), channel_id=1, source_target_pairs={{0,16},{8,24},{16,0},{24,8},{1,17},{9,25},{17,1},{25,9},{2,18},{10... | collective-permute-start | bytes 1376264 | tf_op jit(solution)/shard_map/ppermute | solution.py:20
  98.9 12.5 %collective-permute-start.11 = (bf16[4,16,1792]{2,1,0:T(8,128)(2,1)S(1)}, bf16[4,16,1792]{2,1,0:T(8,128)(2,1)S(1)}, u32[]{:S(2)}, u32[]{:S(2)}) collective-permute-start(bf16[4,16,1792]{2,1,0:T(8,128)(2,1)S(1)} %slice_bitcast_fusion.17), channel_id=1, source_target_pairs={{0,16},{8,24},{16,0},{24,8},{1,17},{9,25},{17,1},{25,9},{2,18},{10... | collective-permute-start | bytes 688136 | tf_op jit(solution)/shard_map/ppermute | solution.py:20
  99.6 12.1 %collective-permute-start.15 = (bf16[4,16,1792]{2,1,0:T(8,128)(2,1)S(1)}, bf16[4,16,1792]{2,1,0:T(8,128)(2,1)S(1)}, u32[]{:S(2)}, u32[]{:S(2)}) collective-permute-start(bf16[4,16,1792]{2,1,0:T(8,128)(2,1)S(1)} %slice_bitcast_fusion.15), channel_id=1, source_target_pairs={{0,8},{8,0},{16,24},{24,16},{1,9},{9,1},{17,25},{25,17},{2,10},{10... | collective-permute-start | bytes 688136 | tf_op jit(solution)/shard_map/ppermute | solution.py:20
  111.9 8.7 %collective-permute-start.16 = (bf16[4,16,1792]{2,1,0:T(8,128)(2,1)S(1)}, bf16[4,16,1792]{2,1,0:T(8,128)(2,1)S(1)}, u32[]{:S(2)}, u32[]{:S(2)}) collective-permute-start(bf16[4,16,1792]{2,1,0:T(8,128)(2,1)S(1)} %get-tuple-element.66), channel_id=1, source_target_pairs={{0,8},{8,0},{16,24},{24,16},{1,9},{9,1},{17,25},{25,17},{2,10},{10... | collective-permute-start | bytes 688136 | tf_op jit(solution)/shard_map/ppermute | solution.py:20
  114.0 8.9 %collective-permute-start.17 = (bf16[4,16,1792]{2,1,0:T(8,128)(2,1)S(1)}, bf16[4,16,1792]{2,1,0:T(8,128)(2,1)S(1)}, u32[]{:S(2)}, u32[]{:S(2)}) collective-permute-start(bf16[4,16,1792]{2,1,0:T(8,128)(2,1)S(1)} %get-tuple-element.66), channel_id=1, source_target_pairs={{0,16},{8,24},{16,0},{24,8},{1,17},{9,25},{17,1},{25,9},{2,18},{10... | collective-permute-start | bytes 688136 | tf_op jit(solution)/shard_map/ppermute | solution.py:20
  115.8 8.7 %collective-permute-start.18 = (bf16[4,16,1792]{2,1,0:T(8,128)(2,1)S(1)}, bf16[4,16,1792]{2,1,0:T(8,128)(2,1)S(1)}, u32[]{:S(2)}, u32[]{:S(2)}) collective-permute-start(bf16[4,16,1792]{2,1,0:T(8,128)(2,1)S(1)} %get-tuple-element.66), channel_id=1, source_target_pairs={{0,24},{8,16},{16,8},{24,0},{1,25},{9,17},{17,9},{25,1},{2,26},{10... | collective-permute-start | bytes 688136 | tf_op jit(solution)/shard_map/ppermute | solution.py:20
  116.0 11.5 %collective-permute-start.35 = (bf16[4,16,1792]{2,1,0:T(8,128)(2,1)S(1)}, bf16[4,16,1792]{2,1,0:T(8,128)(2,1)S(1)}, u32[]{:S(2)}, u32[]{:S(2)}) collective-permute-start(bf16[4,16,1792]{2,1,0:T(8,128)(2,1)S(1)} %slice_bitcast_fusion.13), channel_id=1, source_target_pairs={{0,16},{8,24},{16,0},{24,8},{1,17},{9,25},{17,1},{25,9},{2,18},{10... | collective-permute-start | bytes 688136 | tf_op jit(solution)/shard_map/ppermute | solution.py:20
  126.5 8.9 %collective-permute-start.20 = (bf16[2,1,4,16,1280]{4,3,2,1,0:T(8,128)(2,1)S(1)}, bf16[2,1,4,16,1280]{4,3,2,1,0:T(8,128)(2,1)S(1)}, u32[]{:S(2)}, u32[]{:S(2)}) collective-permute-start(bf16[2,1,4,16,1280]{4,3,2,1,0:T(8,128)(2,1)S(1)} %slice_bitcast_fusion.7), channel_id=1, source_target_pairs={{0,2},{2,0},{4,6},{6,4},{1,3},{3,1},{5,7},{7,5},{8,10},{10,8},{12,... | collective-permute-start | bytes 983048 | tf_op jit(solution)/shard_map/ppermute | solution.py:20
  127.8 8.7 %collective-permute-start.38 = (bf16[4,16,1792]{2,1,0:T(8,128)(2,1)S(1)}, bf16[4,16,1792]{2,1,0:T(8,128)(2,1)S(1)}, u32[]{:S(2)}, u32[]{:S(2)}) collective-permute-start(bf16[4,16,1792]{2,1,0:T(8,128)(2,1)S(1)} %get-tuple-element.64), channel_id=1, source_target_pairs={{0,8},{8,0},{16,24},{24,16},{1,9},{9,1},{17,25},{25,17},{2,10},{10... | collective-permute-start | bytes 688136 | tf_op jit(solution)/shard_map/ppermute | solution.py:20
  129.2 8.7 %collective-permute-start.39 = (bf16[4,16,1792]{2,1,0:T(8,128)(2,1)S(1)}, bf16[4,16,1792]{2,1,0:T(8,128)(2,1)S(1)}, u32[]{:S(2)}, u32[]{:S(2)}) collective-permute-start(bf16[4,16,1792]{2,1,0:T(8,128)(2,1)S(1)} %get-tuple-element.64), channel_id=1, source_target_pairs={{0,16},{8,24},{16,0},{24,8},{1,17},{9,25},{17,1},{25,9},{2,18},{10... | collective-permute-start | bytes 688136 | tf_op jit(solution)/shard_map/ppermute | solution.py:20
  139.7 8.9 %collective-permute-start.41 = (bf16[2,1,4,16,1280]{4,3,2,1,0:T(8,128)(2,1)S(1)}, bf16[2,1,4,16,1280]{4,3,2,1,0:T(8,128)(2,1)S(1)}, u32[]{:S(2)}, u32[]{:S(2)}) collective-permute-start(bf16[2,1,4,16,1280]{4,3,2,1,0:T(8,128)(2,1)S(1)} %slice_bitcast_fusion.3), channel_id=1, source_target_pairs={{0,2},{2,0},{4,6},{6,4},{1,3},{3,1},{5,7},{7,5},{8,10},{10,8},{12,... | collective-permute-start | bytes 983048 | tf_op jit(solution)/shard_map/ppermute | solution.py:20
  148.8 10.2 %collective-permute-start.22 = (bf16[1,16,1280]{2,1,0:T(8,128)(2,1)S(1)}, bf16[1,16,1280]{2,1,0:T(8,128)(2,1)S(1)}, u32[]{:S(2)}, u32[]{:S(2)}) collective-permute-start(bf16[1,16,1280]{2,1,0:T(8,128)(2,1)S(1)} %get-tuple-element.73), channel_id=1, source_target_pairs={{0,8},{8,0},{16,24},{24,16},{1,9},{9,1},{17,25},{25,17},{2,10},{10... | collective-permute-start | bytes 122888 | tf_op jit(solution)/shard_map/ppermute | solution.py:20
  150.5 9.9 %collective-permute-start.23 = (bf16[1,16,1280]{2,1,0:T(8,128)(2,1)S(1)}, bf16[1,16,1280]{2,1,0:T(8,128)(2,1)S(1)}, u32[]{:S(2)}, u32[]{:S(2)}) collective-permute-start(bf16[1,16,1280]{2,1,0:T(8,128)(2,1)S(1)} %get-tuple-element.72), channel_id=1, source_target_pairs={{0,16},{8,24},{16,0},{24,8},{1,17},{9,25},{17,1},{25,9},{2,18},{10... | collective-permute-start | bytes 122888 | tf_op jit(solution)/shard_map/ppermute | solution.py:20
  151.4 9.0 %collective-permute-start.24 = (bf16[1,16,1280]{2,1,0:T(8,128)(2,1)S(1)}, bf16[1,16,1280]{2,1,0:T(8,128)(2,1)S(1)}, u32[]{:S(2)}, u32[]{:S(2)}) collective-permute-start(bf16[1,16,1280]{2,1,0:T(8,128)(2,1)S(1)} %get-tuple-element.71), channel_id=1, source_target_pairs={{0,24},{8,16},{16,8},{24,0},{1,25},{9,17},{17,9},{25,1},{2,26},{10... | collective-permute-start | bytes 122888 | tf_op jit(solution)/shard_map/ppermute | solution.py:20
  (28 other events, 181.7 us)

commit v3 on v1

v3 whole, which is shorter than its diff:
```python
import functools
import math

import jax
import jax.numpy as jnp
import numpy as np
from jax import lax
from jax.experimental import pallas as pl
from jax.experimental.pallas import tpu as pltpu
from jax.sharding import PartitionSpec as P

NEG = -1e30
F32 = jnp.float32
BF16 = jnp.bfloat16
VMEM = pl.BlockSpec(memory_space=pltpu.VMEM)
SMEM = pl.BlockSpec(memory_space=pltpu.SMEM)
HBM = pl.BlockSpec(memory_space=pltpu.HBM)


def staged(body, scalars, arrays, late, out_shape, scratch, limit, name, out_specs=None):
    count = len(arrays)

    def kernel(*refs):
        n = len(scalars)
        sources, refs_out = refs[n:n + count], refs[n + count:n + count + len(out_shape)]
        rest = refs[n + count + len(out_shape):]
        held, sems, extra = rest[:count], rest[count], rest[count + 1:]
        copies = [
            pltpu.make_async_copy(src, dst, sems.at[i])
            for i, (src, dst) in enumerate(zip(sources, held))
        ]
        for copy in copies:
            copy.start()
        for copy in copies[:count - late]:
            copy.wait()
        waits = [lambda copy=copy: copy.wait() for copy in copies[count - late:]]
        body(*refs[:n], *held, *waits, *refs_out, *extra)

    return pl.pallas_call(
        kernel,
        in_specs=[SMEM] * len(scalars) + [HBM] * count,
        out_specs=out_specs or [VMEM] * len(out_shape),
        out_shape=out_shape,
        scratch_shapes=[pltpu.VMEM(a.shape, a.dtype) for a in arrays]
        + [pltpu.SemaphoreType.DMA((count,))] + list(scratch),
        compiler_params=pltpu.CompilerParams(vmem_limit_bytes=limit * 2**20),
        name=name,
    )(*scalars, *arrays)


def swap(a, axis, mask):
    return lax.ppermute(a, axis, [(i, i ^ mask) for i in range(lax.axis_size(axis))])


def reduce_bits(x, axis, order, last=F32):
    first = None
    count = x.shape[0]
    left = list(range(count.bit_length() - 1))[::-1]
    x = x.reshape((2,) * len(left) + x.shape[1:])
    for bit in order:
        dim = left.index(bit)
        left.remove(bit)
        kept = lax.index_in_dim(x, 0, dim, False).astype(F32)
        came = swap(lax.index_in_dim(x, 1, dim, False), axis, 1 << bit)
        x = (kept + came.astype(F32)).astype(BF16 if left else last)
        first = x if first is None else first
    return x, first


def gather_bits(x, axis):
    x = x[None]
    for bit in range(lax.axis_size(axis).bit_length() - 1)[::-1]:
        came = swap(x, axis, 1 << bit)
        x = jnp.stack([x, came], 1).reshape((2 * x.shape[0],) + x.shape[1:])
    return x


def bind(joint, *values):
    return lax.optimization_barrier(values) if joint else values


def trade(pieces, axis, joint=False):
    return [pieces[0], *bind(joint, *(swap(piece, axis, j) for j, piece in enumerate(pieces) if j))]


def reduce_both_ways(nears, fars, axis):
    sums_near, sums_far = [], []
    for near, far in zip(nears, fars):
        came = bind(True, swap(near[1::2], axis, 1), swap(far[2:], axis, 2), *sums_near, *sums_far)
        sums_near.append((near[::2].astype(F32) + came[0].astype(F32)).astype(BF16))
        sums_far.append((far[:2].astype(F32) + came[1].astype(F32)).astype(BF16))
    near, far = jnp.concatenate(sums_near, 1), jnp.concatenate(sums_far, 1)
    more = bind(True, swap(near[1], axis, 2), swap(far[1], axis, 1))
    return near[0].astype(F32) + more[0].astype(F32), far[0].astype(F32) + more[1].astype(F32)


def attention_body(shape, first, *refs):
    first_m, count, rows, together = shape
    if first:
        (scal, table, freq, q_ref, kn_ref, vn_ref, ko_ref, vo_ref, wait_k, wait_v,
         k_out, v_out, q_rot, key_pos, ok_ref, os_ref, inverse, out_sems) = refs
        tokens, head_dim = kn_ref.shape
        pages = table.shape[1]
    else:
        scal, ko_ref, vo_ref, q_rot, key_pos, ok_ref, os_ref = refs
        tokens, head_dim = q_rot.shape[0], ko_ref.shape[2]
    slots, page = ko_ref.shape[0], ko_ref.shape[1]
    heads = q_rot.shape[1] // head_dim
    length, kv_id, blk_id = scal[0], scal[1], scal[2]
    scale = 1.0 / math.sqrt(head_dim)

    if first:
        @pl.loop(0, pages)
        def _(j):
            inverse[table[0, j]] = j

        lane = lax.broadcasted_iota(jnp.int32, (1, page), 1)
        for s in range(slots):
            key_pos[:, s * page:(s + 1) * page] = inverse[blk_id * slots + s] * page + lane

        where_at = (length + lax.broadcasted_iota(jnp.int32, (tokens, head_dim), 0)).astype(F32)
        angle = where_at * freq[...]
        cosine = jnp.cos(angle)
        sine = jnp.sin(angle)
        low = lax.broadcasted_iota(jnp.int32, (tokens, head_dim), 1) < head_dim // 2
        sine = jnp.where(low, -sine, sine)

        def rotate(u):
            u = u.astype(F32)
            return (u * cosine + pltpu.roll(u, head_dim // 2, 1) * sine).astype(BF16)

        for h in range(heads):
            cols = slice(h * head_dim, (h + 1) * head_dim)
            q_rot[:, cols] = rotate(q_ref[:, cols])
        k_rot = rotate(kn_ref[...])

        wait_k()
        wait_v()
        for extra in range(tokens // page + 1):
            logical = length // page + extra
            slot = table[0, jnp.minimum(logical, pages - 1)] - blk_id * slots

            @pl.when((logical < pages) & (slot >= 0) & (slot < slots))
            def _():
                begin = logical * page - length
                at = begin + lax.broadcasted_iota(jnp.int32, (page, tokens), 0)
                pick = (at == lax.broadcasted_iota(jnp.int32, (page, tokens), 1)).astype(BF16)
                fresh_k = jnp.dot(pick, k_rot, preferred_element_type=F32).astype(BF16)
                fresh_v = jnp.dot(pick, vn_ref[...], preferred_element_type=F32).astype(BF16)
                at = begin + lax.broadcasted_iota(jnp.int32, (page, head_dim), 0)
                is_new = (at >= 0) & (at < tokens)
                ko_ref[slot] = jnp.where(is_new, fresh_k, ko_ref[slot])
                vo_ref[slot] = jnp.where(is_new, fresh_v, vo_ref[slot])

        stores = [
            pltpu.make_async_copy(src, dst, out_sems.at[i])
            for i, (src, dst) in enumerate(((ko_ref, k_out), (vo_ref, v_out)))
        ]
        for store in stores:
            store.start()

    keys = ko_ref[...].reshape(slots * page, head_dim)
    values = vo_ref[...].reshape(slots * page, head_dim)
    side_rows = count * rows
    head_rows = 2 * side_rows
    row = lax.broadcasted_iota(jnp.int32, (together * head_rows, 1), 0) % head_rows
    side = row // side_rows
    place = (row % side_rows) // rows + first_m
    token = ((place ^ kv_id) * 2 + (blk_id ^ side)) * rows + row % rows
    lane = lax.broadcasted_iota(jnp.int32, (side_rows, head_dim), 1)
    stats = [jnp.zeros((side_rows, head_dim), F32)] * 2
    for pair in range(heads // together):
        parts = []
        for h in range(pair * together, (pair + 1) * together):
            cols = slice(h * head_dim, (h + 1) * head_dim)
            for s in range(2):
                for m in range(first_m, first_m + count):
                    start = ((kv_id ^ m) * 2 + (blk_id ^ s)) * rows
                    parts.append(q_rot[pl.ds(pl.multiple_of(start, rows), rows), cols])
        queries = jnp.concatenate(parts, 0)
        scores = lax.dot_general(queries, keys, (((1,), (1,)), ((), ())), preferred_element_type=F32)
        masked = jnp.where(key_pos[...] <= length + token, scores, NEG)
        top = jnp.maximum(jnp.max(masked, 1, keepdims=True), 0.1 * NEG)
        weights = jnp.exp2((masked - top) * (scale * math.log2(math.e))).astype(BF16)
        total = jnp.sum(weights.astype(F32), 1, keepdims=True)
        out = jnp.dot(weights, values, preferred_element_type=F32)
        some = total > 0.0
        safe = jnp.where(some, total, 1.0)
        out = (out / safe).astype(BF16)
        log_sum = jnp.where(some, top * scale + jnp.log(safe), NEG)
        for i in range(together):
            h = pair * together + i
            cols = slice(h * head_dim, (h + 1) * head_dim)
            for s, out_ref in enumerate((ok_ref, os_ref)):
                at = i * head_rows + s * side_rows
                out_ref[:, cols] = out[at:at + side_rows]
                here = (lane % heads == h) & (lane < 3 * heads)
                stats[s] = jnp.where(here, log_sum[at:at + side_rows], stats[s])
    for stat, out_ref in zip(stats, (ok_ref, os_ref)):
        one = stat.astype(BF16).astype(F32)
        two = (stat - one).astype(BF16).astype(F32)
        stat = jnp.where(lane < heads, one, jnp.where(lane < 2 * heads, two, stat - one - two))
        out_ref[:, heads * head_dim:] = stat.astype(BF16)
    if first:
        for store in stores:
            store.wait()


def attend_first(scal, table, q, k_new, v_new, k_cache, v_cache, rows, first_m, count):
    tokens, head_dim = k_new.shape
    width = q.shape[1]
    slots, page = k_cache.shape[0], k_cache.shape[1]
    side = count * rows
    pair = np.arange(head_dim) % (head_dim // 2)
    freq = jnp.asarray((1e6 ** (-2.0 * pair / head_dim)).astype(np.float32)[None])
    return staged(
        functools.partial(attention_body, (first_m, count, rows, 4 if count == 1 else 1), True),
        [scal, table], [freq, q, k_new, v_new, k_cache, v_cache], 2,
        [
            jax.ShapeDtypeStruct(k_cache.shape, BF16),
            jax.ShapeDtypeStruct(v_cache.shape, BF16),
            jax.ShapeDtypeStruct((tokens, width), BF16),
            jax.ShapeDtypeStruct((1, slots * page), jnp.int32),
            jax.ShapeDtypeStruct((side, width + head_dim), BF16),
            jax.ShapeDtypeStruct((side, width + head_dim), BF16),
        ],
        [pltpu.SMEM((table.shape[1],), jnp.int32), pltpu.SemaphoreType.DMA((2,))],
        60, "attend_first", [HBM, HBM] + [VMEM] * 4)


def attend_next(scal, keys, values, q_rot, key_pos, rows, first_m, count):
    width, head_dim = q_rot.shape[1], keys.shape[2]
    side = count * rows
    return pl.pallas_call(
        functools.partial(attention_body, (first_m, count, rows, 1), False),
        in_specs=[SMEM] + [VMEM] * 4,
        out_specs=[VMEM] * 2,
        out_shape=[jax.ShapeDtypeStruct((side, width + head_dim), BF16)] * 2,
        compiler_params=pltpu.CompilerParams(vmem_limit_bytes=40 * 2**20),
        name="attend_next",
    )(scal, keys, values, q_rot, key_pos)


def project_body(head_dim, scal, o1, o2, wa, wb, wait_a, wait_b, *rest):
    outs, attn = rest[:-1], rest[-1]
    width = attn.shape[1]
    heads = width // head_dim
    depth, model = wa.shape
    blk_id = scal[2]
    rows = outs[0].shape[0]
    logs = []
    for o in (o1, o2):
        stat = o[:, width:].astype(F32)
        logs.append([sum(stat[:, h + i * heads:h + i * heads + 1] for i in range(3)) for h in range(heads)])
    for h in range(heads):
        cols = slice(h * head_dim, (h + 1) * head_dim)
        first, second = logs[0][h], logs[1][h]
        top = jnp.maximum(first, second)
        f1, f2 = jnp.exp(first - top), jnp.exp(second - top)
        mixed = f1 * o1[:, cols].astype(F32) + f2 * o2[:, cols].astype(F32)
        attn[:, cols] = (mixed / (f1 + f2)).astype(BF16)
    mine = attn[:, pl.ds(pl.multiple_of(blk_id * depth, depth), depth)]
    other = attn[:, pl.ds(pl.multiple_of((1 - blk_id) * depth, depth), depth)]
    wait_a()
    wait_b()
    step = model // 4
    for n in range(0, model, step):
        out = (
            jnp.dot(mine, wa[:, n:n + step], preferred_element_type=F32)
            + jnp.dot(other, wb[:, n:n + step], preferred_element_type=F32)
        ).astype(BF16)
        for i, out_ref in enumerate(outs):
            out_ref[:, n:n + step] = out[i * rows:(i + 1) * rows]


def project(scal, o1, o2, wa, wb, head_dim, count):
    rows = o1.shape[0]
    width = o1.shape[1] - head_dim
    return staged(
        functools.partial(project_body, head_dim), [scal], [o1, o2, wa, wb], 2,
        [jax.ShapeDtypeStruct((rows // count, wa.shape[1]), BF16)] * count,
        [pltpu.VMEM((rows, width), BF16)], 32, "project")


def norm_body(scal, x_ref, gain_ref, *rest):
    terms, resid_ref, pieces, held = rest[:3], rest[3], rest[4:-1], rest[-1]
    part = pieces[0].shape[1]
    resid = x_ref[...].astype(F32)
    for term in terms:
        resid = resid + term[...].astype(F32)
    resid_ref[...] = resid
    scale = lax.rsqrt(jnp.mean(resid * resid, axis=-1, keepdims=True) + 1e-05)
    held[...] = (resid * scale * gain_ref[...].astype(F32)).astype(BF16)
    for j, piece in enumerate(pieces):
        start = pl.multiple_of((scal[3] ^ j) * part, part)
        piece[...] = held[:, pl.ds(start, part)]


def norm_cut(scal, x, terms, gain, reqs):
    rows, model = terms[0].shape
    part = model // reqs
    return staged(
        norm_body, [scal], [x, gain, *terms], 0,
        [jax.ShapeDtypeStruct((rows, model), F32)]
        + [jax.ShapeDtypeStruct((rows, part), BF16)] * reqs,
        [pltpu.VMEM((rows, model), BF16)], 8, "norm_cut")


def partial_gate_up(feds, weights):
    flat = jnp.concatenate(feds, 0)
    flat = flat.reshape(-1, flat.shape[-1])
    both = jnp.concatenate(
        [jnp.dot(flat, w, preferred_element_type=F32).astype(BF16) for w in weights], 1)
    reqs, rows = feds[0].shape[:2]
    return both.reshape(len(feds), reqs, rows, -1).transpose(1, 0, 2, 3)


def down(hiddens, weights, groups):
    hidden = jnp.concatenate(hiddens, 0)
    depth = weights[0].shape[0]
    out = (
        jnp.dot(hidden[:, :depth], weights[0], preferred_element_type=F32)
        + jnp.dot(hidden[:, depth:], weights[1], preferred_element_type=F32)
    ).astype(BF16)
    out = out.reshape(len(hiddens), groups, -1, out.shape[1])
    return [out[:, m].reshape(-1, out.shape[-1]) for m in range(groups)]


def finish_body(chunks, scal, *refs):
    out_ref = refs[-1]
    for c in range(chunks):
        resid, own_a, own_b, own_c, back_x, back_y = refs[6 * c:6 * c + 6]
        rows, half = back_x.shape[0], back_x.shape[1] // 2
        here = slice(c * rows, (c + 1) * rows)
        whole = own_a[...].astype(F32) + own_b[...].astype(F32) + own_c[...].astype(F32)
        for block, side, value in (
            (0, 0, whole[:, :half]), (0, 1, whole[:, half:2 * half]),
            (1, 0, whole[:, 2 * half:3 * half]), (2, 1, whole[:, 3 * half:]),
            (1, 1, back_x[:, :half]), (3, 1, back_x[:, half:]),
            (2, 0, back_y[:, :half]), (3, 0, back_y[:, half:]),
        ):
            start = (scal[3] ^ block) * (2 * half) + side * half
            cols = pl.ds(pl.multiple_of(start, half), half)
            out_ref[here, cols] = (resid[:, cols] + value.astype(F32)).astype(BF16)


def finish(scal, parts):
    rows, model = parts[0][0].shape
    return staged(
        functools.partial(finish_body, len(parts)), [scal], [a for part in parts for a in part], 0,
        [jax.ShapeDtypeStruct((len(parts) * rows, model), BF16)], [], 8, "finish")[0]


def after(a, *others):
    return lax.optimization_barrier((a,) + others)[0]


def hidden_of(both):
    gate, up = jnp.split(both, 2, -1)
    return (jax.nn.silu(gate) * up).astype(BF16)


def reduce_four(x, axis, joint=False):
    came = swap(x[3], axis, 1)
    both = (x[2].astype(F32) + came.astype(F32)).astype(BF16)
    return [x[0], *bind(joint, swap(x[1], axis, 1), swap(both, axis, 2))], both


def halve_four(x, axis, joint=False):
    came = swap(jnp.stack([x[1], x[3]]), axis, 1)
    both = (x[2].astype(F32) + came[1].astype(F32)).astype(BF16)
    return [x[0], came[0], swap(both, axis, 2)], both


def total(terms):
    return terms[0].astype(F32) + terms[1].astype(F32) + terms[2].astype(F32)


def product(rows, weights):
    depth = weights[0][0].shape[0]
    near, far = rows[:, :depth], rows[:, depth:]
    return jnp.concatenate([
        (
            jnp.dot(near, pair[0], preferred_element_type=F32)
            + jnp.dot(far, pair[1], preferred_element_type=F32)
        ).astype(BF16)
        for pair in weights
    ], 1)


def on_device(x_resid, q_new, k_new, v_new, k_cache, v_cache, cache_len, page_table,
              wo, norm_gain, w_gate, w_up, w_down):
    reqs, kvs = lax.axis_size("req"), lax.axis_size("kv")
    rows, model = x_resid.shape[1:]
    head_dim = k_new.shape[2]
    scal = jnp.stack(
        [cache_len[0], lax.axis_index("kv"), lax.axis_index("blk"), lax.axis_index("req")]
    ).astype(jnp.int32)
    wo_far = swap(wo, "blk", 1)
    fast = reqs == 4 and kvs == 4
    first_m = kvs - 1 if fast else 0
    keys_out, values_out, q_rot, key_pos, o_keep, o_send = attend_first(
        scal, page_table, q_new[0], k_new[0], v_new[0], k_cache[0, 0], v_cache[0, 0],
        rows, first_m, kvs - first_m)
    projected = project(scal, o_keep, swap(o_send, "blk", 1), wo, wo_far, head_dim, kvs - first_m)
    if first_m:
        o_keep, o_send = attend_next(
            scal, keys_out, values_out, after(q_rot, projected[0]), key_pos, rows, 0, first_m)
        o_came = swap(o_send, "blk", 1)
        projected = [*project(scal, o_keep, o_came, wo, wo_far, head_dim, first_m), *projected]
    projected = [list(projected)]
    layer = four_way if fast else any_way
    layer_out = layer(x_resid[0], projected, scal, norm_gain[None], w_gate, w_up, w_down, reqs, kvs)
    return layer_out[None], keys_out[None, None], values_out[None, None]


def any_way(x_resid, projected, scal, gain, w_gate, w_up, w_down, reqs, kvs):
    rows, model = x_resid.shape
    part = model // reqs
    req_order = list(range(reqs.bit_length() - 1))
    kv_order = list(range(kvs.bit_length() - 1))
    gate_far, up_far, down_far = (swap(w, "blk", 1) for w in (w_gate, w_up, w_down))
    summed, _ = reduce_bits(jnp.stack(projected[0]), "kv", kv_order)
    resid = x_resid.astype(F32) + summed
    scale = lax.rsqrt(jnp.mean(resid * resid, axis=-1, keepdims=True) + 1e-05)
    cut = (resid * scale * gain.astype(F32)).astype(BF16).reshape(rows, reqs, part)
    pieces = [lax.dynamic_index_in_dim(cut, scal[3] ^ j, 1, False) for j in range(reqs)]
    fed = gather_bits(jnp.stack(trade(pieces, "req")), "kv")
    flat = fed.reshape(kvs * reqs * rows, part)
    hidden = []
    for gate_w, up_w in ((w_gate, w_up), (gate_far, up_far)):
        both = jnp.concatenate(
            [jnp.dot(flat, w, preferred_element_type=F32).astype(BF16) for w in (gate_w, up_w)], 1)
        both = both.reshape(kvs, reqs, rows, -1).transpose(1, 0, 2, 3)
        both, _ = reduce_bits(both, "req", req_order)
        every = jnp.stack(trade([hidden_of(both)] * reqs, "req"))
        hidden.append(every.reshape(reqs * kvs * rows, -1))
    out = (
        jnp.dot(hidden[0], w_down, preferred_element_type=F32)
        + jnp.dot(hidden[1], down_far, preferred_element_type=F32)
    ).astype(BF16)
    out = out.reshape(reqs, kvs, rows, part).transpose(1, 0, 2, 3)
    out, _ = reduce_bits(out, "kv", kv_order, BF16)
    came = jnp.stack(trade([out[j] for j in range(reqs)], "req"))
    mlp = [lax.dynamic_index_in_dim(came, scal[3] ^ j, 0, False) for j in range(reqs)]
    return (resid + jnp.concatenate(mlp, 1).astype(F32)).astype(BF16)


def four_way(x_resid, projected, scal, gain, w_gate, w_up, w_down, reqs, kvs):
    step, model = projected[0][0].shape
    part = model // reqs
    half = part // 2
    cuts = [w_down[:, :half], w_down[:, half:]]
    lent = [swap(cut, "req", mask) for cut, mask in zip(cuts, (1, 2))]
    summed, boths = [], []
    for sums in projected:
        if boths:
            sums[3] = after(sums[3], boths[-1])
        terms, both = reduce_four(sums, "kv", False)
        summed.append(terms)
        boths.append(both)

    resids, fed = [], []
    held = None
    for c, terms in enumerate(summed):
        if c == 0:
            terms[0] = after(terms[0], *lent)
        if held is not None:
            terms[0] = after(terms[0], *held)
        resid, *pieces = norm_cut(scal, x_resid[c * step:(c + 1) * step], terms, gain, reqs)
        resids.append(resid)
        got = jnp.stack(trade(pieces, "req", True))
        two, one = bind(True, swap(got, "kv", 2), swap(got, "kv", 1))
        three = swap(two, "kv", 1)
        fed.append([got, one, two, three])
        held = [one, two]
        gated = [two]

    gate_far, up_far = (swap(w, "blk", 1) for w in (w_gate, w_up))
    weights = [(w, swap(w, "blk", 1)) for w in (*cuts, *lent)]

    hiddens = []
    for got, one, two, three in fed:
        nears = [partial_gate_up([got, one, two], (w_gate, w_up))]
        fars = [partial_gate_up([got, one, two], (gate_far, up_far))]
        three = after(three, nears[0], fars[0])
        nears.append(partial_gate_up([three], (w_gate, w_up)))
        fars.append(partial_gate_up([three], (gate_far, up_far)))
        near, far = reduce_both_ways(nears, fars, "req")
        hidden = jnp.concatenate([hidden_of(near), hidden_of(far)], -1).reshape(kvs * step, -1)
        hiddens.append(hidden)

    owns, rests, parts = [], [], []
    for c, hidden in enumerate(hiddens):
        from_y, from_x = bind(True, swap(hidden, "req", 2), swap(hidden, "req", 1))
        first, second, over_x, over_y = weights
        own, both = reduce_four(product(hidden, weights).reshape(kvs, step, -1), "kv", False)
        from_y = after(from_y, both)
        rest = jnp.concatenate([product(from_y, (first, over_x)), product(from_x, (second, over_y))], 1)
        rest = list(rest.reshape(kvs, step, -1))
        rest[3] = after(rest[3], *own)
        rest, _ = reduce_four(rest, "kv", False)
        rest = total(rest).astype(BF16)
        rests.append(rest)
        back_y, back_x = bind(True, swap(rest[:, :part], "req", 2), swap(rest[:, part:], "req", 1))
        parts.append([resids[c], *own, back_x, back_y])
    return finish(scal, parts)


def solution(mesh):
    in_specs = (
        P("req", ("kv", "blk"), None),
        P("req", None, "kv"),
        P("req", None, "kv"),
        P("req", None, "kv"),
        P("req", "kv", "blk", None, None),
        P("req", "kv", "blk", None, None),
        P("req"),
        P("req", None),
        P(("kv", "blk"), None),
        P(),
        P("req", ("kv", "blk")),
        P("req", ("kv", "blk")),
        P(("kv", "blk"), "req"),
    )
    out_specs = (
        P("req", ("kv", "blk"), None),
        P("req", "kv", "blk", None, None),
        P("req", "kv", "blk", None, None),
    )
    return jax.shard_map(
        on_device, mesh=mesh, in_specs=in_specs, out_specs=out_specs, check_vma=False
    )
```

time: 194 us -> 162 us (0.84)
  starting transfers between devices: 49.8 us -> 35.6 us
  local copies, waits for them, and re-layouts: 16.7 us -> 3.12 us
  waiting for transfers between devices: 95.2 us -> 84.8 us
  Pallas kernels: 14.2 us -> 21.6 us
  other arithmetic: 5.4 us -> 2.32 us
  matrix products: 10.2 us -> 13 us
    ppermute x50 -> x36, starting transfers between devices: 49.8 us -> 35.6 us  [swap(): lax.ppermute(a, axis, [(i, i ^ mask) for i in range(lax.axis_size(axis))])]
    ppermute x50 -> x36, waiting for transfers between devices: 95.2 us -> 84.8 us  [swap(): lax.ppermute(a, axis, [(i, i ^ mask) for i in range(lax.axis_size(axis))])]
    unnamed x41 -> x31, local copies, waits for them, and re-layouts: 10.1 us -> 2.62 us
    pallas_call x2 -> x6, Pallas kernels: 14.2 us -> 21.6 us  [the longest x5 14.7 us: staged(): pl.pallas_call(kernel, in_specs=[SMEM] * len(scalars) + [HBM] * count, ou...]
    dynamic_slice x2 -> x0, local copies, waits for them, and re-layouts: 3.28 us -> none  [on_device(): lax.dynamic_index_in_dim(cut, req_id ^ j, 1, False)]
    dot_general x12 -> x24, matrix products: 10.2 us -> 13 us  [the longest x8 6.81 us: partial_gate_up(): jnp.dot(flat, w, preferred_element_type=F32).astype(BF16)]
    reshape x5 -> x1, local copies, waits for them, and re-layouts: 2.65 us -> 0.09 us  [partial_gate_up(): return both.reshape(len(feds), reqs, rows, -1).transpose(1, 0, 2, 3)]
  transfers between devices with their start and end apart: 50 -> 36, of which waited for: 23 -> 22; matrix products, arithmetic and copies ran while one was open for 10% -> 9% of each run, Pallas kernels for 6% -> 10%
where the time goes in v3:
time: 162 us
  waiting for transfers between devices  84.8 us (52%)
  starting transfers between devices  35.6 us (22%)
  Pallas kernels  21.6 us (13%)
  matrix products  13 us (8%)
  local copies, waits for them, and re-layouts  3.12 us (2%)
  other arithmetic  2.32 us (1%)
  between operations  1.97 us (1%)
    ppermute x36, waiting for transfers between devices, swap(): lax.ppermute(a, axis, [(i, i ^ mask) for i in range(lax.axis_size(axis))])  84.8 us
    ppermute x36, starting transfers between devices, swap(): lax.ppermute(a, axis, [(i, i ^ mask) for i in range(lax.axis_size(axis))])  35.6 us
    pallas_call x5, Pallas kernels, staged(): pl.pallas_call(kernel, in_specs=[SMEM] * len(scalars) + [HBM] * count, ou...  14.7 us
    pallas_call x1, Pallas kernels, attend_next(): pl.pallas_call(functools.partial(attention_body, (first_m, count, rows, 1...  6.87 us
    dot_general x8, matrix products, partial_gate_up(): jnp.dot(flat, w, preferred_element_type=F32).astype(BF16)  6.81 us
  transfers between devices with their start and end apart: 36, of which 22 were waited for; matrix products, arithmetic and copies ran while one was open for 9% of the time, Pallas kernels for 10%

profile of v3, /device:TPU:0, one launch (start us, length us, event | category | flops | bytes accessed | tf_op | source)
XLA Modules:
  0.0 162.4 jit_solution(2326929766242274790)
XLA Ops:
  2.4 5.8 %attend_first.1 = (bf16[32,128,128]{2,1,0:T(8,128)(2,1)}, bf16[32,128,128]{2,1,0:T(8,128)(2,1)}, bf16[256,512]{1,0:T(8,128)(2,1)}, s32[1,4096]{1,0:T(1,128)}, bf...) custom-call(s32[4]{0:T(128)} %pad_add_fusion.refs_0_, s32[1,64]{1,0:T(1,128)} %refs_1_.1, ...), custom_call_target="tpu_custom_call" | custom-call | tf_op jit(solution)/shard_map/attend_first/pallas_call | solution.py:39
  9.7 1.7 %copy-done = bf16[256,5120]{1,0:T(8,128)(2,1)S(1)} copy-done((bf16[256,5120]{1,0:T(8,128)(2,1)S(1)}, bf16[256,5120]{1,0:T(8,128)(2,1)}, u32[]{:S(2)}) %copy-start) | copy-done | bytes 2621464
  12.2 2.3 %project.2 = bf16[32,5120]{1,0:T(8,128)(2,1)S(1)} custom-call(s32[4]{0:T(128)S(1)} %copy-done.7, bf16[32,640]{1,0:T(8,128)(2,1)S(1)} %copy-done.6, bf16[32,640]{1,0:T(8,128)(2,1)S(1)} %collective-permute-done.refs_2_, bf16[256,5120]{1,0:T(8,128)(2,1)S(1)} %copy-done, bf16[256,5120]{1,0:T(8,128)(2,1)S(1)} %collective-permute-done.1.refs_4_), custom_call_target="tpu_custom_call" | custom-call | tf_op jit(solution)/shard_map/project/pallas_call | solution.py:39
  14.5 3.0 %collective-permute-start.6 = (bf16[32,5120]{1,0:T(8,128)(2,1)S(1)}, bf16[32,5120]{1,0:T(8,128)(2,1)S(1)}, u32[]{:S(2)}, u32[]{:S(2)}) collective-permute-start(bf16[32,5120]{1,0:T(8,128)(2,1)S(1)} %project.2), channel_id=1, source_target_pairs={{0,2},{2,0},{4,6},{6,4},{1,3},{3,1},{5,7},{7,5},{8,10},{10,8},{12,... | collective-permute-start | bytes 983048 | tf_op jit(solution)/shard_map/ppermute | solution.py:52
  17.5 6.9 %attend_next.1 = (bf16[96,640]{1,0:T(8,128)(2,1)S(1)}, bf16[96,640]{1,0:T(8,128)(2,1)S(1)}) custom-call(s32[4]{0:T(128)S(1)} %copy-done.7, bf16[32,128,128]{2,1,0:T(8,128)(2,1)S(1)} %copy-done.2, bf16[32,128,128]{2,1,0:T(8,128)(2,1)S(1)} %copy-done.3, bf16[256,512]{1,0:T(8,128)(2,1)S(1)} %copy-done.5, s32[1,4096]{1,0:T(1,128)S(1)} %copy-done.8), custom_call_target="tpu_custom_call" | custom-call | tf_op jit(solution)/shard_map/attend_next/pallas_call | solution.py:234
  24.7 1.4 collective-permute-start.3
  26.1 1.7 %collective-permute-start.4 = (bf16[896,640]{1,0:T(8,128)(2,1)S(1)}, bf16[896,640]{1,0:T(8,128)(2,1)S(1)}, u32[]{:S(2)}, u32[]{:S(2)}) collective-permute-start(bf16[896,640]{1,0:T(8,128)(2,1)S(1)} %get-tuple-element.75), channel_id=1, source_target_pairs={{0,16},{8,24},{16,0},{24,8},{1,17},{9,25},{17,1},{25,9},{2,18},{10... | collective-permute-start | bytes 3440648 | tf_op jit(solution)/shard_map/ppermute | solution.py:52
  27.9 2.5 %project.3 = (bf16[32,5120]{1,0:T(8,128)(2,1)S(1)}, bf16[32,5120]{1,0:T(8,128)(2,1)S(1)}, bf16[32,5120]{1,0:T(8,128)(2,1)S(1)}) custom-call(s32[4]{0:T(128)S(1)} %copy-done.7, bf16[96,640]{1,0:T(8,128)(2,1)S(1)} %get-tuple-element.46.refs_1_, bf16[96,640]{1,0:T(8,128)(2,1)S(1)} %collective-permute-done.2.refs_2_, bf16[256,5120]{1,0:T(8,128)(2,1)S(1)} %copy-done.1, ...), custom_call_target="tpu_custom_call" | custom-call | tf_op jit(solution)/shard_map/project/pallas_call | solution.py:39
  31.0 2.7 %collective-permute-start.7 = (bf16[32,5120]{1,0:T(8,128)(2,1)S(1)}, bf16[32,5120]{1,0:T(8,128)(2,1)S(1)}, u32[]{:S(2)}, u32[]{:S(2)}) collective-permute-start(bf16[32,5120]{1,0:T(8,128)(2,1)S(1)} %add_convert_fusion.2), channel_id=1, source_target_pairs={{0,4},{2,6},{4,0},{6,2},{1,5},{3,7},{5,1},{7,3},{8,12},{10,14},{12... | collective-permute-start | bytes 983048 | tf_op jit(solution)/shard_map/ppermute | solution.py:52
  33.7 18.7 %collective-permute-done.3 = bf16[896,640]{1,0:T(8,128)(2,1)S(1)} collective-permute-done((bf16[896,640]{1,0:T(8,128)(2,1)S(1)}, bf16[896,640]{1,0:T(8,128)(2,1)S(1)}, u32[]{:S(2)}, u32[]{:S(2)}) %collective-permute-start.3) | collective-permute-done | bytes 1146912 | tf_op jit(solution)/shard_map/ppermute | solution.py:52
  53.5 1.6 norm_cut.1
  55.9 1.5 collective-permute-start.9
  61.1 1.6 %collective-permute-done.10 = bf16[32,1280]{1,0:T(8,128)(2,1)S(1)} collective-permute-done((bf16[32,1280]{1,0:T(8,128)(2,1)S(1)}, bf16[32,1280]{1,0:T(8,128)(2,1)S(1)}, u32[]{:S(2)}, u32[]{:S(2)}) %collective-permute-start.10) | collective-permute-done | bytes 81952 | tf_op jit(solution)/shard_map/ppermute | solution.py:52
  62.8 2.7 %collective-permute-start.11 = (bf16[4,32,1280]{2,1,0:T(8,128)(2,1)S(1)}, bf16[4,32,1280]{2,1,0:T(8,128)(2,1)S(1)}, u32[]{:S(2)}, u32[]{:S(2)}) collective-permute-start(bf16[4,32,1280]{2,1,0:T(8,128)(2,1)S(1)} %pad_maximum_fusion.8), channel_id=1, source_target_pairs={{0,4},{2,6},{4,0},{6,2},{1,5},{3,7},{5,1},{7,3},{8,12},{10,14},{12... | collective-permute-start | bytes 983048 | tf_op jit(solution)/shard_map/ppermute | solution.py:52
  65.9 13.1 %collective-permute-done.11 = bf16[4,32,1280]{2,1,0:T(8,128)(2,1)S(1)} collective-permute-done((bf16[4,32,1280]{2,1,0:T(8,128)(2,1)S(1)}, bf16[4,32,1280]{2,1,0:T(8,128)(2,1)S(1)}, u32[]{:S(2)}, u32[]{:S(2)}) %collective-permute-start.11) | collective-permute-done | bytes 327712 | tf_op jit(solution)/shard_map/ppermute | solution.py:52
  92.6 11.5 %collective-permute-done.13 = bf16[2,3,32,1792]{3,2,0,1:T(8,128)(2,1)S(1)} collective-permute-done((bf16[2,3,32,1792]{3,2,0,1:T(8,128)(2,1)S(1)}, bf16[2,3,32,1792]{3,2,0,1:T(8,128)(2,1)S(1)}, u32[]{:S(2)}, u32[]{:S(2)}) %collective-permute-start.13) | collective-permute-done | bytes 688160 | tf_op jit(solution)/shard_map/ppermute | solution.py:52
  105.1 1.5 collective-permute-done.18
  107.9 1.5 collective-permute-start.21
  109.9 7.1 %collective-permute-done.20 = bf16[4,32,1792]{2,1,0:T(8,128)(2,1)S(1)} collective-permute-done((bf16[4,32,1792]{2,1,0:T(8,128)(2,1)S(1)}, bf16[4,32,1792]{2,1,0:T(8,128)(2,1)S(1)}, u32[]{:S(2)}, u32[]{:S(2)}) %collective-permute-start.20) | collective-permute-done | bytes 458784 | tf_op jit(solution)/shard_map/ppermute | solution.py:52
  121.1 1.8 %collective-permute-start.27 = (bf16[32,2560]{1,0:T(8,128)(2,1)S(1)}, bf16[32,2560]{1,0:T(8,128)(2,1)S(1)}, u32[]{:S(2)}, u32[]{:S(2)}) collective-permute-start(bf16[32,2560]{1,0:T(8,128)(2,1)S(1)} %get-tuple-element.79), channel_id=1, source_target_pairs={{0,2},{2,0},{4,6},{6,4},{1,3},{3,1},{5,7},{7,5},{8,10},{10,8},{12,... | collective-permute-start | bytes 491528 | tf_op jit(solution)/shard_map/ppermute | solution.py:52
  122.9 1.6 collective-permute-start.29
  125.9 2.3 %collective-permute-done.27 = bf16[32,2560]{1,0:T(8,128)(2,1)S(1)} collective-permute-done((bf16[32,2560]{1,0:T(8,128)(2,1)S(1)}, bf16[32,2560]{1,0:T(8,128)(2,1)S(1)}, u32[]{:S(2)}, u32[]{:S(2)}) %collective-permute-start.27) | collective-permute-done | bytes 163872 | tf_op jit(solution)/shard_map/ppermute | solution.py:52
  128.2 2.2 %collective-permute-start.28 = (bf16[32,2560]{1,0:T(8,128)(2,1)S(1)}, bf16[32,2560]{1,0:T(8,128)(2,1)S(1)}, u32[]{:S(2)}, u32[]{:S(2)}) collective-permute-start(bf16[32,2560]{1,0:T(8,128)(2,1)S(1)} %add_convert_fusion.6), channel_id=1, source_target_pairs={{0,4},{2,6},{4,0},{6,2},{1,5},{3,7},{5,1},{7,3},{8,12},{10,14},{12... | collective-permute-start | bytes 491528 | tf_op jit(solution)/shard_map/ppermute | solution.py:52
  130.4 4.9 %collective-permute-done.29 = bf16[128,1792]{1,0:T(8,128)(2,1)S(1)} collective-permute-done((bf16[128,1792]{1,0:T(8,128)(2,1)S(1)}, bf16[128,1792]{1,0:T(8,128)(2,1)S(1)}, u32[]{:S(2)}, u32[]{:S(2)}) %collective-permute-start.29) | collective-permute-done | bytes 458784 | tf_op jit(solution)/shard_map/ppermute | solution.py:52
  139.0 1.6 collective-permute-start.31
  140.6 4.9 %collective-permute-done.32 = bf16[32,2560]{1,0:T(8,128)(2,1)S(1)} collective-permute-done((bf16[32,2560]{1,0:T(8,128)(2,1)S(1)}, bf16[32,2560]{1,0:T(8,128)(2,1)S(1)}, u32[]{:S(2)}, u32[]{:S(2)}) %collective-permute-start.32) | collective-permute-done | bytes 163872 | tf_op jit(solution)/shard_map/ppermute | solution.py:52
  146.8 2.3 %collective-permute-done.31 = bf16[32,2560]{1,0:T(8,128)(2,1)S(1)} collective-permute-done((bf16[32,2560]{1,0:T(8,128)(2,1)S(1)}, bf16[32,2560]{1,0:T(8,128)(2,1)S(1)}, u32[]{:S(2)}, u32[]{:S(2)}) %collective-permute-start.31) | collective-permute-done | bytes 163872 | tf_op jit(solution)/shard_map/ppermute | solution.py:52
  149.1 4.6 %collective-permute-done.33 = bf16[32,2560]{1,0:T(8,128)(2,1)S(1)} collective-permute-done((bf16[32,2560]{1,0:T(8,128)(2,1)S(1)}, bf16[32,2560]{1,0:T(8,128)(2,1)S(1)}, u32[]{:S(2)}, u32[]{:S(2)}) %collective-permute-start.33) | collective-permute-done | bytes 163872 | tf_op jit(solution)/shard_map/ppermute | solution.py:52
  153.8 1.5 collective-permute-start.34
  156.6 1.7 %collective-permute-done.34.refs_6_ = bf16[32,1280]{1,0:T(8,128)(2,1)S(1)} collective-permute-done((bf16[32,1280]{1,0:T(8,128)(2,1)S(1)}, bf16[32,1280]{1,0:T(8,128)(2,1)S(1)}, u32[]{:S(2)}, u32[]{:S(2)}) %collective-permute-start.34) | collective-permute-done | bytes 81952 | tf_op jit(solution)/shard_map/ppermute | solution.py:52
  158.3 1.5 collective-permute-done.35.refs_5_
  159.7 2.5 %finish.1 = bf16[32,5120]{1,0:T(8,128)(2,1)} custom-call(s32[4]{0:T(128)S(1)} %copy-done.7, f32[32,5120]{1,0:T(8,128)S(1)} %get-tuple-element.52.refs_1_, bf16[32,2560]{1,0:T(8,128)(2,1)S(1)} %get-tuple-element.81.refs_2_, bf16[32,2560]{1,0:T(8,128)(2,1)S(1)} %collective-permute-done.26.refs_3_, bf16[32,2560]{1,0:T(8,128)(2,1)S(1)} %collective-permute-done.28.refs_4_, ...), custom_call_target="tpu_custom_call" | custom-call | tf_op jit(solution)/shard_map/finish/pallas_call | solution.py:39
  (133 shorter events, 38.2 us)
Async XLA Ops:
  0.6 9.1 %collective-permute-start.1 = (bf16[256,5120]{1,0:T(8,128)(2,1)}, bf16[256,5120]{1,0:T(8,128)(2,1)S(1)}, u32[]{:S(2)}, u32[]{:S(2)}) collective-permute-start(bf16[256,5120]{1,0:T(8,128)(2,1)} %refs_3_.3), channel_id=1, source_target_pairs={{0,1},{1,0},{2,3},{3,2},{4,5},{5,4},{6,7},{7,6},{8,9},{9,8},{10,11... | collective-permute-start | bytes 7864328 | tf_op jit(solution)/shard_map/ppermute | solution.py:52
  14.5 16.4 %collective-permute-start.6 = (bf16[32,5120]{1,0:T(8,128)(2,1)S(1)}, bf16[32,5120]{1,0:T(8,128)(2,1)S(1)}, u32[]{:S(2)}, u32[]{:S(2)}) collective-permute-start(bf16[32,5120]{1,0:T(8,128)(2,1)S(1)} %project.2), channel_id=1, source_target_pairs={{0,2},{2,0},{4,6},{6,4},{1,3},{3,1},{5,7},{7,5},{8,10},{10,8},{12,... | collective-permute-start | bytes 983048 | tf_op jit(solution)/shard_map/ppermute | solution.py:52
  24.7 27.7 %collective-permute-start.3 = (bf16[896,640]{1,0:T(8,128)(2,1)S(1)}, bf16[896,640]{1,0:T(8,128)(2,1)S(1)}, u32[]{:S(2)}, u32[]{:S(2)}) collective-permute-start(bf16[896,640]{1,0:T(8,128)(2,1)S(1)} %get-tuple-element.76), channel_id=1, source_target_pairs={{0,8},{8,0},{16,24},{24,16},{1,9},{9,1},{17,25},{25,17},{2,10},{10... | collective-permute-start | bytes 3440648 | tf_op jit(solution)/shard_map/ppermute | solution.py:52
  26.1 27.3 %collective-permute-start.4 = (bf16[896,640]{1,0:T(8,128)(2,1)S(1)}, bf16[896,640]{1,0:T(8,128)(2,1)S(1)}, u32[]{:S(2)}, u32[]{:S(2)}) collective-permute-start(bf16[896,640]{1,0:T(8,128)(2,1)S(1)} %get-tuple-element.75), channel_id=1, source_target_pairs={{0,16},{8,24},{16,0},{24,8},{1,17},{9,25},{17,1},{25,9},{2,18},{10... | collective-permute-start | bytes 3440648 | tf_op jit(solution)/shard_map/ppermute | solution.py:52
  30.4 23.1 %collective-permute-start.5 = (bf16[32,5120]{1,0:T(8,128)(2,1)S(1)}, bf16[32,5120]{1,0:T(8,128)(2,1)S(1)}, u32[]{:S(2)}, u32[]{:S(2)}) collective-permute-start(bf16[32,5120]{1,0:T(8,128)(2,1)S(1)} %get-tuple-element.50), channel_id=1, source_target_pairs={{0,2},{2,0},{4,6},{6,4},{1,3},{3,1},{5,7},{7,5},{8,10},{10,8},{12,... | collective-permute-start | bytes 983048 | tf_op jit(solution)/shard_map/ppermute | solution.py:52
  31.0 22.5 %collective-permute-start.7 = (bf16[32,5120]{1,0:T(8,128)(2,1)S(1)}, bf16[32,5120]{1,0:T(8,128)(2,1)S(1)}, u32[]{:S(2)}, u32[]{:S(2)}) collective-permute-start(bf16[32,5120]{1,0:T(8,128)(2,1)S(1)} %add_convert_fusion.2), channel_id=1, source_target_pairs={{0,4},{2,6},{4,0},{6,2},{1,5},{3,7},{5,1},{7,3},{8,12},{10,14},{12... | collective-permute-start | bytes 983048 | tf_op jit(solution)/shard_map/ppermute | solution.py:52
  33.7 49.6 %collective-permute-start.15 = (bf16[1280,896]{1,0:T(8,128)(2,1)S(1)}, bf16[1280,896]{1,0:T(8,128)(2,1)S(1)}, u32[]{:S(2)}, u32[]{:S(2)}) collective-permute-start(bf16[1280,896]{1,0:T(8,128)(2,1)S(1)} %copy-done.9), channel_id=1, source_target_pairs={{0,1},{1,0},{2,3},{3,2},{4,5},{5,4},{6,7},{7,6},{8,9},{9,8},{10,11... | collective-permute-start | bytes 6881288 | tf_op jit(solution)/shard_map/ppermute | solution.py:52
  52.4 32.0 %collective-permute-start.14 = (bf16[1280,896]{1,0:T(8,128)(2,1)S(1)}, bf16[1280,896]{1,0:T(8,128)(2,1)S(1)}, u32[]{:S(2)}, u32[]{:S(2)}) collective-permute-start(bf16[1280,896]{1,0:T(8,128)(2,1)S(1)} %copy-done.10), channel_id=1, source_target_pairs={{0,1},{1,0},{2,3},{3,2},{4,5},{5,4},{6,7},{7,6},{8,9},{9,8},{10,11... | collective-permute-start | bytes 6881288 | tf_op jit(solution)/shard_map/ppermute | solution.py:52
  55.1 4.7 %collective-permute-start.8 = (bf16[32,1280]{1,0:T(8,128)(2,1)S(1)}, bf16[32,1280]{1,0:T(8,128)(2,1)S(1)}, u32[]{:S(2)}, u32[]{:S(2)}) collective-permute-start(bf16[32,1280]{1,0:T(8,128)(2,1)S(1)} %get-tuple-element.54), channel_id=1, source_target_pairs={{0,8},{8,0},{16,24},{24,16},{1,9},{9,1},{17,25},{25,17},{2,10},{10... | collective-permute-start | bytes 245768 | tf_op jit(solution)/shard_map/ppermute | solution.py:52
  55.9 5.2 %collective-permute-start.9 = (bf16[32,1280]{1,0:T(8,128)(2,1)S(1)}, bf16[32,1280]{1,0:T(8,128)(2,1)S(1)}, u32[]{:S(2)}, u32[]{:S(2)}) collective-permute-start(bf16[32,1280]{1,0:T(8,128)(2,1)S(1)} %get-tuple-element.55), channel_id=1, source_target_pairs={{0,16},{8,24},{16,0},{24,8},{1,17},{9,25},{17,1},{25,9},{2,18},{10... | collective-permute-start | bytes 245768 | tf_op jit(solution)/shard_map/ppermute | solution.py:52
  57.4 5.3 %collective-permute-start.10 = (bf16[32,1280]{1,0:T(8,128)(2,1)S(1)}, bf16[32,1280]{1,0:T(8,128)(2,1)S(1)}, u32[]{:S(2)}, u32[]{:S(2)}) collective-permute-start(bf16[32,1280]{1,0:T(8,128)(2,1)S(1)} %get-tuple-element.56), channel_id=1, source_target_pairs={{0,24},{8,16},{16,8},{24,0},{1,25},{9,17},{17,9},{25,1},{2,26},{10... | collective-permute-start | bytes 245768 | tf_op jit(solution)/shard_map/ppermute | solution.py:52
  62.8 16.3 %collective-permute-start.11 = (bf16[4,32,1280]{2,1,0:T(8,128)(2,1)S(1)}, bf16[4,32,1280]{2,1,0:T(8,128)(2,1)S(1)}, u32[]{:S(2)}, u32[]{:S(2)}) collective-permute-start(bf16[4,32,1280]{2,1,0:T(8,128)(2,1)S(1)} %pad_maximum_fusion.8), channel_id=1, source_target_pairs={{0,4},{2,6},{4,0},{6,2},{1,5},{3,7},{5,1},{7,3},{8,12},{10,14},{12... | collective-permute-start | bytes 983048 | tf_op jit(solution)/shard_map/ppermute | solution.py:52
  65.4 14.9 %collective-permute-start.12 = (bf16[4,32,1280]{2,1,0:T(8,128)(2,1)S(1)}, bf16[4,32,1280]{2,1,0:T(8,128)(2,1)S(1)}, u32[]{:S(2)}, u32[]{:S(2)}) collective-permute-start(bf16[4,32,1280]{2,1,0:T(8,128)(2,1)S(1)} %pad_maximum_fusion.8), channel_id=1, source_target_pairs={{0,2},{2,0},{4,6},{6,4},{1,3},{3,1},{5,7},{7,5},{8,10},{10,8},{12,... | collective-permute-start | bytes 983048 | tf_op jit(solution)/shard_map/ppermute | solution.py:52
  80.4 8.3 %collective-permute-start.17 = (bf16[4,32,1280]{2,1,0:T(8,128)(2,1)S(1)}, bf16[4,32,1280]{2,1,0:T(8,128)(2,1)S(1)}, u32[]{:S(2)}, u32[]{:S(2)}) collective-permute-start(bf16[4,32,1280]{2,1,0:T(8,128)(2,1)S(1)} %collective-permute-done.11), channel_id=1, source_target_pairs={{0,2},{2,0},{4,6},{6,4},{1,3},{3,1},{5,7},{7,5},{8,10},{10,8},{12,... | collective-permute-start | bytes 983048 | tf_op jit(solution)/shard_map/ppermute | solution.py:52
  86.0 18.1 %collective-permute-start.13 = (bf16[2,3,32,1792]{3,2,0,1:T(8,128)(2,1)S(1)}, bf16[2,3,32,1792]{3,2,0,1:T(8,128)(2,1)S(1)}, u32[]{:S(2)}, u32[]{:S(2)}) collective-permute-start(bf16[2,3,32,1792]{3,2,0,1:T(8,128)(2,1)S(1)} %slice.93), channel_id=1, source_target_pairs={{0,8},{8,0},{16,24},{24,16},{1,9},{9,1},{17,25},{25,17},{2,10},{10... | collective-permute-start | bytes 2064392 | tf_op jit(solution)/shard_map/ppermute | solution.py:52
  86.9 17.8 %collective-permute-start.16 = (bf16[2,3,32,1792]{3,2,1,0:T(8,128)(2,1)S(1)}, bf16[2,3,32,1792]{3,2,1,0:T(8,128)(2,1)S(1)}, u32[]{:S(2)}, u32[]{:S(2)}) collective-permute-start(bf16[2,3,32,1792]{3,2,1,0:T(8,128)(2,1)S(1)} %slice.117), channel_id=1, source_target_pairs={{0,16},{8,24},{16,0},{24,8},{1,17},{9,25},{17,1},{25,9},{2,18},{10... | collective-permute-start | bytes 2064392 | tf_op jit(solution)/shard_map/ppermute | solution.py:52
  89.8 16.8 %collective-permute-start.18 = (bf16[2,1,32,1792]{3,2,0,1:T(8,128)(2,1)S(1)}, bf16[2,1,32,1792]{3,2,0,1:T(8,128)(2,1)S(1)}, u32[]{:S(2)}, u32[]{:S(2)}) collective-permute-start(bf16[2,1,32,1792]{3,2,0,1:T(8,128)(2,1)S(1)} %slice.96), channel_id=1, source_target_pairs={{0,8},{8,0},{16,24},{24,16},{1,9},{9,1},{17,25},{25,17},{2,10},{10... | collective-permute-start | bytes 688136 | tf_op jit(solution)/shard_map/ppermute | solution.py:52
  91.7 15.6 %collective-permute-start.19 = (bf16[2,1,32,1792]{3,2,1,0:T(8,128)(2,1)S(1)}, bf16[2,1,32,1792]{3,2,1,0:T(8,128)(2,1)S(1)}, u32[]{:S(2)}, u32[]{:S(2)}) collective-permute-start(bf16[2,1,32,1792]{3,2,1,0:T(8,128)(2,1)S(1)} %bitcast.116), channel_id=1, source_target_pairs={{0,16},{8,24},{16,0},{24,8},{1,17},{9,25},{17,1},{25,9},{2,18},{10... | collective-permute-start | bytes 688136 | tf_op jit(solution)/shard_map/ppermute | solution.py:52
  107.4 9.6 %collective-permute-start.20 = (bf16[4,32,1792]{2,1,0:T(8,128)(2,1)S(1)}, bf16[4,32,1792]{2,1,0:T(8,128)(2,1)S(1)}, u32[]{:S(2)}, u32[]{:S(2)}) collective-permute-start(bf16[4,32,1792]{2,1,0:T(8,128)(2,1)S(1)} %fusion.15), channel_id=1, source_target_pairs={{0,16},{8,24},{16,0},{24,8},{1,17},{9,25},{17,1},{25,9},{2,18},{10... | collective-permute-start | bytes 1376264 | tf_op jit(solution)/shard_map/ppermute | solution.py:52
  107.9 9.1 %collective-permute-start.21 = (bf16[4,32,1792]{2,1,0:T(8,128)(2,1)S(1)}, bf16[4,32,1792]{2,1,0:T(8,128)(2,1)S(1)}, u32[]{:S(2)}, u32[]{:S(2)}) collective-permute-start(bf16[4,32,1792]{2,1,0:T(8,128)(2,1)S(1)} %fusion.9), channel_id=1, source_target_pairs={{0,8},{8,0},{16,24},{24,16},{1,9},{9,1},{17,25},{25,17},{2,10},{10... | collective-permute-start | bytes 1376264 | tf_op jit(solution)/shard_map/ppermute | solution.py:52
  109.4 10.8 %collective-permute-start.23 = (bf16[896,640]{1,0:T(8,128)(2,1)S(1)}, bf16[896,640]{1,0:T(8,128)(2,1)S(1)}, u32[]{:S(2)}, u32[]{:S(2)}) collective-permute-start(bf16[896,640]{1,0:T(8,128)(2,1)S(1)} %get-tuple-element.75), channel_id=1, source_target_pairs={{0,1},{1,0},{2,3},{3,2},{4,5},{5,4},{6,7},{7,6},{8,9},{9,8},{10,11... | collective-permute-start | bytes 3440648 | tf_op jit(solution)/shard_map/ppermute | solution.py:52
  109.4 11.2 %collective-permute-start.22 = (bf16[896,640]{1,0:T(8,128)(2,1)S(1)}, bf16[896,640]{1,0:T(8,128)(2,1)S(1)}, u32[]{:S(2)}, u32[]{:S(2)}) collective-permute-start(bf16[896,640]{1,0:T(8,128)(2,1)S(1)} %get-tuple-element.76), channel_id=1, source_target_pairs={{0,1},{1,0},{2,3},{3,2},{4,5},{5,4},{6,7},{7,6},{8,9},{9,8},{10,11... | collective-permute-start | bytes 3440648 | tf_op jit(solution)/shard_map/ppermute | solution.py:52
  109.9 9.2 %collective-permute-start.25 = (bf16[896,640]{1,0:T(8,128)(2,1)S(1)}, bf16[896,640]{1,0:T(8,128)(2,1)S(1)}, u32[]{:S(2)}, u32[]{:S(2)}) collective-permute-start(bf16[896,640]{1,0:T(8,128)(2,1)S(1)} %collective-permute-done.4), channel_id=1, source_target_pairs={{0,1},{1,0},{2,3},{3,2},{4,5},{5,4},{6,7},{7,6},{8,9},{9,8},{10,11... | collective-permute-start | bytes 3440648 | tf_op jit(solution)/shard_map/ppermute | solution.py:52
  121.1 7.1 %collective-permute-start.27 = (bf16[32,2560]{1,0:T(8,128)(2,1)S(1)}, bf16[32,2560]{1,0:T(8,128)(2,1)S(1)}, u32[]{:S(2)}, u32[]{:S(2)}) collective-permute-start(bf16[32,2560]{1,0:T(8,128)(2,1)S(1)} %get-tuple-element.79), channel_id=1, source_target_pairs={{0,2},{2,0},{4,6},{6,4},{1,3},{3,1},{5,7},{7,5},{8,10},{10,8},{12,... | collective-permute-start | bytes 491528 | tf_op jit(solution)/shard_map/ppermute | solution.py:52
  122.9 12.4 %collective-permute-start.29 = (bf16[128,1792]{1,0:T(8,128)(2,1)S(1)}, bf16[128,1792]{1,0:T(8,128)(2,1)S(1)}, u32[]{:S(2)}, u32[]{:S(2)}) collective-permute-start(bf16[128,1792]{1,0:T(8,128)(2,1)S(1)} %bitcast.95), channel_id=1, source_target_pairs={{0,16},{8,24},{16,0},{24,8},{1,17},{9,25},{17,1},{25,9},{2,18},{10... | collective-permute-start | bytes 1376264 | tf_op jit(solution)/shard_map/ppermute | solution.py:52
  124.5 10.8 %collective-permute-start.30 = (bf16[128,1792]{1,0:T(8,128)(2,1)S(1)}, bf16[128,1792]{1,0:T(8,128)(2,1)S(1)}, u32[]{:S(2)}, u32[]{:S(2)}) collective-permute-start(bf16[128,1792]{1,0:T(8,128)(2,1)S(1)} %bitcast.96), channel_id=1, source_target_pairs={{0,8},{8,0},{16,24},{24,16},{1,9},{9,1},{17,25},{25,17},{2,10},{10... | collective-permute-start | bytes 1376264 | tf_op jit(solution)/shard_map/ppermute | solution.py:52
  125.7 12.8 %collective-permute-start.26 = (bf16[32,2560]{1,0:T(8,128)(2,1)S(1)}, bf16[32,2560]{1,0:T(8,128)(2,1)S(1)}, u32[]{:S(2)}, u32[]{:S(2)}) collective-permute-start(bf16[32,2560]{1,0:T(8,128)(2,1)S(1)} %get-tuple-element.80), channel_id=1, source_target_pairs={{0,2},{2,0},{4,6},{6,4},{1,3},{3,1},{5,7},{7,5},{8,10},{10,8},{12,... | collective-permute-start | bytes 491528 | tf_op jit(solution)/shard_map/ppermute | solution.py:52
  128.2 10.3 %collective-permute-start.28 = (bf16[32,2560]{1,0:T(8,128)(2,1)S(1)}, bf16[32,2560]{1,0:T(8,128)(2,1)S(1)}, u32[]{:S(2)}, u32[]{:S(2)}) collective-permute-start(bf16[32,2560]{1,0:T(8,128)(2,1)S(1)} %add_convert_fusion.6), channel_id=1, source_target_pairs={{0,4},{2,6},{4,0},{6,2},{1,5},{3,7},{5,1},{7,3},{8,12},{10,14},{12... | collective-permute-start | bytes 491528 | tf_op jit(solution)/shard_map/ppermute | solution.py:52
  138.5 7.0 %collective-permute-start.32 = (bf16[32,2560]{1,0:T(8,128)(2,1)S(1)}, bf16[32,2560]{1,0:T(8,128)(2,1)S(1)}, u32[]{:S(2)}, u32[]{:S(2)}) collective-permute-start(bf16[32,2560]{1,0:T(8,128)(2,1)S(1)} %get-tuple-element.72), channel_id=1, source_target_pairs={{0,2},{2,0},{4,6},{6,4},{1,3},{3,1},{5,7},{7,5},{8,10},{10,8},{12,... | collective-permute-start | bytes 491528 | tf_op jit(solution)/shard_map/ppermute | solution.py:52
  139.0 10.0 %collective-permute-start.31 = (bf16[32,2560]{1,0:T(8,128)(2,1)S(1)}, bf16[32,2560]{1,0:T(8,128)(2,1)S(1)}, u32[]{:S(2)}, u32[]{:S(2)}) collective-permute-start(bf16[32,2560]{1,0:T(8,128)(2,1)S(1)} %get-tuple-element.77), channel_id=1, source_target_pairs={{0,2},{2,0},{4,6},{6,4},{1,3},{3,1},{5,7},{7,5},{8,10},{10,8},{12,... | collective-permute-start | bytes 491528 | tf_op jit(solution)/shard_map/ppermute | solution.py:52
  145.6 8.0 %collective-permute-start.33 = (bf16[32,2560]{1,0:T(8,128)(2,1)S(1)}, bf16[32,2560]{1,0:T(8,128)(2,1)S(1)}, u32[]{:S(2)}, u32[]{:S(2)}) collective-permute-start(bf16[32,2560]{1,0:T(8,128)(2,1)S(1)} %add_convert_fusion.5), channel_id=1, source_target_pairs={{0,4},{2,6},{4,0},{6,2},{1,5},{3,7},{5,1},{7,3},{8,12},{10,14},{12... | collective-permute-start | bytes 491528 | tf_op jit(solution)/shard_map/ppermute | solution.py:52
  153.8 4.5 %collective-permute-start.34 = (bf16[32,1280]{1,0:T(8,128)(2,1)S(1)}, bf16[32,1280]{1,0:T(8,128)(2,1)S(1)}, u32[]{:S(2)}, u32[]{:S(2)}) collective-permute-start(bf16[32,1280]{1,0:T(8,128)(2,1)S(1)} %get-tuple-element.85), channel_id=1, source_target_pairs={{0,16},{8,24},{16,0},{24,8},{1,17},{9,25},{17,1},{25,9},{2,18},{10... | collective-permute-start | bytes 245768 | tf_op jit(solution)/shard_map/ppermute | solution.py:52
  (17 other events, 118.5 us)

commit v4 on v3

--- a/solution.py
+++ b/solution.py
@@ -48,6 +48,18 @@
     )(*scalars, *arrays)
 
 
+def direct(body, scalars, arrays, out_shape, scratch, limit, name):
+    return pl.pallas_call(
+        body,
+        in_specs=[SMEM] * len(scalars) + [VMEM] * len(arrays),
+        out_specs=[VMEM] * len(out_shape),
+        out_shape=out_shape,
+        scratch_shapes=list(scratch),
+        compiler_params=pltpu.CompilerParams(vmem_limit_bytes=limit * 2**20),
+        name=name,
+    )(*scalars, *arrays)
+
+
 def swap(a, axis, mask):
     return lax.ppermute(a, axis, [(i, i ^ mask) for i in range(lax.axis_size(axis))])
 
@@ -86,7 +98,7 @@
 def reduce_both_ways(nears, fars, axis):
     sums_near, sums_far = [], []
     for near, far in zip(nears, fars):
-        came = bind(True, swap(near[1::2], axis, 1), swap(far[2:], axis, 2), *sums_near, *sums_far)
+        came = bind(len(sums_near) > 0, swap(near[1::2], axis, 1), swap(far[2:], axis, 2), *sums_near, *sums_far)
         sums_near.append((near[::2].astype(F32) + came[0].astype(F32)).astype(BF16))
         sums_far.append((far[:2].astype(F32) + came[1].astype(F32)).astype(BF16))
     near, far = jnp.concatenate(sums_near, 1), jnp.concatenate(sums_far, 1)
@@ -237,6 +249,7 @@
         out_specs=[VMEM] * 2,
         out_shape=[jax.ShapeDtypeStruct((side, width + head_dim), BF16)] * 2,
         compiler_params=pltpu.CompilerParams(vmem_limit_bytes=40 * 2**20),
+        cost_estimate=pl.CostEstimate(flops=8 * 10**9, bytes_accessed=10**6, transcendentals=0),
         name="attend_next",
     )(scal, keys, values, q_rot, key_pos)
 
@@ -346,8 +359,8 @@
 
 def finish(scal, parts):
     rows, model = parts[0][0].shape
-    return staged(
-        functools.partial(finish_body, len(parts)), [scal], [a for part in parts for a in part], 0,
+    return direct(
+        functools.partial(finish_body, len(parts)), [scal], [a for part in parts for a in part],
         [jax.ShapeDtypeStruct((len(parts) * rows, model), BF16)], [], 8, "finish")[0]
 
 
@@ -398,6 +411,8 @@
     ).astype(jnp.int32)
     wo_far = swap(wo, "blk", 1)
     fast = reqs == 4 and kvs == 4
+    half = model // reqs // 2
+    cuts = [w_down[:, :half], w_down[:, half:]]
     first_m = kvs - 1 if fast else 0
     keys_out, values_out, q_rot, key_pos, o_keep, o_send = attend_first(
         scal, page_table, q_new[0], k_new[0], v_new[0], k_cache[0, 0], v_cache[0, 0],
@@ -405,12 +420,12 @@
     projected = project(scal, o_keep, swap(o_send, "blk", 1), wo, wo_far, head_dim, kvs - first_m)
     if first_m:
         o_keep, o_send = attend_next(
-            scal, keys_out, values_out, after(q_rot, projected[0]), key_pos, rows, 0, first_m)
+            scal, keys_out, values_out, after(q_rot, projected[0], *cuts), key_pos, rows, 0, first_m)
         o_came = swap(o_send, "blk", 1)
         projected = [*project(scal, o_keep, o_came, wo, wo_far, head_dim, first_m), *projected]
     projected = [list(projected)]
     layer = four_way if fast else any_way
-    layer_out = layer(x_resid[0], projected, scal, norm_gain[None], w_gate, w_up, w_down, reqs, kvs)
+    layer_out = layer(x_resid[0], projected, scal, norm_gain[None], w_gate, w_up, cuts if fast else w_down, reqs, kvs)
     return layer_out[None], keys_out[None, None], values_out[None, None]
 
 
@@ -446,11 +461,10 @@
     return (resid + jnp.concatenate(mlp, 1).astype(F32)).astype(BF16)
 
 
-def four_way(x_resid, projected, scal, gain, w_gate, w_up, w_down, reqs, kvs):
+def four_way(x_resid, projected, scal, gain, w_gate, w_up, cuts, reqs, kvs):
     step, model = projected[0][0].shape
     part = model // reqs
     half = part // 2
-    cuts = [w_down[:, :half], w_down[:, half:]]
     lent = [swap(cut, "req", mask) for cut, mask in zip(cuts, (1, 2))]
     summed, boths = [], []
     for sums in projected:
@@ -463,12 +477,11 @@
     resids, fed = [], []
     held = None
     for c, terms in enumerate(summed):
-        if c == 0:
-            terms[0] = after(terms[0], *lent)
         if held is not None:
             terms[0] = after(terms[0], *held)
         resid, *pieces = norm_cut(scal, x_resid[c * step:(c + 1) * step], terms, gain, reqs)
         resids.append(resid)
+        pieces[1:] = [after(piece, *lent) for piece in pieces[1:]]
         got = jnp.stack(trade(pieces, "req", True))
         two, one = bind(True, swap(got, "kv", 2), swap(got, "kv", 1))
         three = swap(two, "kv", 1)

time: 162 us -> 158 us (0.975)
  waiting for transfers between devices: 84.8 us -> 79.7 us
    ppermute x36, waiting for transfers between devices: 84.8 us -> 79.7 us  [swap(): lax.ppermute(a, axis, [(i, i ^ mask) for i in range(lax.axis_size(axis))])]
    pallas_call x5 -> x4, Pallas kernels: 14.7 us -> 12.2 us  [staged(): pl.pallas_call(kernel, in_specs=[SMEM] * len(scalars) + [HBM] * count, ou...]
    slice x1, local copies, waits for them, and re-layouts: 0.2 us -> 1.96 us  [on_device(): cuts = [w_down[:, :half], w_down[:, half:]]]
  transfers between devices with their start and end apart: 36 -> 36, of which waited for: 22 -> 22; matrix products, arithmetic and copies ran while one was open for 9% -> 11% of each run, Pallas kernels for 10% -> 10%
where the time goes in v4:
time: 158 us
  waiting for transfers between devices  79.7 us (50%)
  starting transfers between devices  36.7 us (23%)
  Pallas kernels  20.2 us (13%)
  matrix products  13 us (8%)
  local copies, waits for them, and re-layouts  3.79 us (2%)
  other arithmetic  2.3 us (1%)
  between operations  1.86 us (1%)
    ppermute x36, waiting for transfers between devices, swap(): lax.ppermute(a, axis, [(i, i ^ mask) for i in range(lax.axis_size(axis))])  79.7 us
    ppermute x36, starting transfers between devices, swap(): lax.ppermute(a, axis, [(i, i ^ mask) for i in range(lax.axis_size(axis))])  36.7 us
    pallas_call x4, Pallas kernels, staged(): pl.pallas_call(kernel, in_specs=[SMEM] * len(scalars) + [HBM] * count, ou...  12.2 us
    dot_general x8, matrix products, partial_gate_up(): jnp.dot(flat, w, preferred_element_type=F32).astype(BF16)  6.82 us
    pallas_call x1, Pallas kernels, attend_next(): pl.pallas_call(functools.partial(attention_body, (first_m, count, rows, 1...  6.61 us
  transfers between devices with their start and end apart: 36, of which 22 were waited for; matrix products, arithmetic and copies ran while one was open for 11% of the time, Pallas kernels for 10%

profile of v4, /device:TPU:0, one launch (start us, length us, event | category | flops | bytes accessed | tf_op | source)
XLA Modules:
  0.0 157.6 jit_solution(1359851922871455364)
XLA Ops:
  2.4 5.7 %attend_first.1 = (bf16[32,128,128]{2,1,0:T(8,128)(2,1)}, bf16[32,128,128]{2,1,0:T(8,128)(2,1)}, bf16[256,512]{1,0:T(8,128)(2,1)}, s32[1,4096]{1,0:T(1,128)}, bf...) custom-call(s32[4]{0:T(128)} %pad_add_fusion.refs_0_.scal, s32[1,64]{1,0:T(1,128)} %refs_1_.1, ...), custom_call_target="tpu_custom_call" | custom-call | tf_op jit(solution)/shard_map/attend_first/pallas_call | solution.py:39
  8.5 2.0 %fusion.46 = (bf16[896,640]{1,0:T(8,128)(2,1)S(1)}, bf16[896,640]{1,0:T(8,128)(2,1)S(1)}) fusion(bf16[896,1280]{1,0:T(8,128)(2,1)} %param.26), kind=kLoop, calls=%fused_computation.98 | loop fusion | bytes 4587520 | tf_op jit(solution)/shard_map/slice | solution.py:415
  10.6 2.3 %project.2 = bf16[32,5120]{1,0:T(8,128)(2,1)S(1)} custom-call(s32[4]{0:T(128)S(1)} %copy-done.3, bf16[32,640]{1,0:T(8,128)(2,1)S(1)} %copy-done.2, bf16[32,640]{1,0:T(8,128)(2,1)S(1)} %collective-permute-done.refs_2_, bf16[256,5120]{1,0:T(8,128)(2,1)S(1)} %copy-done, bf16[256,5120]{1,0:T(8,128)(2,1)S(1)} %collective-permute-done.1.refs_4_), custom_call_target="tpu_custom_call" | custom-call | tf_op jit(solution)/shard_map/project/pallas_call | solution.py:39
  12.9 2.9 %collective-permute-start.4 = (bf16[32,5120]{1,0:T(8,128)(2,1)S(1)}, bf16[32,5120]{1,0:T(8,128)(2,1)S(1)}, u32[]{:S(2)}, u32[]{:S(2)}) collective-permute-start(bf16[32,5120]{1,0:T(8,128)(2,1)S(1)} %project.2), channel_id=1, source_target_pairs={{0,2},{2,0},{4,6},{6,4},{1,3},{3,1},{5,7},{7,5},{8,10},{10,8},{12,... | collective-permute-start | bytes 983048 | tf_op jit(solution)/shard_map/ppermute | solution.py:64
  15.8 6.6 %attend_next.1 = (bf16[96,640]{1,0:T(8,128)(2,1)S(1)}, bf16[96,640]{1,0:T(8,128)(2,1)S(1)}) custom-call(s32[4]{0:T(128)S(1)} %copy-done.3, bf16[32,128,128]{2,1,0:T(8,128)(2,1)S(1)} %copy-done.4, bf16[32,128,128]{2,1,0:T(8,128)(2,1)S(1)} %copy-done.5, bf16[256,512]{1,0:T(8,128)(2,1)S(1)} %copy-done.6, s32[1,4096]{1,0:T(1,128)S(1)} %copy-done.7), custom_call_target="tpu_custom_call" | custom-call | flops 8000000000 | bytes 1000000 | tf_op jit(solution)/shard_map/attend_next/pallas_call | solution.py:246
  22.6 1.4 collective-permute-start.7
  24.1 1.5 collective-permute-start.6
  25.6 2.6 %project.3 = (bf16[32,5120]{1,0:T(8,128)(2,1)S(1)}, bf16[32,5120]{1,0:T(8,128)(2,1)S(1)}, bf16[32,5120]{1,0:T(8,128)(2,1)S(1)}) custom-call(s32[4]{0:T(128)S(1)} %copy-done.3, bf16[96,640]{1,0:T(8,128)(2,1)S(1)} %get-tuple-element.46.refs_1_, bf16[96,640]{1,0:T(8,128)(2,1)S(1)} %collective-permute-done.2.refs_2_, bf16[256,5120]{1,0:T(8,128)(2,1)S(1)} %copy-done, ...), custom_call_target="tpu_custom_call" | custom-call | tf_op jit(solution)/shard_map/project/pallas_call | solution.py:39
  28.8 2.6 %collective-permute-start.5 = (bf16[32,5120]{1,0:T(8,128)(2,1)S(1)}, bf16[32,5120]{1,0:T(8,128)(2,1)S(1)}, u32[]{:S(2)}, u32[]{:S(2)}) collective-permute-start(bf16[32,5120]{1,0:T(8,128)(2,1)S(1)} %add_convert_fusion.2), channel_id=1, source_target_pairs={{0,4},{2,6},{4,0},{6,2},{1,5},{3,7},{5,1},{7,3},{8,12},{10,14},{12... | collective-permute-start | bytes 983048 | tf_op jit(solution)/shard_map/ppermute | solution.py:64
  31.4 13.3 %collective-permute-done.3.refs_4_ = bf16[32,5120]{1,0:T(8,128)(2,1)S(1)} collective-permute-done((bf16[32,5120]{1,0:T(8,128)(2,1)S(1)}, bf16[32,5120]{1,0:T(8,128)(2,1)S(1)}, u32[]{:S(2)}, u32[]{:S(2)}) %collective-permute-start.3) | collective-permute-done | bytes 327712 | tf_op jit(solution)/shard_map/ppermute | solution.py:64
  44.8 1.6 %norm_cut.1 = (f32[32,5120]{1,0:T(8,128)S(1)}, bf16[32,1280]{1,0:T(8,128)(2,1)S(1)}, bf16[32,1280]{1,0:T(8,128)(2,1)S(1)}, bf16[32,1280]{1,0:T(8,128)(2,1)S(1)}, bf16[32,1280]{1,0:T(8,128)(2,1)S(1)}) custom-call(s32[4]{0:T(128)S(1)} %copy-done.3, bf16[32,5120]{1,0:T(8,128)(2,1)S(1)} %bitcast.84, bf16[1,5120]{1,0:T(2,128)(2,1)S(1)} %broadcast_in_dim.12.refs_2_, ...), custom_call_target="tpu_custom_call" | custom-call | tf_op jit(solution)/shard_map/norm_cut/pallas_call | solution.py:39
  46.4 3.8 %collective-permute-done.7 = bf16[896,640]{1,0:T(8,128)(2,1)S(1)} collective-permute-done((bf16[896,640]{1,0:T(8,128)(2,1)S(1)}, bf16[896,640]{1,0:T(8,128)(2,1)S(1)}, u32[]{:S(2)}, u32[]{:S(2)}) %collective-permute-start.7) | collective-permute-done | bytes 1146912 | tf_op jit(solution)/shard_map/ppermute | solution.py:64
  51.4 1.5 collective-permute-start.8
  53.4 1.5 collective-permute-start.10
  56.0 1.5 collective-permute-done.9
  58.8 2.6 %collective-permute-start.11 = (bf16[4,32,1280]{2,1,0:T(8,128)(2,1)S(1)}, bf16[4,32,1280]{2,1,0:T(8,128)(2,1)S(1)}, u32[]{:S(2)}, u32[]{:S(2)}) collective-permute-start(bf16[4,32,1280]{2,1,0:T(8,128)(2,1)S(1)} %pad_maximum_fusion.8), channel_id=1, source_target_pairs={{0,4},{2,6},{4,0},{6,2},{1,5},{3,7},{5,1},{7,3},{8,12},{10,14},{12... | collective-permute-start | bytes 983048 | tf_op jit(solution)/shard_map/ppermute | solution.py:64
  61.9 12.2 %collective-permute-done.11 = bf16[4,32,1280]{2,1,0:T(8,128)(2,1)S(1)} collective-permute-done((bf16[4,32,1280]{2,1,0:T(8,128)(2,1)S(1)}, bf16[4,32,1280]{2,1,0:T(8,128)(2,1)S(1)}, u32[]{:S(2)}, u32[]{:S(2)}) %collective-permute-start.11) | collective-permute-done | bytes 327712 | tf_op jit(solution)/shard_map/ppermute | solution.py:64
  81.1 1.4 collective-permute-start.13
  82.6 1.3 collective-permute-start.19
  87.3 1.4 collective-permute-start.18
  88.7 10.5 %collective-permute-done.13 = bf16[2,3,32,1792]{3,2,0,1:T(8,128)(2,1)S(1)} collective-permute-done((bf16[2,3,32,1792]{3,2,0,1:T(8,128)(2,1)S(1)}, bf16[2,3,32,1792]{3,2,0,1:T(8,128)(2,1)S(1)}, u32[]{:S(2)}, u32[]{:S(2)}) %collective-permute-start.13) | collective-permute-done | bytes 688160 | tf_op jit(solution)/shard_map/ppermute | solution.py:64
  106.1 6.5 %collective-permute-done.20 = bf16[4,32,1792]{2,1,0:T(8,128)(2,1)S(1)} collective-permute-done((bf16[4,32,1792]{2,1,0:T(8,128)(2,1)S(1)}, bf16[4,32,1792]{2,1,0:T(8,128)(2,1)S(1)}, u32[]{:S(2)}, u32[]{:S(2)}) %collective-permute-start.20) | collective-permute-done | bytes 458784 | tf_op jit(solution)/shard_map/ppermute | solution.py:64
  118.7 2.0 %collective-permute-start.27 = (bf16[32,2560]{1,0:T(8,128)(2,1)S(1)}, bf16[32,2560]{1,0:T(8,128)(2,1)S(1)}, u32[]{:S(2)}, u32[]{:S(2)}) collective-permute-start(bf16[32,2560]{1,0:T(8,128)(2,1)S(1)} %get-tuple-element.79), channel_id=1, source_target_pairs={{0,2},{2,0},{4,6},{6,4},{1,3},{3,1},{5,7},{7,5},{8,10},{10,8},{12,... | collective-permute-start | bytes 491528 | tf_op jit(solution)/shard_map/ppermute | solution.py:64
  122.3 3.0 %collective-permute-done.27 = bf16[32,2560]{1,0:T(8,128)(2,1)S(1)} collective-permute-done((bf16[32,2560]{1,0:T(8,128)(2,1)S(1)}, bf16[32,2560]{1,0:T(8,128)(2,1)S(1)}, u32[]{:S(2)}, u32[]{:S(2)}) %collective-permute-start.27) | collective-permute-done | bytes 163872 | tf_op jit(solution)/shard_map/ppermute | solution.py:64
  125.4 2.7 %collective-permute-start.28 = (bf16[32,2560]{1,0:T(8,128)(2,1)S(1)}, bf16[32,2560]{1,0:T(8,128)(2,1)S(1)}, u32[]{:S(2)}, u32[]{:S(2)}) collective-permute-start(bf16[32,2560]{1,0:T(8,128)(2,1)S(1)} %add_convert_fusion.6), channel_id=1, source_target_pairs={{0,4},{2,6},{4,0},{6,2},{1,5},{3,7},{5,1},{7,3},{8,12},{10,14},{12... | collective-permute-start | bytes 491528 | tf_op jit(solution)/shard_map/ppermute | solution.py:64
  128.1 4.1 %collective-permute-done.29 = bf16[128,1792]{1,0:T(8,128)(2,1)S(1)} collective-permute-done((bf16[128,1792]{1,0:T(8,128)(2,1)S(1)}, bf16[128,1792]{1,0:T(8,128)(2,1)S(1)}, u32[]{:S(2)}, u32[]{:S(2)}) %collective-permute-start.29) | collective-permute-done | bytes 458784 | tf_op jit(solution)/shard_map/ppermute | solution.py:64
  136.9 1.7 %collective-permute-start.31 = (bf16[32,2560]{1,0:T(8,128)(2,1)S(1)}, bf16[32,2560]{1,0:T(8,128)(2,1)S(1)}, u32[]{:S(2)}, u32[]{:S(2)}) collective-permute-start(bf16[32,2560]{1,0:T(8,128)(2,1)S(1)} %get-tuple-element.77), channel_id=1, source_target_pairs={{0,2},{2,0},{4,6},{6,4},{1,3},{3,1},{5,7},{7,5},{8,10},{10,8},{12,... | collective-permute-start | bytes 491528 | tf_op jit(solution)/shard_map/ppermute | solution.py:64
  138.6 4.4 %collective-permute-done.32 = bf16[32,2560]{1,0:T(8,128)(2,1)S(1)} collective-permute-done((bf16[32,2560]{1,0:T(8,128)(2,1)S(1)}, bf16[32,2560]{1,0:T(8,128)(2,1)S(1)}, u32[]{:S(2)}, u32[]{:S(2)}) %collective-permute-start.32) | collective-permute-done | bytes 163872 | tf_op jit(solution)/shard_map/ppermute | solution.py:64
  144.2 2.2 %collective-permute-done.31 = bf16[32,2560]{1,0:T(8,128)(2,1)S(1)} collective-permute-done((bf16[32,2560]{1,0:T(8,128)(2,1)S(1)}, bf16[32,2560]{1,0:T(8,128)(2,1)S(1)}, u32[]{:S(2)}, u32[]{:S(2)}) %collective-permute-start.31) | collective-permute-done | bytes 163872 | tf_op jit(solution)/shard_map/ppermute | solution.py:64
  146.4 4.6 %collective-permute-done.33 = bf16[32,2560]{1,0:T(8,128)(2,1)S(1)} collective-permute-done((bf16[32,2560]{1,0:T(8,128)(2,1)S(1)}, bf16[32,2560]{1,0:T(8,128)(2,1)S(1)}, u32[]{:S(2)}, u32[]{:S(2)}) %collective-permute-start.33) | collective-permute-done | bytes 163872 | tf_op jit(solution)/shard_map/ppermute | solution.py:64
  153.0 2.6 %collective-permute-done.34.refs_5_ = bf16[32,1280]{1,0:T(8,128)(2,1)S(1)} collective-permute-done((bf16[32,1280]{1,0:T(8,128)(2,1)S(1)}, bf16[32,1280]{1,0:T(8,128)(2,1)S(1)}, u32[]{:S(2)}, u32[]{:S(2)}) %collective-permute-start.34) | collective-permute-done | bytes 81952 | tf_op jit(solution)/shard_map/ppermute | solution.py:64
  156.2 1.4 finish.1
  (131 shorter events, 40.2 us)
Async XLA Ops:
  0.6 9.8 %collective-permute-start.1 = (bf16[256,5120]{1,0:T(8,128)(2,1)}, bf16[256,5120]{1,0:T(8,128)(2,1)S(1)}, u32[]{:S(2)}, u32[]{:S(2)}) collective-permute-start(bf16[256,5120]{1,0:T(8,128)(2,1)} %refs_3_.3), channel_id=1, source_target_pairs={{0,1},{1,0},{2,3},{3,2},{4,5},{5,4},{6,7},{7,6},{8,9},{9,8},{10,11... | collective-permute-start | bytes 7864328 | tf_op jit(solution)/shard_map/ppermute | solution.py:64
  12.9 15.8 %collective-permute-start.4 = (bf16[32,5120]{1,0:T(8,128)(2,1)S(1)}, bf16[32,5120]{1,0:T(8,128)(2,1)S(1)}, u32[]{:S(2)}, u32[]{:S(2)}) collective-permute-start(bf16[32,5120]{1,0:T(8,128)(2,1)S(1)} %project.2), channel_id=1, source_target_pairs={{0,2},{2,0},{4,6},{6,4},{1,3},{3,1},{5,7},{7,5},{8,10},{10,8},{12,... | collective-permute-start | bytes 983048 | tf_op jit(solution)/shard_map/ppermute | solution.py:64
  22.6 27.5 %collective-permute-start.7 = (bf16[896,640]{1,0:T(8,128)(2,1)S(1)}, bf16[896,640]{1,0:T(8,128)(2,1)S(1)}, u32[]{:S(2)}, u32[]{:S(2)}) collective-permute-start(bf16[896,640]{1,0:T(8,128)(2,1)S(1)} %get-tuple-element.75), channel_id=1, source_target_pairs={{0,16},{8,24},{16,0},{24,8},{1,17},{9,25},{17,1},{25,9},{2,18},{10... | collective-permute-start | bytes 3440648 | tf_op jit(solution)/shard_map/ppermute | solution.py:64
  24.1 27.3 %collective-permute-start.6 = (bf16[896,640]{1,0:T(8,128)(2,1)S(1)}, bf16[896,640]{1,0:T(8,128)(2,1)S(1)}, u32[]{:S(2)}, u32[]{:S(2)}) collective-permute-start(bf16[896,640]{1,0:T(8,128)(2,1)S(1)} %get-tuple-element.76), channel_id=1, source_target_pairs={{0,8},{8,0},{16,24},{24,16},{1,9},{9,1},{17,25},{25,17},{2,10},{10... | collective-permute-start | bytes 3440648 | tf_op jit(solution)/shard_map/ppermute | solution.py:64
  28.2 16.6 %collective-permute-start.3 = (bf16[32,5120]{1,0:T(8,128)(2,1)S(1)}, bf16[32,5120]{1,0:T(8,128)(2,1)S(1)}, u32[]{:S(2)}, u32[]{:S(2)}) collective-permute-start(bf16[32,5120]{1,0:T(8,128)(2,1)S(1)} %get-tuple-element.49), channel_id=1, source_target_pairs={{0,2},{2,0},{4,6},{6,4},{1,3},{3,1},{5,7},{7,5},{8,10},{10,8},{12,... | collective-permute-start | bytes 983048 | tf_op jit(solution)/shard_map/ppermute | solution.py:64
  28.8 16.0 %collective-permute-start.5 = (bf16[32,5120]{1,0:T(8,128)(2,1)S(1)}, bf16[32,5120]{1,0:T(8,128)(2,1)S(1)}, u32[]{:S(2)}, u32[]{:S(2)}) collective-permute-start(bf16[32,5120]{1,0:T(8,128)(2,1)S(1)} %add_convert_fusion.2), channel_id=1, source_target_pairs={{0,4},{2,6},{4,0},{6,2},{1,5},{3,7},{5,1},{7,3},{8,12},{10,14},{12... | collective-permute-start | bytes 983048 | tf_op jit(solution)/shard_map/ppermute | solution.py:64
  31.4 46.9 %collective-permute-start.16 = (bf16[1280,896]{1,0:T(8,128)(2,1)S(1)}, bf16[1280,896]{1,0:T(8,128)(2,1)S(1)}, u32[]{:S(2)}, u32[]{:S(2)}) collective-permute-start(bf16[1280,896]{1,0:T(8,128)(2,1)S(1)} %copy-done.8), channel_id=1, source_target_pairs={{0,1},{1,0},{2,3},{3,2},{4,5},{5,4},{6,7},{7,6},{8,9},{9,8},{10,11... | collective-permute-start | bytes 6881288 | tf_op jit(solution)/shard_map/ppermute | solution.py:64
  44.7 34.8 %collective-permute-start.15 = (bf16[1280,896]{1,0:T(8,128)(2,1)S(1)}, bf16[1280,896]{1,0:T(8,128)(2,1)S(1)}, u32[]{:S(2)}, u32[]{:S(2)}) collective-permute-start(bf16[1280,896]{1,0:T(8,128)(2,1)S(1)} %copy-done.9), channel_id=1, source_target_pairs={{0,1},{1,0},{2,3},{3,2},{4,5},{5,4},{6,7},{7,6},{8,9},{9,8},{10,11... | collective-permute-start | bytes 6881288 | tf_op jit(solution)/shard_map/ppermute | solution.py:64
  51.4 4.6 %collective-permute-start.8 = (bf16[32,1280]{1,0:T(8,128)(2,1)S(1)}, bf16[32,1280]{1,0:T(8,128)(2,1)S(1)}, u32[]{:S(2)}, u32[]{:S(2)}) collective-permute-start(bf16[32,1280]{1,0:T(8,128)(2,1)S(1)} %get-tuple-element.54), channel_id=1, source_target_pairs={{0,8},{8,0},{16,24},{24,16},{1,9},{9,1},{17,25},{25,17},{2,10},{10... | collective-permute-start | bytes 245768 | tf_op jit(solution)/shard_map/ppermute | solution.py:64
  52.9 4.6 %collective-permute-start.9 = (bf16[32,1280]{1,0:T(8,128)(2,1)S(1)}, bf16[32,1280]{1,0:T(8,128)(2,1)S(1)}, u32[]{:S(2)}, u32[]{:S(2)}) collective-permute-start(bf16[32,1280]{1,0:T(8,128)(2,1)S(1)} %get-tuple-element.56), channel_id=1, source_target_pairs={{0,16},{8,24},{16,0},{24,8},{1,17},{9,25},{17,1},{25,9},{2,18},{10... | collective-permute-start | bytes 245768 | tf_op jit(solution)/shard_map/ppermute | solution.py:64
  53.4 5.3 %collective-permute-start.10 = (bf16[32,1280]{1,0:T(8,128)(2,1)S(1)}, bf16[32,1280]{1,0:T(8,128)(2,1)S(1)}, u32[]{:S(2)}, u32[]{:S(2)}) collective-permute-start(bf16[32,1280]{1,0:T(8,128)(2,1)S(1)} %get-tuple-element.58), channel_id=1, source_target_pairs={{0,24},{8,16},{16,8},{24,0},{1,25},{9,17},{17,9},{25,1},{2,26},{10... | collective-permute-start | bytes 245768 | tf_op jit(solution)/shard_map/ppermute | solution.py:64
  58.8 15.4 %collective-permute-start.11 = (bf16[4,32,1280]{2,1,0:T(8,128)(2,1)S(1)}, bf16[4,32,1280]{2,1,0:T(8,128)(2,1)S(1)}, u32[]{:S(2)}, u32[]{:S(2)}) collective-permute-start(bf16[4,32,1280]{2,1,0:T(8,128)(2,1)S(1)} %pad_maximum_fusion.8), channel_id=1, source_target_pairs={{0,4},{2,6},{4,0},{6,2},{1,5},{3,7},{5,1},{7,3},{8,12},{10,14},{12... | collective-permute-start | bytes 983048 | tf_op jit(solution)/shard_map/ppermute | solution.py:64
  61.4 14.0 %collective-permute-start.12 = (bf16[4,32,1280]{2,1,0:T(8,128)(2,1)S(1)}, bf16[4,32,1280]{2,1,0:T(8,128)(2,1)S(1)}, u32[]{:S(2)}, u32[]{:S(2)}) collective-permute-start(bf16[4,32,1280]{2,1,0:T(8,128)(2,1)S(1)} %pad_maximum_fusion.8), channel_id=1, source_target_pairs={{0,2},{2,0},{4,6},{6,4},{1,3},{3,1},{5,7},{7,5},{8,10},{10,8},{12,... | collective-permute-start | bytes 983048 | tf_op jit(solution)/shard_map/ppermute | solution.py:64
  75.5 8.5 %collective-permute-start.14 = (bf16[4,32,1280]{2,1,0:T(8,128)(2,1)S(1)}, bf16[4,32,1280]{2,1,0:T(8,128)(2,1)S(1)}, u32[]{:S(2)}, u32[]{:S(2)}) collective-permute-start(bf16[4,32,1280]{2,1,0:T(8,128)(2,1)S(1)} %collective-permute-done.11), channel_id=1, source_target_pairs={{0,2},{2,0},{4,6},{6,4},{1,3},{3,1},{5,7},{7,5},{8,10},{10,8},{12,... | collective-permute-start | bytes 983048 | tf_op jit(solution)/shard_map/ppermute | solution.py:64
  81.1 18.1 %collective-permute-start.13 = (bf16[2,3,32,1792]{3,2,0,1:T(8,128)(2,1)S(1)}, bf16[2,3,32,1792]{3,2,0,1:T(8,128)(2,1)S(1)}, u32[]{:S(2)}, u32[]{:S(2)}) collective-permute-start(bf16[2,3,32,1792]{3,2,0,1:T(8,128)(2,1)S(1)} %slice.93), channel_id=1, source_target_pairs={{0,8},{8,0},{16,24},{24,16},{1,9},{9,1},{17,25},{25,17},{2,10},{10... | collective-permute-start | bytes 2064392 | tf_op jit(solution)/shard_map/ppermute | solution.py:64
  82.6 17.8 %collective-permute-start.19 = (bf16[2,3,32,1792]{3,2,1,0:T(8,128)(2,1)S(1)}, bf16[2,3,32,1792]{3,2,1,0:T(8,128)(2,1)S(1)}, u32[]{:S(2)}, u32[]{:S(2)}) collective-permute-start(bf16[2,3,32,1792]{3,2,1,0:T(8,128)(2,1)S(1)} %slice.120), channel_id=1, source_target_pairs={{0,16},{8,24},{16,0},{24,8},{1,17},{9,25},{17,1},{25,9},{2,18},{10... | collective-permute-start | bytes 2064392 | tf_op jit(solution)/shard_map/ppermute | solution.py:64
  85.0 16.6 %collective-permute-start.17 = (bf16[2,1,32,1792]{3,2,0,1:T(8,128)(2,1)S(1)}, bf16[2,1,32,1792]{3,2,0,1:T(8,128)(2,1)S(1)}, u32[]{:S(2)}, u32[]{:S(2)}) collective-permute-start(bf16[2,1,32,1792]{3,2,0,1:T(8,128)(2,1)S(1)} %slice.95), channel_id=1, source_target_pairs={{0,8},{8,0},{16,24},{24,16},{1,9},{9,1},{17,25},{25,17},{2,10},{10... | collective-permute-start | bytes 688136 | tf_op jit(solution)/shard_map/ppermute | solution.py:64
  87.3 15.7 %collective-permute-start.18 = (bf16[2,1,32,1792]{3,2,1,0:T(8,128)(2,1)S(1)}, bf16[2,1,32,1792]{3,2,1,0:T(8,128)(2,1)S(1)}, u32[]{:S(2)}, u32[]{:S(2)}) collective-permute-start(bf16[2,1,32,1792]{3,2,1,0:T(8,128)(2,1)S(1)} %bitcast.116), channel_id=1, source_target_pairs={{0,16},{8,24},{16,0},{24,8},{1,17},{9,25},{17,1},{25,9},{2,18},{10... | collective-permute-start | bytes 688136 | tf_op jit(solution)/shard_map/ppermute | solution.py:64
  103.1 9.5 %collective-permute-start.20 = (bf16[4,32,1792]{2,1,0:T(8,128)(2,1)S(1)}, bf16[4,32,1792]{2,1,0:T(8,128)(2,1)S(1)}, u32[]{:S(2)}, u32[]{:S(2)}) collective-permute-start(bf16[4,32,1792]{2,1,0:T(8,128)(2,1)S(1)} %fusion.15), channel_id=1, source_target_pairs={{0,16},{8,24},{16,0},{24,8},{1,17},{9,25},{17,1},{25,9},{2,18},{10... | collective-permute-start | bytes 1376264 | tf_op jit(solution)/shard_map/ppermute | solution.py:64
  104.5 9.1 %collective-permute-start.21 = (bf16[4,32,1792]{2,1,0:T(8,128)(2,1)S(1)}, bf16[4,32,1792]{2,1,0:T(8,128)(2,1)S(1)}, u32[]{:S(2)}, u32[]{:S(2)}) collective-permute-start(bf16[4,32,1792]{2,1,0:T(8,128)(2,1)S(1)} %fusion.9), channel_id=1, source_target_pairs={{0,8},{8,0},{16,24},{24,16},{1,9},{9,1},{17,25},{25,17},{2,10},{10... | collective-permute-start | bytes 1376264 | tf_op jit(solution)/shard_map/ppermute | solution.py:64
  105.6 12.2 %collective-permute-start.23 = (bf16[896,640]{1,0:T(8,128)(2,1)S(1)}, bf16[896,640]{1,0:T(8,128)(2,1)S(1)}, u32[]{:S(2)}, u32[]{:S(2)}) collective-permute-start(bf16[896,640]{1,0:T(8,128)(2,1)S(1)} %get-tuple-element.75), channel_id=1, source_target_pairs={{0,1},{1,0},{2,3},{3,2},{4,5},{5,4},{6,7},{7,6},{8,9},{9,8},{10,11... | collective-permute-start | bytes 3440648 | tf_op jit(solution)/shard_map/ppermute | solution.py:64
  105.6 12.6 %collective-permute-start.22 = (bf16[896,640]{1,0:T(8,128)(2,1)S(1)}, bf16[896,640]{1,0:T(8,128)(2,1)S(1)}, u32[]{:S(2)}, u32[]{:S(2)}) collective-permute-start(bf16[896,640]{1,0:T(8,128)(2,1)S(1)} %get-tuple-element.76), channel_id=1, source_target_pairs={{0,1},{1,0},{2,3},{3,2},{4,5},{5,4},{6,7},{7,6},{8,9},{9,8},{10,11... | collective-permute-start | bytes 3440648 | tf_op jit(solution)/shard_map/ppermute | solution.py:64
  106.1 10.9 %collective-permute-start.25 = (bf16[896,640]{1,0:T(8,128)(2,1)S(1)}, bf16[896,640]{1,0:T(8,128)(2,1)S(1)}, u32[]{:S(2)}, u32[]{:S(2)}) collective-permute-start(bf16[896,640]{1,0:T(8,128)(2,1)S(1)} %collective-permute-done.7), channel_id=1, source_target_pairs={{0,1},{1,0},{2,3},{3,2},{4,5},{5,4},{6,7},{7,6},{8,9},{9,8},{10,11... | collective-permute-start | bytes 3440648 | tf_op jit(solution)/shard_map/ppermute | solution.py:64
  112.6 4.8 %collective-permute-start.24 = (bf16[896,640]{1,0:T(8,128)(2,1)S(1)}, bf16[896,640]{1,0:T(8,128)(2,1)S(1)}, u32[]{:S(2)}, u32[]{:S(2)}) collective-permute-start(bf16[896,640]{1,0:T(8,128)(2,1)S(1)} %collective-permute-done.6), channel_id=1, source_target_pairs={{0,1},{1,0},{2,3},{3,2},{4,5},{5,4},{6,7},{7,6},{8,9},{9,8},{10,11... | collective-permute-start | bytes 3440648 | tf_op jit(solution)/shard_map/ppermute | solution.py:64
  118.7 6.6 %collective-permute-start.27 = (bf16[32,2560]{1,0:T(8,128)(2,1)S(1)}, bf16[32,2560]{1,0:T(8,128)(2,1)S(1)}, u32[]{:S(2)}, u32[]{:S(2)}) collective-permute-start(bf16[32,2560]{1,0:T(8,128)(2,1)S(1)} %get-tuple-element.79), channel_id=1, source_target_pairs={{0,2},{2,0},{4,6},{6,4},{1,3},{3,1},{5,7},{7,5},{8,10},{10,8},{12,... | collective-permute-start | bytes 491528 | tf_op jit(solution)/shard_map/ppermute | solution.py:64
  120.7 11.6 %collective-permute-start.29 = (bf16[128,1792]{1,0:T(8,128)(2,1)S(1)}, bf16[128,1792]{1,0:T(8,128)(2,1)S(1)}, u32[]{:S(2)}, u32[]{:S(2)}) collective-permute-start(bf16[128,1792]{1,0:T(8,128)(2,1)S(1)} %bitcast.95), channel_id=1, source_target_pairs={{0,16},{8,24},{16,0},{24,8},{1,17},{9,25},{17,1},{25,9},{2,18},{10... | collective-permute-start | bytes 1376264 | tf_op jit(solution)/shard_map/ppermute | solution.py:64
  121.4 11.9 %collective-permute-start.30 = (bf16[128,1792]{1,0:T(8,128)(2,1)S(1)}, bf16[128,1792]{1,0:T(8,128)(2,1)S(1)}, u32[]{:S(2)}, u32[]{:S(2)}) collective-permute-start(bf16[128,1792]{1,0:T(8,128)(2,1)S(1)} %bitcast.96), channel_id=1, source_target_pairs={{0,8},{8,0},{16,24},{24,16},{1,9},{9,1},{17,25},{25,17},{2,10},{10... | collective-permute-start | bytes 1376264 | tf_op jit(solution)/shard_map/ppermute | solution.py:64
  122.1 14.3 %collective-permute-start.26 = (bf16[32,2560]{1,0:T(8,128)(2,1)S(1)}, bf16[32,2560]{1,0:T(8,128)(2,1)S(1)}, u32[]{:S(2)}, u32[]{:S(2)}) collective-permute-start(bf16[32,2560]{1,0:T(8,128)(2,1)S(1)} %get-tuple-element.80), channel_id=1, source_target_pairs={{0,2},{2,0},{4,6},{6,4},{1,3},{3,1},{5,7},{7,5},{8,10},{10,8},{12,... | collective-permute-start | bytes 491528 | tf_op jit(solution)/shard_map/ppermute | solution.py:64
  125.4 11.1 %collective-permute-start.28 = (bf16[32,2560]{1,0:T(8,128)(2,1)S(1)}, bf16[32,2560]{1,0:T(8,128)(2,1)S(1)}, u32[]{:S(2)}, u32[]{:S(2)}) collective-permute-start(bf16[32,2560]{1,0:T(8,128)(2,1)S(1)} %add_convert_fusion.6), channel_id=1, source_target_pairs={{0,4},{2,6},{4,0},{6,2},{1,5},{3,7},{5,1},{7,3},{8,12},{10,14},{12... | collective-permute-start | bytes 491528 | tf_op jit(solution)/shard_map/ppermute | solution.py:64
  136.5 6.5 %collective-permute-start.32 = (bf16[32,2560]{1,0:T(8,128)(2,1)S(1)}, bf16[32,2560]{1,0:T(8,128)(2,1)S(1)}, u32[]{:S(2)}, u32[]{:S(2)}) collective-permute-start(bf16[32,2560]{1,0:T(8,128)(2,1)S(1)} %get-tuple-element.72), channel_id=1, source_target_pairs={{0,2},{2,0},{4,6},{6,4},{1,3},{3,1},{5,7},{7,5},{8,10},{10,8},{12,... | collective-permute-start | bytes 491528 | tf_op jit(solution)/shard_map/ppermute | solution.py:64
  136.9 9.6 %collective-permute-start.31 = (bf16[32,2560]{1,0:T(8,128)(2,1)S(1)}, bf16[32,2560]{1,0:T(8,128)(2,1)S(1)}, u32[]{:S(2)}, u32[]{:S(2)}) collective-permute-start(bf16[32,2560]{1,0:T(8,128)(2,1)S(1)} %get-tuple-element.77), channel_id=1, source_target_pairs={{0,2},{2,0},{4,6},{6,4},{1,3},{3,1},{5,7},{7,5},{8,10},{10,8},{12,... | collective-permute-start | bytes 491528 | tf_op jit(solution)/shard_map/ppermute | solution.py:64
  143.0 8.0 %collective-permute-start.33 = (bf16[32,2560]{1,0:T(8,128)(2,1)S(1)}, bf16[32,2560]{1,0:T(8,128)(2,1)S(1)}, u32[]{:S(2)}, u32[]{:S(2)}) collective-permute-start(bf16[32,2560]{1,0:T(8,128)(2,1)S(1)} %add_convert_fusion.5), channel_id=1, source_target_pairs={{0,4},{2,6},{4,0},{6,2},{1,5},{3,7},{5,1},{7,3},{8,12},{10,14},{12... | collective-permute-start | bytes 491528 | tf_op jit(solution)/shard_map/ppermute | solution.py:64
  (16 other events, 94.2 us)

commit v5 on v4

--- a/solution.py
+++ b/solution.py
@@ -237,7 +237,7 @@
             jax.ShapeDtypeStruct((side, width + head_dim), BF16),
         ],
         [pltpu.SMEM((table.shape[1],), jnp.int32), pltpu.SemaphoreType.DMA((2,))],
-        60, "attend_first", [HBM, HBM] + [VMEM] * 4)
+        56, "attend_first", [HBM, HBM] + [VMEM] * 4)
 
 
 def attend_next(scal, keys, values, q_rot, key_pos, rows, first_m, count):
@@ -254,7 +254,7 @@
     )(scal, keys, values, q_rot, key_pos)
 
 
-def project_body(head_dim, scal, o1, o2, wa, wb, wait_a, wait_b, *rest):
+def project_body(head_dim, scal, o1, o2, wa, wb, *rest):
     outs, attn = rest[:-1], rest[-1]
     width = attn.shape[1]
     heads = width // head_dim
@@ -274,8 +274,6 @@
         attn[:, cols] = (mixed / (f1 + f2)).astype(BF16)
     mine = attn[:, pl.ds(pl.multiple_of(blk_id * depth, depth), depth)]
     other = attn[:, pl.ds(pl.multiple_of((1 - blk_id) * depth, depth), depth)]
-    wait_a()
-    wait_b()
     step = model // 4
     for n in range(0, model, step):
         out = (
@@ -289,8 +287,8 @@
 def project(scal, o1, o2, wa, wb, head_dim, count):
     rows = o1.shape[0]
     width = o1.shape[1] - head_dim
-    return staged(
-        functools.partial(project_body, head_dim), [scal], [o1, o2, wa, wb], 2,
+    return direct(
+        functools.partial(project_body, head_dim), [scal], [o1, o2, wa, wb],
         [jax.ShapeDtypeStruct((rows // count, wa.shape[1]), BF16)] * count,
         [pltpu.VMEM((rows, width), BF16)], 32, "project")
 
@@ -312,8 +310,8 @@
 def norm_cut(scal, x, terms, gain, reqs):
     rows, model = terms[0].shape
     part = model // reqs
-    return staged(
-        norm_body, [scal], [x, gain, *terms], 0,
+    return direct(
+        norm_body, [scal], [x, gain, *terms],
         [jax.ShapeDtypeStruct((rows, model), F32)]
         + [jax.ShapeDtypeStruct((rows, part), BF16)] * reqs,
         [pltpu.VMEM((rows, model), BF16)], 8, "norm_cut")

time: 158 us -> 155 us (0.981)
  local copies, waits for them, and re-layouts: 3.79 us -> 0.82 us
  Pallas kernels: 20.2 us -> 18.4 us
    pallas_call x4 -> x1, Pallas kernels: 12.2 us -> 5.9 us  [staged(): pl.pallas_call(kernel, in_specs=[SMEM] * len(scalars) + [HBM] * count, ou...]
    pallas_call x1 -> x4, Pallas kernels: 1.37 us -> 5.92 us  [direct(): pl.pallas_call(body, in_specs=[SMEM] * len(scalars) + [VMEM] * len(arrays...]
    slice x1, local copies, waits for them, and re-layouts: 1.96 us -> 0.2 us  [on_device(): cuts = [w_down[:, :half], w_down[:, half:]]]
  transfers between devices with their start and end apart: 36 -> 36, of which waited for: 22 -> 24; matrix products, arithmetic and copies ran while one was open for 11% -> 10% of each run, Pallas kernels for 10% -> 10%
where the time goes in v5:
time: 155 us
  waiting for transfers between devices  81.1 us (52%)
  starting transfers between devices  37 us (24%)
  Pallas kernels  18.4 us (12%)
  matrix products  12.9 us (8%)
  other arithmetic  2.3 us (1%)
  between operations  1.99 us (1%)
    ppermute x36, waiting for transfers between devices, swap(): lax.ppermute(a, axis, [(i, i ^ mask) for i in range(lax.axis_size(axis))])  81.1 us
    ppermute x36, starting transfers between devices, swap(): lax.ppermute(a, axis, [(i, i ^ mask) for i in range(lax.axis_size(axis))])  37 us
    dot_general x8, matrix products, partial_gate_up(): jnp.dot(flat, w, preferred_element_type=F32).astype(BF16)  6.81 us
    pallas_call x1, Pallas kernels, attend_next(): pl.pallas_call(functools.partial(attention_body, (first_m, count, rows, 1...  6.62 us
    pallas_call x4, Pallas kernels, direct(): pl.pallas_call(body, in_specs=[SMEM] * len(scalars) + [VMEM] * len(arrays...  5.92 us
    pallas_call x1, Pallas kernels, staged(): pl.pallas_call(kernel, in_specs=[SMEM] * len(scalars) + [HBM] * count, ou...  5.9 us
  transfers between devices with their start and end apart: 36, of which 24 were waited for; matrix products, arithmetic and copies ran while one was open for 10% of the time, Pallas kernels for 10%

profile of v5, /device:TPU:0, one launch (start us, length us, event | category | flops | bytes accessed | tf_op | source)
XLA Modules:
  0.0 154.7 jit_solution(10515629670559236911)
XLA Ops:
  2.5 5.9 %attend_first.1 = (bf16[32,128,128]{2,1,0:T(8,128)(2,1)}, bf16[32,128,128]{2,1,0:T(8,128)(2,1)}, bf16[256,512]{1,0:T(8,128)(2,1)}, s32[1,4096]{1,0:T(1,128)}, bf...) custom-call(s32[4]{0:T(128)} %pad_add_fusion.refs_0_.scal, s32[1,64]{1,0:T(1,128)} %refs_1_.1, ...), custom_call_target="tpu_custom_call" | custom-call | tf_op jit(solution)/shard_map/attend_first/pallas_call | solution.py:39
  10.2 1.8 %project.2 = bf16[32,5120]{1,0:T(8,128)(2,1)S(1)} custom-call(s32[4]{0:T(128)S(1)} %copy-done.3, bf16[32,640]{1,0:T(8,128)(2,1)S(1)} %copy-done.2, bf16[32,640]{1,0:T(8,128)(2,1)S(1)} %collective-permute-done.o2, bf16[256,5120]{1,0:T(8,128)(2,1)S(1)} %copy-done, bf16[256,5120]{1,0:T(8,128)(2,1)S(1)} %collective-permute-done.1.wb), custom_call_target="tpu_custom_call" | custom-call | tf_op jit(solution)/shard_map/project/pallas_call | solution.py:52
  12.0 2.7 %collective-permute-start.4 = (bf16[32,5120]{1,0:T(8,128)(2,1)S(1)}, bf16[32,5120]{1,0:T(8,128)(2,1)S(1)}, u32[]{:S(2)}, u32[]{:S(2)}) collective-permute-start(bf16[32,5120]{1,0:T(8,128)(2,1)S(1)} %project.2), channel_id=1, source_target_pairs={{0,2},{2,0},{4,6},{6,4},{1,3},{3,1},{5,7},{7,5},{8,10},{10,8},{12,... | collective-permute-start | bytes 983048 | tf_op jit(solution)/shard_map/ppermute | solution.py:64
  14.7 6.6 %attend_next.1 = (bf16[96,640]{1,0:T(8,128)(2,1)S(1)}, bf16[96,640]{1,0:T(8,128)(2,1)S(1)}) custom-call(s32[4]{0:T(128)S(1)} %copy-done.3, bf16[32,128,128]{2,1,0:T(8,128)(2,1)S(1)} %copy-done.4, bf16[32,128,128]{2,1,0:T(8,128)(2,1)S(1)} %copy-done.5, bf16[256,512]{1,0:T(8,128)(2,1)S(1)} %copy-done.6, s32[1,4096]{1,0:T(1,128)S(1)} %copy-done.7), custom_call_target="tpu_custom_call" | custom-call | flops 8000000000 | bytes 1000000 | tf_op jit(solution)/shard_map/attend_next/pallas_call | solution.py:246
  21.4 1.7 %collective-permute-start.7 = (bf16[896,640]{1,0:T(8,128)(2,1)S(1)}, bf16[896,640]{1,0:T(8,128)(2,1)S(1)}, u32[]{:S(2)}, u32[]{:S(2)}) collective-permute-start(bf16[896,640]{1,0:T(8,128)(2,1)S(1)} %get-tuple-element.75), channel_id=1, source_target_pairs={{0,16},{8,24},{16,0},{24,8},{1,17},{9,25},{17,1},{25,9},{2,18},{10... | collective-permute-start | bytes 3440648 | tf_op jit(solution)/shard_map/ppermute | solution.py:64
  23.1 1.5 collective-permute-start.6
  24.6 1.8 %project.3 = (bf16[32,5120]{1,0:T(8,128)(2,1)S(1)}, bf16[32,5120]{1,0:T(8,128)(2,1)S(1)}, bf16[32,5120]{1,0:T(8,128)(2,1)S(1)}) custom-call(s32[4]{0:T(128)S(1)} %copy-done.3, bf16[96,640]{1,0:T(8,128)(2,1)S(1)} %get-tuple-element.46.o1, bf16[96,640]{1,0:T(8,128)(2,1)S(1)} %collective-permute-done.2.o2, bf16[256,5120]{1,0:T(8,128)(2,1)S(1)} %copy-done, ...), custom_call_target="tpu_custom_call" | custom-call | tf_op jit(solution)/shard_map/project/pallas_call | solution.py:52
  27.1 2.7 %collective-permute-start.5 = (bf16[32,5120]{1,0:T(8,128)(2,1)S(1)}, bf16[32,5120]{1,0:T(8,128)(2,1)S(1)}, u32[]{:S(2)}, u32[]{:S(2)}) collective-permute-start(bf16[32,5120]{1,0:T(8,128)(2,1)S(1)} %add_convert_fusion.2), channel_id=1, source_target_pairs={{0,4},{2,6},{4,0},{6,2},{1,5},{3,7},{5,1},{7,3},{8,12},{10,14},{12... | collective-permute-start | bytes 983048 | tf_op jit(solution)/shard_map/ppermute | solution.py:64
  29.8 13.3 %collective-permute-done.3.rest_1_ = bf16[32,5120]{1,0:T(8,128)(2,1)S(1)} collective-permute-done((bf16[32,5120]{1,0:T(8,128)(2,1)S(1)}, bf16[32,5120]{1,0:T(8,128)(2,1)S(1)}, u32[]{:S(2)}, u32[]{:S(2)}) %collective-permute-start.3) | collective-permute-done | bytes 327712 | tf_op jit(solution)/shard_map/ppermute | solution.py:64
  44.1 5.0 %collective-permute-done.7 = bf16[896,640]{1,0:T(8,128)(2,1)S(1)} collective-permute-done((bf16[896,640]{1,0:T(8,128)(2,1)S(1)}, bf16[896,640]{1,0:T(8,128)(2,1)S(1)}, u32[]{:S(2)}, u32[]{:S(2)}) %collective-permute-start.7) | collective-permute-done | bytes 1146912 | tf_op jit(solution)/shard_map/ppermute | solution.py:64
  50.2 1.7 %collective-permute-start.8 = (bf16[32,1280]{1,0:T(8,128)(2,1)S(1)}, bf16[32,1280]{1,0:T(8,128)(2,1)S(1)}, u32[]{:S(2)}, u32[]{:S(2)}) collective-permute-start(bf16[32,1280]{1,0:T(8,128)(2,1)S(1)} %get-tuple-element.54), channel_id=1, source_target_pairs={{0,8},{8,0},{16,24},{24,16},{1,9},{9,1},{17,25},{25,17},{2,10},{10... | collective-permute-start | bytes 245768 | tf_op jit(solution)/shard_map/ppermute | solution.py:64
  52.2 1.5 collective-permute-start.10
  54.7 1.9 %collective-permute-done.9 = bf16[32,1280]{1,0:T(8,128)(2,1)S(1)} collective-permute-done((bf16[32,1280]{1,0:T(8,128)(2,1)S(1)}, bf16[32,1280]{1,0:T(8,128)(2,1)S(1)}, u32[]{:S(2)}, u32[]{:S(2)}) %collective-permute-start.9) | collective-permute-done | bytes 81952 | tf_op jit(solution)/shard_map/ppermute | solution.py:64
  57.6 2.7 %collective-permute-start.11 = (bf16[4,32,1280]{2,1,0:T(8,128)(2,1)S(1)}, bf16[4,32,1280]{2,1,0:T(8,128)(2,1)S(1)}, u32[]{:S(2)}, u32[]{:S(2)}) collective-permute-start(bf16[4,32,1280]{2,1,0:T(8,128)(2,1)S(1)} %pad_maximum_fusion.8), channel_id=1, source_target_pairs={{0,4},{2,6},{4,0},{6,2},{1,5},{3,7},{5,1},{7,3},{8,12},{10,14},{12... | collective-permute-start | bytes 983048 | tf_op jit(solution)/shard_map/ppermute | solution.py:64
  60.8 12.4 %collective-permute-done.11 = bf16[4,32,1280]{2,1,0:T(8,128)(2,1)S(1)} collective-permute-done((bf16[4,32,1280]{2,1,0:T(8,128)(2,1)S(1)}, bf16[4,32,1280]{2,1,0:T(8,128)(2,1)S(1)}, u32[]{:S(2)}, u32[]{:S(2)}) %collective-permute-start.11) | collective-permute-done | bytes 327712 | tf_op jit(solution)/shard_map/ppermute | solution.py:64
  73.2 1.3 collective-permute-done.12
  81.3 1.2 collective-permute-start.19
  87.3 10.9 %collective-permute-done.13 = bf16[2,3,32,1792]{3,2,0,1:T(8,128)(2,1)S(1)} collective-permute-done((bf16[2,3,32,1792]{3,2,0,1:T(8,128)(2,1)S(1)}, bf16[2,3,32,1792]{3,2,0,1:T(8,128)(2,1)S(1)}, u32[]{:S(2)}, u32[]{:S(2)}) %collective-permute-start.13) | collective-permute-done | bytes 688160 | tf_op jit(solution)/shard_map/ppermute | solution.py:64
  99.3 1.4 collective-permute-done.17
  103.2 1.4 collective-permute-start.21
  105.1 6.3 %collective-permute-done.20 = bf16[4,32,1792]{2,1,0:T(8,128)(2,1)S(1)} collective-permute-done((bf16[4,32,1792]{2,1,0:T(8,128)(2,1)S(1)}, bf16[4,32,1792]{2,1,0:T(8,128)(2,1)S(1)}, u32[]{:S(2)}, u32[]{:S(2)}) %collective-permute-start.20) | collective-permute-done | bytes 458784 | tf_op jit(solution)/shard_map/ppermute | solution.py:64
  116.0 2.0 %collective-permute-start.27 = (bf16[32,2560]{1,0:T(8,128)(2,1)S(1)}, bf16[32,2560]{1,0:T(8,128)(2,1)S(1)}, u32[]{:S(2)}, u32[]{:S(2)}) collective-permute-start(bf16[32,2560]{1,0:T(8,128)(2,1)S(1)} %get-tuple-element.79), channel_id=1, source_target_pairs={{0,2},{2,0},{4,6},{6,4},{1,3},{3,1},{5,7},{7,5},{8,10},{10,8},{12,... | collective-permute-start | bytes 491528 | tf_op jit(solution)/shard_map/ppermute | solution.py:64
  120.1 2.5 %collective-permute-done.27 = bf16[32,2560]{1,0:T(8,128)(2,1)S(1)} collective-permute-done((bf16[32,2560]{1,0:T(8,128)(2,1)S(1)}, bf16[32,2560]{1,0:T(8,128)(2,1)S(1)}, u32[]{:S(2)}, u32[]{:S(2)}) %collective-permute-start.27) | collective-permute-done | bytes 163872 | tf_op jit(solution)/shard_map/ppermute | solution.py:64
  122.6 2.8 %collective-permute-start.28 = (bf16[32,2560]{1,0:T(8,128)(2,1)S(1)}, bf16[32,2560]{1,0:T(8,128)(2,1)S(1)}, u32[]{:S(2)}, u32[]{:S(2)}) collective-permute-start(bf16[32,2560]{1,0:T(8,128)(2,1)S(1)} %add_convert_fusion.6), channel_id=1, source_target_pairs={{0,4},{2,6},{4,0},{6,2},{1,5},{3,7},{5,1},{7,3},{8,12},{10,14},{12... | collective-permute-start | bytes 491528 | tf_op jit(solution)/shard_map/ppermute | solution.py:64
  125.4 4.2 %collective-permute-done.29 = bf16[128,1792]{1,0:T(8,128)(2,1)S(1)} collective-permute-done((bf16[128,1792]{1,0:T(8,128)(2,1)S(1)}, bf16[128,1792]{1,0:T(8,128)(2,1)S(1)}, u32[]{:S(2)}, u32[]{:S(2)}) %collective-permute-start.29) | collective-permute-done | bytes 458784 | tf_op jit(solution)/shard_map/ppermute | solution.py:64
  134.2 1.7 %collective-permute-start.31 = (bf16[32,2560]{1,0:T(8,128)(2,1)S(1)}, bf16[32,2560]{1,0:T(8,128)(2,1)S(1)}, u32[]{:S(2)}, u32[]{:S(2)}) collective-permute-start(bf16[32,2560]{1,0:T(8,128)(2,1)S(1)} %get-tuple-element.77), channel_id=1, source_target_pairs={{0,2},{2,0},{4,6},{6,4},{1,3},{3,1},{5,7},{7,5},{8,10},{10,8},{12,... | collective-permute-start | bytes 491528 | tf_op jit(solution)/shard_map/ppermute | solution.py:64
  135.8 4.2 %collective-permute-done.32 = bf16[32,2560]{1,0:T(8,128)(2,1)S(1)} collective-permute-done((bf16[32,2560]{1,0:T(8,128)(2,1)S(1)}, bf16[32,2560]{1,0:T(8,128)(2,1)S(1)}, u32[]{:S(2)}, u32[]{:S(2)}) %collective-permute-start.32) | collective-permute-done | bytes 163872 | tf_op jit(solution)/shard_map/ppermute | solution.py:64
  141.3 2.3 %collective-permute-done.31 = bf16[32,2560]{1,0:T(8,128)(2,1)S(1)} collective-permute-done((bf16[32,2560]{1,0:T(8,128)(2,1)S(1)}, bf16[32,2560]{1,0:T(8,128)(2,1)S(1)}, u32[]{:S(2)}, u32[]{:S(2)}) %collective-permute-start.31) | collective-permute-done | bytes 163872 | tf_op jit(solution)/shard_map/ppermute | solution.py:64
  143.5 4.6 %collective-permute-done.33 = bf16[32,2560]{1,0:T(8,128)(2,1)S(1)} collective-permute-done((bf16[32,2560]{1,0:T(8,128)(2,1)S(1)}, bf16[32,2560]{1,0:T(8,128)(2,1)S(1)}, u32[]{:S(2)}, u32[]{:S(2)}) %collective-permute-start.33) | collective-permute-done | bytes 163872 | tf_op jit(solution)/shard_map/ppermute | solution.py:64
  148.9 1.7 %collective-permute-start.35 = (bf16[32,1280]{1,0:T(8,128)(2,1)S(1)}, bf16[32,1280]{1,0:T(8,128)(2,1)S(1)}, u32[]{:S(2)}, u32[]{:S(2)}) collective-permute-start(bf16[32,1280]{1,0:T(8,128)(2,1)S(1)} %get-tuple-element.84), channel_id=1, source_target_pairs={{0,8},{8,0},{16,24},{24,16},{1,9},{9,1},{17,25},{25,17},{2,10},{10... | collective-permute-start | bytes 245768 | tf_op jit(solution)/shard_map/ppermute | solution.py:64
  150.6 2.2 %collective-permute-done.34.refs_5_ = bf16[32,1280]{1,0:T(8,128)(2,1)S(1)} collective-permute-done((bf16[32,1280]{1,0:T(8,128)(2,1)S(1)}, bf16[32,1280]{1,0:T(8,128)(2,1)S(1)}, u32[]{:S(2)}, u32[]{:S(2)}) %collective-permute-start.34) | collective-permute-done | bytes 81952 | tf_op jit(solution)/shard_map/ppermute | solution.py:64
  153.3 1.4 finish.1
  (131 shorter events, 37.5 us)
Async XLA Ops:
  0.6 9.4 %collective-permute-start.1 = (bf16[256,5120]{1,0:T(8,128)(2,1)}, bf16[256,5120]{1,0:T(8,128)(2,1)S(1)}, u32[]{:S(2)}, u32[]{:S(2)}) collective-permute-start(bf16[256,5120]{1,0:T(8,128)(2,1)} %wa.3), channel_id=1, source_target_pairs={{0,1},{1,0},{2,3},{3,2},{4,5},{5,4},{6,7},{7,6},{8,9},{9,8},{10,11... | collective-permute-start | bytes 7864328 | tf_op jit(solution)/shard_map/ppermute | solution.py:64
  12.0 15.0 %collective-permute-start.4 = (bf16[32,5120]{1,0:T(8,128)(2,1)S(1)}, bf16[32,5120]{1,0:T(8,128)(2,1)S(1)}, u32[]{:S(2)}, u32[]{:S(2)}) collective-permute-start(bf16[32,5120]{1,0:T(8,128)(2,1)S(1)} %project.2), channel_id=1, source_target_pairs={{0,2},{2,0},{4,6},{6,4},{1,3},{3,1},{5,7},{7,5},{8,10},{10,8},{12,... | collective-permute-start | bytes 983048 | tf_op jit(solution)/shard_map/ppermute | solution.py:64
  21.4 27.6 %collective-permute-start.7 = (bf16[896,640]{1,0:T(8,128)(2,1)S(1)}, bf16[896,640]{1,0:T(8,128)(2,1)S(1)}, u32[]{:S(2)}, u32[]{:S(2)}) collective-permute-start(bf16[896,640]{1,0:T(8,128)(2,1)S(1)} %get-tuple-element.75), channel_id=1, source_target_pairs={{0,16},{8,24},{16,0},{24,8},{1,17},{9,25},{17,1},{25,9},{2,18},{10... | collective-permute-start | bytes 3440648 | tf_op jit(solution)/shard_map/ppermute | solution.py:64
  23.1 27.2 %collective-permute-start.6 = (bf16[896,640]{1,0:T(8,128)(2,1)S(1)}, bf16[896,640]{1,0:T(8,128)(2,1)S(1)}, u32[]{:S(2)}, u32[]{:S(2)}) collective-permute-start(bf16[896,640]{1,0:T(8,128)(2,1)S(1)} %get-tuple-element.76), channel_id=1, source_target_pairs={{0,8},{8,0},{16,24},{24,16},{1,9},{9,1},{17,25},{25,17},{2,10},{10... | collective-permute-start | bytes 3440648 | tf_op jit(solution)/shard_map/ppermute | solution.py:64
  26.5 16.6 %collective-permute-start.3 = (bf16[32,5120]{1,0:T(8,128)(2,1)S(1)}, bf16[32,5120]{1,0:T(8,128)(2,1)S(1)}, u32[]{:S(2)}, u32[]{:S(2)}) collective-permute-start(bf16[32,5120]{1,0:T(8,128)(2,1)S(1)} %get-tuple-element.49), channel_id=1, source_target_pairs={{0,2},{2,0},{4,6},{6,4},{1,3},{3,1},{5,7},{7,5},{8,10},{10,8},{12,... | collective-permute-start | bytes 983048 | tf_op jit(solution)/shard_map/ppermute | solution.py:64
  27.1 16.0 %collective-permute-start.5 = (bf16[32,5120]{1,0:T(8,128)(2,1)S(1)}, bf16[32,5120]{1,0:T(8,128)(2,1)S(1)}, u32[]{:S(2)}, u32[]{:S(2)}) collective-permute-start(bf16[32,5120]{1,0:T(8,128)(2,1)S(1)} %add_convert_fusion.2), channel_id=1, source_target_pairs={{0,4},{2,6},{4,0},{6,2},{1,5},{3,7},{5,1},{7,3},{8,12},{10,14},{12... | collective-permute-start | bytes 983048 | tf_op jit(solution)/shard_map/ppermute | solution.py:64
  29.7 47.6 %collective-permute-start.16 = (bf16[1280,896]{1,0:T(8,128)(2,1)S(1)}, bf16[1280,896]{1,0:T(8,128)(2,1)S(1)}, u32[]{:S(2)}, u32[]{:S(2)}) collective-permute-start(bf16[1280,896]{1,0:T(8,128)(2,1)S(1)} %copy-done.8), channel_id=1, source_target_pairs={{0,1},{1,0},{2,3},{3,2},{4,5},{5,4},{6,7},{7,6},{8,9},{9,8},{10,11... | collective-permute-start | bytes 6881288 | tf_op jit(solution)/shard_map/ppermute | solution.py:64
  43.1 35.5 %collective-permute-start.15 = (bf16[1280,896]{1,0:T(8,128)(2,1)S(1)}, bf16[1280,896]{1,0:T(8,128)(2,1)S(1)}, u32[]{:S(2)}, u32[]{:S(2)}) collective-permute-start(bf16[1280,896]{1,0:T(8,128)(2,1)S(1)} %copy-done.9), channel_id=1, source_target_pairs={{0,1},{1,0},{2,3},{3,2},{4,5},{5,4},{6,7},{7,6},{8,9},{9,8},{10,11... | collective-permute-start | bytes 6881288 | tf_op jit(solution)/shard_map/ppermute | solution.py:64
  50.2 4.4 %collective-permute-start.8 = (bf16[32,1280]{1,0:T(8,128)(2,1)S(1)}, bf16[32,1280]{1,0:T(8,128)(2,1)S(1)}, u32[]{:S(2)}, u32[]{:S(2)}) collective-permute-start(bf16[32,1280]{1,0:T(8,128)(2,1)S(1)} %get-tuple-element.54), channel_id=1, source_target_pairs={{0,8},{8,0},{16,24},{24,16},{1,9},{9,1},{17,25},{25,17},{2,10},{10... | collective-permute-start | bytes 245768 | tf_op jit(solution)/shard_map/ppermute | solution.py:64
  51.9 4.6 %collective-permute-start.9 = (bf16[32,1280]{1,0:T(8,128)(2,1)S(1)}, bf16[32,1280]{1,0:T(8,128)(2,1)S(1)}, u32[]{:S(2)}, u32[]{:S(2)}) collective-permute-start(bf16[32,1280]{1,0:T(8,128)(2,1)S(1)} %get-tuple-element.56), channel_id=1, source_target_pairs={{0,16},{8,24},{16,0},{24,8},{1,17},{9,25},{17,1},{25,9},{2,18},{10... | collective-permute-start | bytes 245768 | tf_op jit(solution)/shard_map/ppermute | solution.py:64
  52.2 5.3 %collective-permute-start.10 = (bf16[32,1280]{1,0:T(8,128)(2,1)S(1)}, bf16[32,1280]{1,0:T(8,128)(2,1)S(1)}, u32[]{:S(2)}, u32[]{:S(2)}) collective-permute-start(bf16[32,1280]{1,0:T(8,128)(2,1)S(1)} %get-tuple-element.58), channel_id=1, source_target_pairs={{0,24},{8,16},{16,8},{24,0},{1,25},{9,17},{17,9},{25,1},{2,26},{10... | collective-permute-start | bytes 245768 | tf_op jit(solution)/shard_map/ppermute | solution.py:64
  57.6 15.6 %collective-permute-start.11 = (bf16[4,32,1280]{2,1,0:T(8,128)(2,1)S(1)}, bf16[4,32,1280]{2,1,0:T(8,128)(2,1)S(1)}, u32[]{:S(2)}, u32[]{:S(2)}) collective-permute-start(bf16[4,32,1280]{2,1,0:T(8,128)(2,1)S(1)} %pad_maximum_fusion.8), channel_id=1, source_target_pairs={{0,4},{2,6},{4,0},{6,2},{1,5},{3,7},{5,1},{7,3},{8,12},{10,14},{12... | collective-permute-start | bytes 983048 | tf_op jit(solution)/shard_map/ppermute | solution.py:64
  60.3 14.2 %collective-permute-start.12 = (bf16[4,32,1280]{2,1,0:T(8,128)(2,1)S(1)}, bf16[4,32,1280]{2,1,0:T(8,128)(2,1)S(1)}, u32[]{:S(2)}, u32[]{:S(2)}) collective-permute-start(bf16[4,32,1280]{2,1,0:T(8,128)(2,1)S(1)} %pad_maximum_fusion.8), channel_id=1, source_target_pairs={{0,2},{2,0},{4,6},{6,4},{1,3},{3,1},{5,7},{7,5},{8,10},{10,8},{12,... | collective-permute-start | bytes 983048 | tf_op jit(solution)/shard_map/ppermute | solution.py:64
  74.5 8.3 %collective-permute-start.14 = (bf16[4,32,1280]{2,1,0:T(8,128)(2,1)S(1)}, bf16[4,32,1280]{2,1,0:T(8,128)(2,1)S(1)}, u32[]{:S(2)}, u32[]{:S(2)}) collective-permute-start(bf16[4,32,1280]{2,1,0:T(8,128)(2,1)S(1)} %collective-permute-done.11), channel_id=1, source_target_pairs={{0,2},{2,0},{4,6},{6,4},{1,3},{3,1},{5,7},{7,5},{8,10},{10,8},{12,... | collective-permute-start | bytes 983048 | tf_op jit(solution)/shard_map/ppermute | solution.py:64
  80.2 18.1 %collective-permute-start.13 = (bf16[2,3,32,1792]{3,2,0,1:T(8,128)(2,1)S(1)}, bf16[2,3,32,1792]{3,2,0,1:T(8,128)(2,1)S(1)}, u32[]{:S(2)}, u32[]{:S(2)}) collective-permute-start(bf16[2,3,32,1792]{3,2,0,1:T(8,128)(2,1)S(1)} %slice.93), channel_id=1, source_target_pairs={{0,8},{8,0},{16,24},{24,16},{1,9},{9,1},{17,25},{25,17},{2,10},{10... | collective-permute-start | bytes 2064392 | tf_op jit(solution)/shard_map/ppermute | solution.py:64
  81.3 17.8 %collective-permute-start.19 = (bf16[2,3,32,1792]{3,2,1,0:T(8,128)(2,1)S(1)}, bf16[2,3,32,1792]{3,2,1,0:T(8,128)(2,1)S(1)}, u32[]{:S(2)}, u32[]{:S(2)}) collective-permute-start(bf16[2,3,32,1792]{3,2,1,0:T(8,128)(2,1)S(1)} %slice.120), channel_id=1, source_target_pairs={{0,16},{8,24},{16,0},{24,8},{1,17},{9,25},{17,1},{25,9},{2,18},{10... | collective-permute-start | bytes 2064392 | tf_op jit(solution)/shard_map/ppermute | solution.py:64
  83.9 16.8 %collective-permute-start.17 = (bf16[2,1,32,1792]{3,2,0,1:T(8,128)(2,1)S(1)}, bf16[2,1,32,1792]{3,2,0,1:T(8,128)(2,1)S(1)}, u32[]{:S(2)}, u32[]{:S(2)}) collective-permute-start(bf16[2,1,32,1792]{3,2,0,1:T(8,128)(2,1)S(1)} %slice.95), channel_id=1, source_target_pairs={{0,8},{8,0},{16,24},{24,16},{1,9},{9,1},{17,25},{25,17},{2,10},{10... | collective-permute-start | bytes 688136 | tf_op jit(solution)/shard_map/ppermute | solution.py:64
  86.1 15.5 %collective-permute-start.18 = (bf16[2,1,32,1792]{3,2,1,0:T(8,128)(2,1)S(1)}, bf16[2,1,32,1792]{3,2,1,0:T(8,128)(2,1)S(1)}, u32[]{:S(2)}, u32[]{:S(2)}) collective-permute-start(bf16[2,1,32,1792]{3,2,1,0:T(8,128)(2,1)S(1)} %bitcast.116), channel_id=1, source_target_pairs={{0,16},{8,24},{16,0},{24,8},{1,17},{9,25},{17,1},{25,9},{2,18},{10... | collective-permute-start | bytes 688136 | tf_op jit(solution)/shard_map/ppermute | solution.py:64
  101.8 9.6 %collective-permute-start.20 = (bf16[4,32,1792]{2,1,0:T(8,128)(2,1)S(1)}, bf16[4,32,1792]{2,1,0:T(8,128)(2,1)S(1)}, u32[]{:S(2)}, u32[]{:S(2)}) collective-permute-start(bf16[4,32,1792]{2,1,0:T(8,128)(2,1)S(1)} %fusion.15), channel_id=1, source_target_pairs={{0,16},{8,24},{16,0},{24,8},{1,17},{9,25},{17,1},{25,9},{2,18},{10... | collective-permute-start | bytes 1376264 | tf_op jit(solution)/shard_map/ppermute | solution.py:64
  103.2 9.1 %collective-permute-start.21 = (bf16[4,32,1792]{2,1,0:T(8,128)(2,1)S(1)}, bf16[4,32,1792]{2,1,0:T(8,128)(2,1)S(1)}, u32[]{:S(2)}, u32[]{:S(2)}) collective-permute-start(bf16[4,32,1792]{2,1,0:T(8,128)(2,1)S(1)} %fusion.9), channel_id=1, source_target_pairs={{0,8},{8,0},{16,24},{24,16},{1,9},{9,1},{17,25},{25,17},{2,10},{10... | collective-permute-start | bytes 1376264 | tf_op jit(solution)/shard_map/ppermute | solution.py:64
  104.6 10.5 %collective-permute-start.23 = (bf16[896,640]{1,0:T(8,128)(2,1)S(1)}, bf16[896,640]{1,0:T(8,128)(2,1)S(1)}, u32[]{:S(2)}, u32[]{:S(2)}) collective-permute-start(bf16[896,640]{1,0:T(8,128)(2,1)S(1)} %get-tuple-element.75), channel_id=1, source_target_pairs={{0,1},{1,0},{2,3},{3,2},{4,5},{5,4},{6,7},{7,6},{8,9},{9,8},{10,11... | collective-permute-start | bytes 3440648 | tf_op jit(solution)/shard_map/ppermute | solution.py:64
  104.6 11.0 %collective-permute-start.22 = (bf16[896,640]{1,0:T(8,128)(2,1)S(1)}, bf16[896,640]{1,0:T(8,128)(2,1)S(1)}, u32[]{:S(2)}, u32[]{:S(2)}) collective-permute-start(bf16[896,640]{1,0:T(8,128)(2,1)S(1)} %get-tuple-element.76), channel_id=1, source_target_pairs={{0,1},{1,0},{2,3},{3,2},{4,5},{5,4},{6,7},{7,6},{8,9},{9,8},{10,11... | collective-permute-start | bytes 3440648 | tf_op jit(solution)/shard_map/ppermute | solution.py:64
  105.1 9.2 %collective-permute-start.25 = (bf16[896,640]{1,0:T(8,128)(2,1)S(1)}, bf16[896,640]{1,0:T(8,128)(2,1)S(1)}, u32[]{:S(2)}, u32[]{:S(2)}) collective-permute-start(bf16[896,640]{1,0:T(8,128)(2,1)S(1)} %collective-permute-done.7), channel_id=1, source_target_pairs={{0,1},{1,0},{2,3},{3,2},{4,5},{5,4},{6,7},{7,6},{8,9},{9,8},{10,11... | collective-permute-start | bytes 3440648 | tf_op jit(solution)/shard_map/ppermute | solution.py:64
  116.0 6.6 %collective-permute-start.27 = (bf16[32,2560]{1,0:T(8,128)(2,1)S(1)}, bf16[32,2560]{1,0:T(8,128)(2,1)S(1)}, u32[]{:S(2)}, u32[]{:S(2)}) collective-permute-start(bf16[32,2560]{1,0:T(8,128)(2,1)S(1)} %get-tuple-element.79), channel_id=1, source_target_pairs={{0,2},{2,0},{4,6},{6,4},{1,3},{3,1},{5,7},{7,5},{8,10},{10,8},{12,... | collective-permute-start | bytes 491528 | tf_op jit(solution)/shard_map/ppermute | solution.py:64
  118.0 11.7 %collective-permute-start.29 = (bf16[128,1792]{1,0:T(8,128)(2,1)S(1)}, bf16[128,1792]{1,0:T(8,128)(2,1)S(1)}, u32[]{:S(2)}, u32[]{:S(2)}) collective-permute-start(bf16[128,1792]{1,0:T(8,128)(2,1)S(1)} %bitcast.95), channel_id=1, source_target_pairs={{0,16},{8,24},{16,0},{24,8},{1,17},{9,25},{17,1},{25,9},{2,18},{10... | collective-permute-start | bytes 1376264 | tf_op jit(solution)/shard_map/ppermute | solution.py:64
  118.8 11.7 %collective-permute-start.30 = (bf16[128,1792]{1,0:T(8,128)(2,1)S(1)}, bf16[128,1792]{1,0:T(8,128)(2,1)S(1)}, u32[]{:S(2)}, u32[]{:S(2)}) collective-permute-start(bf16[128,1792]{1,0:T(8,128)(2,1)S(1)} %bitcast.96), channel_id=1, source_target_pairs={{0,8},{8,0},{16,24},{24,16},{1,9},{9,1},{17,25},{25,17},{2,10},{10... | collective-permute-start | bytes 1376264 | tf_op jit(solution)/shard_map/ppermute | solution.py:64
  119.8 13.9 %collective-permute-start.26 = (bf16[32,2560]{1,0:T(8,128)(2,1)S(1)}, bf16[32,2560]{1,0:T(8,128)(2,1)S(1)}, u32[]{:S(2)}, u32[]{:S(2)}) collective-permute-start(bf16[32,2560]{1,0:T(8,128)(2,1)S(1)} %get-tuple-element.80), channel_id=1, source_target_pairs={{0,2},{2,0},{4,6},{6,4},{1,3},{3,1},{5,7},{7,5},{8,10},{10,8},{12,... | collective-permute-start | bytes 491528 | tf_op jit(solution)/shard_map/ppermute | solution.py:64
  122.6 11.1 %collective-permute-start.28 = (bf16[32,2560]{1,0:T(8,128)(2,1)S(1)}, bf16[32,2560]{1,0:T(8,128)(2,1)S(1)}, u32[]{:S(2)}, u32[]{:S(2)}) collective-permute-start(bf16[32,2560]{1,0:T(8,128)(2,1)S(1)} %add_convert_fusion.6), channel_id=1, source_target_pairs={{0,4},{2,6},{4,0},{6,2},{1,5},{3,7},{5,1},{7,3},{8,12},{10,14},{12... | collective-permute-start | bytes 491528 | tf_op jit(solution)/shard_map/ppermute | solution.py:64
  133.8 6.3 %collective-permute-start.32 = (bf16[32,2560]{1,0:T(8,128)(2,1)S(1)}, bf16[32,2560]{1,0:T(8,128)(2,1)S(1)}, u32[]{:S(2)}, u32[]{:S(2)}) collective-permute-start(bf16[32,2560]{1,0:T(8,128)(2,1)S(1)} %get-tuple-element.72), channel_id=1, source_target_pairs={{0,2},{2,0},{4,6},{6,4},{1,3},{3,1},{5,7},{7,5},{8,10},{10,8},{12,... | collective-permute-start | bytes 491528 | tf_op jit(solution)/shard_map/ppermute | solution.py:64
  134.2 9.4 %collective-permute-start.31 = (bf16[32,2560]{1,0:T(8,128)(2,1)S(1)}, bf16[32,2560]{1,0:T(8,128)(2,1)S(1)}, u32[]{:S(2)}, u32[]{:S(2)}) collective-permute-start(bf16[32,2560]{1,0:T(8,128)(2,1)S(1)} %get-tuple-element.77), channel_id=1, source_target_pairs={{0,2},{2,0},{4,6},{6,4},{1,3},{3,1},{5,7},{7,5},{8,10},{10,8},{12,... | collective-permute-start | bytes 491528 | tf_op jit(solution)/shard_map/ppermute | solution.py:64
  140.1 8.0 %collective-permute-start.33 = (bf16[32,2560]{1,0:T(8,128)(2,1)S(1)}, bf16[32,2560]{1,0:T(8,128)(2,1)S(1)}, u32[]{:S(2)}, u32[]{:S(2)}) collective-permute-start(bf16[32,2560]{1,0:T(8,128)(2,1)S(1)} %add_convert_fusion.5), channel_id=1, source_target_pairs={{0,4},{2,6},{4,0},{6,2},{1,5},{3,7},{5,1},{7,3},{8,12},{10,14},{12... | collective-permute-start | bytes 491528 | tf_op jit(solution)/shard_map/ppermute | solution.py:64
  148.2 4.5 %collective-permute-start.34 = (bf16[32,1280]{1,0:T(8,128)(2,1)S(1)}, bf16[32,1280]{1,0:T(8,128)(2,1)S(1)}, u32[]{:S(2)}, u32[]{:S(2)}) collective-permute-start(bf16[32,1280]{1,0:T(8,128)(2,1)S(1)} %get-tuple-element.85), channel_id=1, source_target_pairs={{0,16},{8,24},{16,0},{24,8},{1,17},{9,25},{17,1},{25,9},{2,18},{10... | collective-permute-start | bytes 245768 | tf_op jit(solution)/shard_map/ppermute | solution.py:64
  (16 other events, 90.1 us)

commit v6 on v5

--- a/solution.py
+++ b/solution.py
@@ -479,7 +479,7 @@
             terms[0] = after(terms[0], *held)
         resid, *pieces = norm_cut(scal, x_resid[c * step:(c + 1) * step], terms, gain, reqs)
         resids.append(resid)
-        pieces[1:] = [after(piece, *lent) for piece in pieces[1:]]
+        pieces[-1] = after(pieces[-1], *lent)
         got = jnp.stack(trade(pieces, "req", True))
         two, one = bind(True, swap(got, "kv", 2), swap(got, "kv", 1))
         three = swap(two, "kv", 1)

time: 155 us -> 155 us (level)
  waiting for transfers between devices: 81.1 us -> 84.1 us
  starting transfers between devices: 37 us -> 34.1 us
    ppermute x36, starting transfers between devices: 37 us -> 34.1 us  [swap(): lax.ppermute(a, axis, [(i, i ^ mask) for i in range(lax.axis_size(axis))])]
    ppermute x36, waiting for transfers between devices: 81.1 us -> 84.1 us  [swap(): lax.ppermute(a, axis, [(i, i ^ mask) for i in range(lax.axis_size(axis))])]
  transfers between devices with their start and end apart: 36 -> 36, of which waited for: 24 -> 23; matrix products, arithmetic and copies ran while one was open for 10% -> 10% of each run, Pallas kernels for 10% -> 10%
where the time goes in v6:
time: 155 us; the launch traced here: 154 us
  waiting for transfers between devices  84.1 us (54%)
  starting transfers between devices  34.1 us (22%)
  Pallas kernels  18.3 us (12%)
  matrix products  12.9 us (8%)
  other arithmetic  2.3 us (1%)
  between operations  1.97 us (1%)
    ppermute x36, waiting for transfers between devices, swap(): lax.ppermute(a, axis, [(i, i ^ mask) for i in range(lax.axis_size(axis))])  84.1 us
    ppermute x36, starting transfers between devices, swap(): lax.ppermute(a, axis, [(i, i ^ mask) for i in range(lax.axis_size(axis))])  34.1 us
    dot_general x8, matrix products, partial_gate_up(): jnp.dot(flat, w, preferred_element_type=F32).astype(BF16)  6.81 us
    pallas_call x1, Pallas kernels, attend_next(): pl.pallas_call(functools.partial(attention_body, (first_m, count, rows, 1...  6.62 us
    pallas_call x4, Pallas kernels, direct(): pl.pallas_call(body, in_specs=[SMEM] * len(scalars) + [VMEM] * len(arrays...  5.92 us
    pallas_call x1, Pallas kernels, staged(): pl.pallas_call(kernel, in_specs=[SMEM] * len(scalars) + [HBM] * count, ou...  5.74 us
  transfers between devices with their start and end apart: 36, of which 23 were waited for; matrix products, arithmetic and copies ran while one was open for 10% of the time, Pallas kernels for 10%

profile of v6, /device:TPU:0, one launch (start us, length us, event | category | flops | bytes accessed | tf_op | source)
XLA Modules:
  0.0 154.5 jit_solution(3553310709593674204)
XLA Ops:
  2.5 5.7 %attend_first.1 = (bf16[32,128,128]{2,1,0:T(8,128)(2,1)}, bf16[32,128,128]{2,1,0:T(8,128)(2,1)}, bf16[256,512]{1,0:T(8,128)(2,1)}, s32[1,4096]{1,0:T(1,128)}, bf...) custom-call(s32[4]{0:T(128)} %pad_add_fusion.refs_0_.scal, s32[1,64]{1,0:T(1,128)} %refs_1_.1, ...), custom_call_target="tpu_custom_call" | custom-call | tf_op jit(solution)/shard_map/attend_first/pallas_call | solution.py:39
  10.1 1.8 %project.2 = bf16[32,5120]{1,0:T(8,128)(2,1)S(1)} custom-call(s32[4]{0:T(128)S(1)} %copy-done.3, bf16[32,640]{1,0:T(8,128)(2,1)S(1)} %copy-done.2, bf16[32,640]{1,0:T(8,128)(2,1)S(1)} %collective-permute-done.o2, bf16[256,5120]{1,0:T(8,128)(2,1)S(1)} %copy-done, bf16[256,5120]{1,0:T(8,128)(2,1)S(1)} %collective-permute-done.1.wb), custom_call_target="tpu_custom_call" | custom-call | tf_op jit(solution)/shard_map/project/pallas_call | solution.py:52
  11.8 2.8 %collective-permute-start.4 = (bf16[32,5120]{1,0:T(8,128)(2,1)S(1)}, bf16[32,5120]{1,0:T(8,128)(2,1)S(1)}, u32[]{:S(2)}, u32[]{:S(2)}) collective-permute-start(bf16[32,5120]{1,0:T(8,128)(2,1)S(1)} %project.2), channel_id=1, source_target_pairs={{0,2},{2,0},{4,6},{6,4},{1,3},{3,1},{5,7},{7,5},{8,10},{10,8},{12,... | collective-permute-start | bytes 983048 | tf_op jit(solution)/shard_map/ppermute | solution.py:64
  14.6 6.6 %attend_next.1 = (bf16[96,640]{1,0:T(8,128)(2,1)S(1)}, bf16[96,640]{1,0:T(8,128)(2,1)S(1)}) custom-call(s32[4]{0:T(128)S(1)} %copy-done.3, bf16[32,128,128]{2,1,0:T(8,128)(2,1)S(1)} %copy-done.4, bf16[32,128,128]{2,1,0:T(8,128)(2,1)S(1)} %copy-done.5, bf16[256,512]{1,0:T(8,128)(2,1)S(1)} %copy-done.6, s32[1,4096]{1,0:T(1,128)S(1)} %copy-done.7), custom_call_target="tpu_custom_call" | custom-call | flops 8000000000 | bytes 1000000 | tf_op jit(solution)/shard_map/attend_next/pallas_call | solution.py:246
  21.5 1.5 collective-permute-start.9
  24.5 1.8 %project.3 = (bf16[32,5120]{1,0:T(8,128)(2,1)S(1)}, bf16[32,5120]{1,0:T(8,128)(2,1)S(1)}, bf16[32,5120]{1,0:T(8,128)(2,1)S(1)}) custom-call(s32[4]{0:T(128)S(1)} %copy-done.3, bf16[96,640]{1,0:T(8,128)(2,1)S(1)} %get-tuple-element.44.o1, bf16[96,640]{1,0:T(8,128)(2,1)S(1)} %collective-permute-done.2.o2, bf16[256,5120]{1,0:T(8,128)(2,1)S(1)} %copy-done, ...), custom_call_target="tpu_custom_call" | custom-call | tf_op jit(solution)/shard_map/project/pallas_call | solution.py:52
  26.9 2.7 %collective-permute-start.5 = (bf16[32,5120]{1,0:T(8,128)(2,1)S(1)}, bf16[32,5120]{1,0:T(8,128)(2,1)S(1)}, u32[]{:S(2)}, u32[]{:S(2)}) collective-permute-start(bf16[32,5120]{1,0:T(8,128)(2,1)S(1)} %add_convert_fusion.2), channel_id=1, source_target_pairs={{0,4},{2,6},{4,0},{6,2},{1,5},{3,7},{5,1},{7,3},{8,12},{10,14},{12... | collective-permute-start | bytes 983048 | tf_op jit(solution)/shard_map/ppermute | solution.py:64
  29.6 13.3 %collective-permute-done.3.rest_1_ = bf16[32,5120]{1,0:T(8,128)(2,1)S(1)} collective-permute-done((bf16[32,5120]{1,0:T(8,128)(2,1)S(1)}, bf16[32,5120]{1,0:T(8,128)(2,1)S(1)}, u32[]{:S(2)}, u32[]{:S(2)}) %collective-permute-start.3) | collective-permute-done | bytes 327712 | tf_op jit(solution)/shard_map/ppermute | solution.py:64
  44.4 4.6 %collective-permute-done.9 = bf16[896,640]{1,0:T(8,128)(2,1)S(1)} collective-permute-done((bf16[896,640]{1,0:T(8,128)(2,1)S(1)}, bf16[896,640]{1,0:T(8,128)(2,1)S(1)}, u32[]{:S(2)}, u32[]{:S(2)}) %collective-permute-start.9) | collective-permute-done | bytes 1146912 | tf_op jit(solution)/shard_map/ppermute | solution.py:64
  49.0 1.5 collective-permute-start.7
  52.4 1.9 %collective-permute-done.7 = bf16[32,1280]{1,0:T(8,128)(2,1)S(1)} collective-permute-done((bf16[32,1280]{1,0:T(8,128)(2,1)S(1)}, bf16[32,1280]{1,0:T(8,128)(2,1)S(1)}, u32[]{:S(2)}, u32[]{:S(2)}) %collective-permute-start.7) | collective-permute-done | bytes 81952 | tf_op jit(solution)/shard_map/ppermute | solution.py:64
  54.3 2.1 %collective-permute-done.10 = bf16[32,1280]{1,0:T(8,128)(2,1)S(1)} collective-permute-done((bf16[32,1280]{1,0:T(8,128)(2,1)S(1)}, bf16[32,1280]{1,0:T(8,128)(2,1)S(1)}, u32[]{:S(2)}, u32[]{:S(2)}) %collective-permute-start.10) | collective-permute-done | bytes 81952 | tf_op jit(solution)/shard_map/ppermute | solution.py:64
  56.5 2.6 %collective-permute-start.11 = (bf16[4,32,1280]{2,1,0:T(8,128)(2,1)S(1)}, bf16[4,32,1280]{2,1,0:T(8,128)(2,1)S(1)}, u32[]{:S(2)}, u32[]{:S(2)}) collective-permute-start(bf16[4,32,1280]{2,1,0:T(8,128)(2,1)S(1)} %pad_maximum_fusion.8), channel_id=1, source_target_pairs={{0,4},{2,6},{4,0},{6,2},{1,5},{3,7},{5,1},{7,3},{8,12},{10,14},{12... | collective-permute-start | bytes 983048 | tf_op jit(solution)/shard_map/ppermute | solution.py:64
  59.6 11.9 %collective-permute-done.11 = bf16[4,32,1280]{2,1,0:T(8,128)(2,1)S(1)} collective-permute-done((bf16[4,32,1280]{2,1,0:T(8,128)(2,1)S(1)}, bf16[4,32,1280]{2,1,0:T(8,128)(2,1)S(1)}, u32[]{:S(2)}, u32[]{:S(2)}) %collective-permute-start.11) | collective-permute-done | bytes 327712 | tf_op jit(solution)/shard_map/ppermute | solution.py:64
  78.6 1.7 %collective-permute-start.13 = (bf16[2,3,32,1792]{3,2,0,1:T(8,128)(2,1)S(1)}, bf16[2,3,32,1792]{3,2,0,1:T(8,128)(2,1)S(1)}, u32[]{:S(2)}, u32[]{:S(2)}) collective-permute-start(bf16[2,3,32,1792]{3,2,0,1:T(8,128)(2,1)S(1)} %slice.93), channel_id=1, source_target_pairs={{0,8},{8,0},{16,24},{24,16},{1,9},{9,1},{17,25},{25,17},{2,10},{10... | collective-permute-start | bytes 2064392 | tf_op jit(solution)/shard_map/ppermute | solution.py:64
  82.3 1.8 %collective-permute-start.17 = (bf16[2,1,32,1792]{3,2,0,1:T(8,128)(2,1)S(1)}, bf16[2,1,32,1792]{3,2,0,1:T(8,128)(2,1)S(1)}, u32[]{:S(2)}, u32[]{:S(2)}) collective-permute-start(bf16[2,1,32,1792]{3,2,0,1:T(8,128)(2,1)S(1)} %slice.95), channel_id=1, source_target_pairs={{0,8},{8,0},{16,24},{24,16},{1,9},{9,1},{17,25},{25,17},{2,10},{10... | collective-permute-start | bytes 688136 | tf_op jit(solution)/shard_map/ppermute | solution.py:64
  85.5 11.1 %collective-permute-done.13 = bf16[2,3,32,1792]{3,2,0,1:T(8,128)(2,1)S(1)} collective-permute-done((bf16[2,3,32,1792]{3,2,0,1:T(8,128)(2,1)S(1)}, bf16[2,3,32,1792]{3,2,0,1:T(8,128)(2,1)S(1)}, u32[]{:S(2)}, u32[]{:S(2)}) %collective-permute-start.13) | collective-permute-done | bytes 688160 | tf_op jit(solution)/shard_map/ppermute | solution.py:64
  99.1 1.7 %collective-permute-done.18 = bf16[2,1,32,1792]{3,2,1,0:T(8,128)(2,1)S(1)} collective-permute-done((bf16[2,1,32,1792]{3,2,1,0:T(8,128)(2,1)S(1)}, bf16[2,1,32,1792]{3,2,1,0:T(8,128)(2,1)S(1)}, u32[]{:S(2)}, u32[]{:S(2)}) %collective-permute-start.18) | collective-permute-done | bytes 229408 | tf_op jit(solution)/shard_map/ppermute | solution.py:64
  102.5 7.9 %collective-permute-done.20 = bf16[4,32,1792]{2,1,0:T(8,128)(2,1)S(1)} collective-permute-done((bf16[4,32,1792]{2,1,0:T(8,128)(2,1)S(1)}, bf16[4,32,1792]{2,1,0:T(8,128)(2,1)S(1)}, u32[]{:S(2)}, u32[]{:S(2)}) %collective-permute-start.20) | collective-permute-done | bytes 458784 | tf_op jit(solution)/shard_map/ppermute | solution.py:64
  114.5 1.8 %collective-permute-start.27 = (bf16[32,2560]{1,0:T(8,128)(2,1)S(1)}, bf16[32,2560]{1,0:T(8,128)(2,1)S(1)}, u32[]{:S(2)}, u32[]{:S(2)}) collective-permute-start(bf16[32,2560]{1,0:T(8,128)(2,1)S(1)} %get-tuple-element.75), channel_id=1, source_target_pairs={{0,2},{2,0},{4,6},{6,4},{1,3},{3,1},{5,7},{7,5},{8,10},{10,8},{12,... | collective-permute-start | bytes 491528 | tf_op jit(solution)/shard_map/ppermute | solution.py:64
  116.4 1.5 collective-permute-start.29
  118.5 3.1 %collective-permute-done.27 = bf16[32,2560]{1,0:T(8,128)(2,1)S(1)} collective-permute-done((bf16[32,2560]{1,0:T(8,128)(2,1)S(1)}, bf16[32,2560]{1,0:T(8,128)(2,1)S(1)}, u32[]{:S(2)}, u32[]{:S(2)}) %collective-permute-start.27) | collective-permute-done | bytes 163872 | tf_op jit(solution)/shard_map/ppermute | solution.py:64
  121.7 2.2 %collective-permute-start.28 = (bf16[32,2560]{1,0:T(8,128)(2,1)S(1)}, bf16[32,2560]{1,0:T(8,128)(2,1)S(1)}, u32[]{:S(2)}, u32[]{:S(2)}) collective-permute-start(bf16[32,2560]{1,0:T(8,128)(2,1)S(1)} %add_convert_fusion.6), channel_id=1, source_target_pairs={{0,4},{2,6},{4,0},{6,2},{1,5},{3,7},{5,1},{7,3},{8,12},{10,14},{12... | collective-permute-start | bytes 491528 | tf_op jit(solution)/shard_map/ppermute | solution.py:64
  123.8 4.9 %collective-permute-done.29 = bf16[128,1792]{1,0:T(8,128)(2,1)S(1)} collective-permute-done((bf16[128,1792]{1,0:T(8,128)(2,1)S(1)}, bf16[128,1792]{1,0:T(8,128)(2,1)S(1)}, u32[]{:S(2)}, u32[]{:S(2)}) %collective-permute-start.29) | collective-permute-done | bytes 458784 | tf_op jit(solution)/shard_map/ppermute | solution.py:64
  132.4 1.7 %collective-permute-start.31 = (bf16[32,2560]{1,0:T(8,128)(2,1)S(1)}, bf16[32,2560]{1,0:T(8,128)(2,1)S(1)}, u32[]{:S(2)}, u32[]{:S(2)}) collective-permute-start(bf16[32,2560]{1,0:T(8,128)(2,1)S(1)} %get-tuple-element.73), channel_id=1, source_target_pairs={{0,2},{2,0},{4,6},{6,4},{1,3},{3,1},{5,7},{7,5},{8,10},{10,8},{12,... | collective-permute-start | bytes 491528 | tf_op jit(solution)/shard_map/ppermute | solution.py:64
  134.1 4.8 %collective-permute-done.32 = bf16[32,2560]{1,0:T(8,128)(2,1)S(1)} collective-permute-done((bf16[32,2560]{1,0:T(8,128)(2,1)S(1)}, bf16[32,2560]{1,0:T(8,128)(2,1)S(1)}, u32[]{:S(2)}, u32[]{:S(2)}) %collective-permute-start.32) | collective-permute-done | bytes 163872 | tf_op jit(solution)/shard_map/ppermute | solution.py:64
  140.2 2.2 %collective-permute-done.31 = bf16[32,2560]{1,0:T(8,128)(2,1)S(1)} collective-permute-done((bf16[32,2560]{1,0:T(8,128)(2,1)S(1)}, bf16[32,2560]{1,0:T(8,128)(2,1)S(1)}, u32[]{:S(2)}, u32[]{:S(2)}) %collective-permute-start.31) | collective-permute-done | bytes 163872 | tf_op jit(solution)/shard_map/ppermute | solution.py:64
  142.4 4.6 %collective-permute-done.33 = bf16[32,2560]{1,0:T(8,128)(2,1)S(1)} collective-permute-done((bf16[32,2560]{1,0:T(8,128)(2,1)S(1)}, bf16[32,2560]{1,0:T(8,128)(2,1)S(1)}, u32[]{:S(2)}, u32[]{:S(2)}) %collective-permute-start.33) | collective-permute-done | bytes 163872 | tf_op jit(solution)/shard_map/ppermute | solution.py:64
  147.1 1.6 %collective-permute-start.34 = (bf16[32,1280]{1,0:T(8,128)(2,1)S(1)}, bf16[32,1280]{1,0:T(8,128)(2,1)S(1)}, u32[]{:S(2)}, u32[]{:S(2)}) collective-permute-start(bf16[32,1280]{1,0:T(8,128)(2,1)S(1)} %get-tuple-element.81), channel_id=1, source_target_pairs={{0,16},{8,24},{16,0},{24,8},{1,17},{9,25},{17,1},{25,9},{2,18},{10... | collective-permute-start | bytes 245768 | tf_op jit(solution)/shard_map/ppermute | solution.py:64
  148.9 2.6 %collective-permute-done.34.refs_5_ = bf16[32,1280]{1,0:T(8,128)(2,1)S(1)} collective-permute-done((bf16[32,1280]{1,0:T(8,128)(2,1)S(1)}, bf16[32,1280]{1,0:T(8,128)(2,1)S(1)}, u32[]{:S(2)}, u32[]{:S(2)}) %collective-permute-start.34) | collective-permute-done | bytes 81952 | tf_op jit(solution)/shard_map/ppermute | solution.py:64
  151.6 1.5 collective-permute-done.35.refs_4_
  153.1 1.4 finish.1
  (131 shorter events, 33.6 us)
Async XLA Ops:
  0.6 9.2 %collective-permute-start.1 = (bf16[256,5120]{1,0:T(8,128)(2,1)}, bf16[256,5120]{1,0:T(8,128)(2,1)S(1)}, u32[]{:S(2)}, u32[]{:S(2)}) collective-permute-start(bf16[256,5120]{1,0:T(8,128)(2,1)} %wa.3), channel_id=1, source_target_pairs={{0,1},{1,0},{2,3},{3,2},{4,5},{5,4},{6,7},{7,6},{8,9},{9,8},{10,11... | collective-permute-start | bytes 7864328 | tf_op jit(solution)/shard_map/ppermute | solution.py:64
  11.8 15.0 %collective-permute-start.4 = (bf16[32,5120]{1,0:T(8,128)(2,1)S(1)}, bf16[32,5120]{1,0:T(8,128)(2,1)S(1)}, u32[]{:S(2)}, u32[]{:S(2)}) collective-permute-start(bf16[32,5120]{1,0:T(8,128)(2,1)S(1)} %project.2), channel_id=1, source_target_pairs={{0,2},{2,0},{4,6},{6,4},{1,3},{3,1},{5,7},{7,5},{8,10},{10,8},{12,... | collective-permute-start | bytes 983048 | tf_op jit(solution)/shard_map/ppermute | solution.py:64
  21.5 27.4 %collective-permute-start.9 = (bf16[896,640]{1,0:T(8,128)(2,1)S(1)}, bf16[896,640]{1,0:T(8,128)(2,1)S(1)}, u32[]{:S(2)}, u32[]{:S(2)}) collective-permute-start(bf16[896,640]{1,0:T(8,128)(2,1)S(1)} %get-tuple-element.71), channel_id=1, source_target_pairs={{0,16},{8,24},{16,0},{24,8},{1,17},{9,25},{17,1},{25,9},{2,18},{10... | collective-permute-start | bytes 3440648 | tf_op jit(solution)/shard_map/ppermute | solution.py:64
  23.1 28.0 %collective-permute-start.8 = (bf16[896,640]{1,0:T(8,128)(2,1)S(1)}, bf16[896,640]{1,0:T(8,128)(2,1)S(1)}, u32[]{:S(2)}, u32[]{:S(2)}) collective-permute-start(bf16[896,640]{1,0:T(8,128)(2,1)S(1)} %get-tuple-element.72), channel_id=1, source_target_pairs={{0,8},{8,0},{16,24},{24,16},{1,9},{9,1},{17,25},{25,17},{2,10},{10... | collective-permute-start | bytes 3440648 | tf_op jit(solution)/shard_map/ppermute | solution.py:64
  26.3 16.6 %collective-permute-start.3 = (bf16[32,5120]{1,0:T(8,128)(2,1)S(1)}, bf16[32,5120]{1,0:T(8,128)(2,1)S(1)}, u32[]{:S(2)}, u32[]{:S(2)}) collective-permute-start(bf16[32,5120]{1,0:T(8,128)(2,1)S(1)} %get-tuple-element.47), channel_id=1, source_target_pairs={{0,2},{2,0},{4,6},{6,4},{1,3},{3,1},{5,7},{7,5},{8,10},{10,8},{12,... | collective-permute-start | bytes 983048 | tf_op jit(solution)/shard_map/ppermute | solution.py:64
  26.9 16.0 %collective-permute-start.5 = (bf16[32,5120]{1,0:T(8,128)(2,1)S(1)}, bf16[32,5120]{1,0:T(8,128)(2,1)S(1)}, u32[]{:S(2)}, u32[]{:S(2)}) collective-permute-start(bf16[32,5120]{1,0:T(8,128)(2,1)S(1)} %add_convert_fusion.2), channel_id=1, source_target_pairs={{0,4},{2,6},{4,0},{6,2},{1,5},{3,7},{5,1},{7,3},{8,12},{10,14},{12... | collective-permute-start | bytes 983048 | tf_op jit(solution)/shard_map/ppermute | solution.py:64
  29.6 46.2 %collective-permute-start.16 = (bf16[1280,896]{1,0:T(8,128)(2,1)S(1)}, bf16[1280,896]{1,0:T(8,128)(2,1)S(1)}, u32[]{:S(2)}, u32[]{:S(2)}) collective-permute-start(bf16[1280,896]{1,0:T(8,128)(2,1)S(1)} %copy-done.8), channel_id=1, source_target_pairs={{0,1},{1,0},{2,3},{3,2},{4,5},{5,4},{6,7},{7,6},{8,9},{9,8},{10,11... | collective-permute-start | bytes 6881288 | tf_op jit(solution)/shard_map/ppermute | solution.py:64
  42.9 34.1 %collective-permute-start.15 = (bf16[1280,896]{1,0:T(8,128)(2,1)S(1)}, bf16[1280,896]{1,0:T(8,128)(2,1)S(1)}, u32[]{:S(2)}, u32[]{:S(2)}) collective-permute-start(bf16[1280,896]{1,0:T(8,128)(2,1)S(1)} %copy-done.9), channel_id=1, source_target_pairs={{0,1},{1,0},{2,3},{3,2},{4,5},{5,4},{6,7},{7,6},{8,9},{9,8},{10,11... | collective-permute-start | bytes 6881288 | tf_op jit(solution)/shard_map/ppermute | solution.py:64
  43.9 8.5 %collective-permute-start.6 = (bf16[32,1280]{1,0:T(8,128)(2,1)S(1)}, bf16[32,1280]{1,0:T(8,128)(2,1)S(1)}, u32[]{:S(2)}, u32[]{:S(2)}) collective-permute-start(bf16[32,1280]{1,0:T(8,128)(2,1)S(1)} %get-tuple-element.51), channel_id=1, source_target_pairs={{0,8},{8,0},{16,24},{24,16},{1,9},{9,1},{17,25},{25,17},{2,10},{10... | collective-permute-start | bytes 245768 | tf_op jit(solution)/shard_map/ppermute | solution.py:64
  49.0 5.3 %collective-permute-start.7 = (bf16[32,1280]{1,0:T(8,128)(2,1)S(1)}, bf16[32,1280]{1,0:T(8,128)(2,1)S(1)}, u32[]{:S(2)}, u32[]{:S(2)}) collective-permute-start(bf16[32,1280]{1,0:T(8,128)(2,1)S(1)} %get-tuple-element.52), channel_id=1, source_target_pairs={{0,16},{8,24},{16,0},{24,8},{1,17},{9,25},{17,1},{25,9},{2,18},{10... | collective-permute-start | bytes 245768 | tf_op jit(solution)/shard_map/ppermute | solution.py:64
  51.1 5.3 %collective-permute-start.10 = (bf16[32,1280]{1,0:T(8,128)(2,1)S(1)}, bf16[32,1280]{1,0:T(8,128)(2,1)S(1)}, u32[]{:S(2)}, u32[]{:S(2)}) collective-permute-start(bf16[32,1280]{1,0:T(8,128)(2,1)S(1)} %get-tuple-element.54), channel_id=1, source_target_pairs={{0,24},{8,16},{16,8},{24,0},{1,25},{9,17},{17,9},{25,1},{2,26},{10... | collective-permute-start | bytes 245768 | tf_op jit(solution)/shard_map/ppermute | solution.py:64
  56.5 15.1 %collective-permute-start.11 = (bf16[4,32,1280]{2,1,0:T(8,128)(2,1)S(1)}, bf16[4,32,1280]{2,1,0:T(8,128)(2,1)S(1)}, u32[]{:S(2)}, u32[]{:S(2)}) collective-permute-start(bf16[4,32,1280]{2,1,0:T(8,128)(2,1)S(1)} %pad_maximum_fusion.8), channel_id=1, source_target_pairs={{0,4},{2,6},{4,0},{6,2},{1,5},{3,7},{5,1},{7,3},{8,12},{10,14},{12... | collective-permute-start | bytes 983048 | tf_op jit(solution)/shard_map/ppermute | solution.py:64
  59.1 13.8 %collective-permute-start.12 = (bf16[4,32,1280]{2,1,0:T(8,128)(2,1)S(1)}, bf16[4,32,1280]{2,1,0:T(8,128)(2,1)S(1)}, u32[]{:S(2)}, u32[]{:S(2)}) collective-permute-start(bf16[4,32,1280]{2,1,0:T(8,128)(2,1)S(1)} %pad_maximum_fusion.8), channel_id=1, source_target_pairs={{0,2},{2,0},{4,6},{6,4},{1,3},{3,1},{5,7},{7,5},{8,10},{10,8},{12,... | collective-permute-start | bytes 983048 | tf_op jit(solution)/shard_map/ppermute | solution.py:64
  72.9 8.2 %collective-permute-start.14 = (bf16[4,32,1280]{2,1,0:T(8,128)(2,1)S(1)}, bf16[4,32,1280]{2,1,0:T(8,128)(2,1)S(1)}, u32[]{:S(2)}, u32[]{:S(2)}) collective-permute-start(bf16[4,32,1280]{2,1,0:T(8,128)(2,1)S(1)} %collective-permute-done.11), channel_id=1, source_target_pairs={{0,2},{2,0},{4,6},{6,4},{1,3},{3,1},{5,7},{7,5},{8,10},{10,8},{12,... | collective-permute-start | bytes 983048 | tf_op jit(solution)/shard_map/ppermute | solution.py:64
  78.6 18.1 %collective-permute-start.13 = (bf16[2,3,32,1792]{3,2,0,1:T(8,128)(2,1)S(1)}, bf16[2,3,32,1792]{3,2,0,1:T(8,128)(2,1)S(1)}, u32[]{:S(2)}, u32[]{:S(2)}) collective-permute-start(bf16[2,3,32,1792]{3,2,0,1:T(8,128)(2,1)S(1)} %slice.93), channel_id=1, source_target_pairs={{0,8},{8,0},{16,24},{24,16},{1,9},{9,1},{17,25},{25,17},{2,10},{10... | collective-permute-start | bytes 2064392 | tf_op jit(solution)/shard_map/ppermute | solution.py:64
  80.3 17.8 %collective-permute-start.19 = (bf16[2,3,32,1792]{3,2,1,0:T(8,128)(2,1)S(1)}, bf16[2,3,32,1792]{3,2,1,0:T(8,128)(2,1)S(1)}, u32[]{:S(2)}, u32[]{:S(2)}) collective-permute-start(bf16[2,3,32,1792]{3,2,1,0:T(8,128)(2,1)S(1)} %slice.120), channel_id=1, source_target_pairs={{0,16},{8,24},{16,0},{24,8},{1,17},{9,25},{17,1},{25,9},{2,18},{10... | collective-permute-start | bytes 2064392 | tf_op jit(solution)/shard_map/ppermute | solution.py:64
  82.3 16.8 %collective-permute-start.17 = (bf16[2,1,32,1792]{3,2,0,1:T(8,128)(2,1)S(1)}, bf16[2,1,32,1792]{3,2,0,1:T(8,128)(2,1)S(1)}, u32[]{:S(2)}, u32[]{:S(2)}) collective-permute-start(bf16[2,1,32,1792]{3,2,0,1:T(8,128)(2,1)S(1)} %slice.95), channel_id=1, source_target_pairs={{0,8},{8,0},{16,24},{24,16},{1,9},{9,1},{17,25},{25,17},{2,10},{10... | collective-permute-start | bytes 688136 | tf_op jit(solution)/shard_map/ppermute | solution.py:64
  85.1 15.6 %collective-permute-start.18 = (bf16[2,1,32,1792]{3,2,1,0:T(8,128)(2,1)S(1)}, bf16[2,1,32,1792]{3,2,1,0:T(8,128)(2,1)S(1)}, u32[]{:S(2)}, u32[]{:S(2)}) collective-permute-start(bf16[2,1,32,1792]{3,2,1,0:T(8,128)(2,1)S(1)} %bitcast.116), channel_id=1, source_target_pairs={{0,16},{8,24},{16,0},{24,8},{1,17},{9,25},{17,1},{25,9},{2,18},{10... | collective-permute-start | bytes 688136 | tf_op jit(solution)/shard_map/ppermute | solution.py:64
  100.9 9.6 %collective-permute-start.20 = (bf16[4,32,1792]{2,1,0:T(8,128)(2,1)S(1)}, bf16[4,32,1792]{2,1,0:T(8,128)(2,1)S(1)}, u32[]{:S(2)}, u32[]{:S(2)}) collective-permute-start(bf16[4,32,1792]{2,1,0:T(8,128)(2,1)S(1)} %fusion.15), channel_id=1, source_target_pairs={{0,16},{8,24},{16,0},{24,8},{1,17},{9,25},{17,1},{25,9},{2,18},{10... | collective-permute-start | bytes 1376264 | tf_op jit(solution)/shard_map/ppermute | solution.py:64
  101.4 9.1 %collective-permute-start.21 = (bf16[4,32,1792]{2,1,0:T(8,128)(2,1)S(1)}, bf16[4,32,1792]{2,1,0:T(8,128)(2,1)S(1)}, u32[]{:S(2)}, u32[]{:S(2)}) collective-permute-start(bf16[4,32,1792]{2,1,0:T(8,128)(2,1)S(1)} %fusion.9), channel_id=1, source_target_pairs={{0,8},{8,0},{16,24},{24,16},{1,9},{9,1},{17,25},{25,17},{2,10},{10... | collective-permute-start | bytes 1376264 | tf_op jit(solution)/shard_map/ppermute | solution.py:64
  102.0 11.6 %collective-permute-start.23 = (bf16[896,640]{1,0:T(8,128)(2,1)S(1)}, bf16[896,640]{1,0:T(8,128)(2,1)S(1)}, u32[]{:S(2)}, u32[]{:S(2)}) collective-permute-start(bf16[896,640]{1,0:T(8,128)(2,1)S(1)} %get-tuple-element.71), channel_id=1, source_target_pairs={{0,1},{1,0},{2,3},{3,2},{4,5},{5,4},{6,7},{7,6},{8,9},{9,8},{10,11... | collective-permute-start | bytes 3440648 | tf_op jit(solution)/shard_map/ppermute | solution.py:64
  102.0 12.0 %collective-permute-start.22 = (bf16[896,640]{1,0:T(8,128)(2,1)S(1)}, bf16[896,640]{1,0:T(8,128)(2,1)S(1)}, u32[]{:S(2)}, u32[]{:S(2)}) collective-permute-start(bf16[896,640]{1,0:T(8,128)(2,1)S(1)} %get-tuple-element.72), channel_id=1, source_target_pairs={{0,1},{1,0},{2,3},{3,2},{4,5},{5,4},{6,7},{7,6},{8,9},{9,8},{10,11... | collective-permute-start | bytes 3440648 | tf_op jit(solution)/shard_map/ppermute | solution.py:64
  102.5 10.0 %collective-permute-start.25 = (bf16[896,640]{1,0:T(8,128)(2,1)S(1)}, bf16[896,640]{1,0:T(8,128)(2,1)S(1)}, u32[]{:S(2)}, u32[]{:S(2)}) collective-permute-start(bf16[896,640]{1,0:T(8,128)(2,1)S(1)} %collective-permute-done.9), channel_id=1, source_target_pairs={{0,1},{1,0},{2,3},{3,2},{4,5},{5,4},{6,7},{7,6},{8,9},{9,8},{10,11... | collective-permute-start | bytes 3440648 | tf_op jit(solution)/shard_map/ppermute | solution.py:64
  114.5 7.1 %collective-permute-start.27 = (bf16[32,2560]{1,0:T(8,128)(2,1)S(1)}, bf16[32,2560]{1,0:T(8,128)(2,1)S(1)}, u32[]{:S(2)}, u32[]{:S(2)}) collective-permute-start(bf16[32,2560]{1,0:T(8,128)(2,1)S(1)} %get-tuple-element.75), channel_id=1, source_target_pairs={{0,2},{2,0},{4,6},{6,4},{1,3},{3,1},{5,7},{7,5},{8,10},{10,8},{12,... | collective-permute-start | bytes 491528 | tf_op jit(solution)/shard_map/ppermute | solution.py:64
  116.4 12.3 %collective-permute-start.29 = (bf16[128,1792]{1,0:T(8,128)(2,1)S(1)}, bf16[128,1792]{1,0:T(8,128)(2,1)S(1)}, u32[]{:S(2)}, u32[]{:S(2)}) collective-permute-start(bf16[128,1792]{1,0:T(8,128)(2,1)S(1)} %bitcast.95), channel_id=1, source_target_pairs={{0,16},{8,24},{16,0},{24,8},{1,17},{9,25},{17,1},{25,9},{2,18},{10... | collective-permute-start | bytes 1376264 | tf_op jit(solution)/shard_map/ppermute | solution.py:64
  117.9 10.9 %collective-permute-start.30 = (bf16[128,1792]{1,0:T(8,128)(2,1)S(1)}, bf16[128,1792]{1,0:T(8,128)(2,1)S(1)}, u32[]{:S(2)}, u32[]{:S(2)}) collective-permute-start(bf16[128,1792]{1,0:T(8,128)(2,1)S(1)} %bitcast.96), channel_id=1, source_target_pairs={{0,8},{8,0},{16,24},{24,16},{1,9},{9,1},{17,25},{25,17},{2,10},{10... | collective-permute-start | bytes 1376264 | tf_op jit(solution)/shard_map/ppermute | solution.py:64
  118.4 13.6 %collective-permute-start.26 = (bf16[32,2560]{1,0:T(8,128)(2,1)S(1)}, bf16[32,2560]{1,0:T(8,128)(2,1)S(1)}, u32[]{:S(2)}, u32[]{:S(2)}) collective-permute-start(bf16[32,2560]{1,0:T(8,128)(2,1)S(1)} %get-tuple-element.76), channel_id=1, source_target_pairs={{0,2},{2,0},{4,6},{6,4},{1,3},{3,1},{5,7},{7,5},{8,10},{10,8},{12,... | collective-permute-start | bytes 491528 | tf_op jit(solution)/shard_map/ppermute | solution.py:64
  121.7 10.3 %collective-permute-start.28 = (bf16[32,2560]{1,0:T(8,128)(2,1)S(1)}, bf16[32,2560]{1,0:T(8,128)(2,1)S(1)}, u32[]{:S(2)}, u32[]{:S(2)}) collective-permute-start(bf16[32,2560]{1,0:T(8,128)(2,1)S(1)} %add_convert_fusion.6), channel_id=1, source_target_pairs={{0,4},{2,6},{4,0},{6,2},{1,5},{3,7},{5,1},{7,3},{8,12},{10,14},{12... | collective-permute-start | bytes 491528 | tf_op jit(solution)/shard_map/ppermute | solution.py:64
  132.0 6.9 %collective-permute-start.32 = (bf16[32,2560]{1,0:T(8,128)(2,1)S(1)}, bf16[32,2560]{1,0:T(8,128)(2,1)S(1)}, u32[]{:S(2)}, u32[]{:S(2)}) collective-permute-start(bf16[32,2560]{1,0:T(8,128)(2,1)S(1)} %get-tuple-element.68), channel_id=1, source_target_pairs={{0,2},{2,0},{4,6},{6,4},{1,3},{3,1},{5,7},{7,5},{8,10},{10,8},{12,... | collective-permute-start | bytes 491528 | tf_op jit(solution)/shard_map/ppermute | solution.py:64
  132.4 10.0 %collective-permute-start.31 = (bf16[32,2560]{1,0:T(8,128)(2,1)S(1)}, bf16[32,2560]{1,0:T(8,128)(2,1)S(1)}, u32[]{:S(2)}, u32[]{:S(2)}) collective-permute-start(bf16[32,2560]{1,0:T(8,128)(2,1)S(1)} %get-tuple-element.73), channel_id=1, source_target_pairs={{0,2},{2,0},{4,6},{6,4},{1,3},{3,1},{5,7},{7,5},{8,10},{10,8},{12,... | collective-permute-start | bytes 491528 | tf_op jit(solution)/shard_map/ppermute | solution.py:64
  138.9 8.0 %collective-permute-start.33 = (bf16[32,2560]{1,0:T(8,128)(2,1)S(1)}, bf16[32,2560]{1,0:T(8,128)(2,1)S(1)}, u32[]{:S(2)}, u32[]{:S(2)}) collective-permute-start(bf16[32,2560]{1,0:T(8,128)(2,1)S(1)} %add_convert_fusion.5), channel_id=1, source_target_pairs={{0,4},{2,6},{4,0},{6,2},{1,5},{3,7},{5,1},{7,3},{8,12},{10,14},{12... | collective-permute-start | bytes 491528 | tf_op jit(solution)/shard_map/ppermute | solution.py:64
  147.1 4.5 %collective-permute-start.34 = (bf16[32,1280]{1,0:T(8,128)(2,1)S(1)}, bf16[32,1280]{1,0:T(8,128)(2,1)S(1)}, u32[]{:S(2)}, u32[]{:S(2)}) collective-permute-start(bf16[32,1280]{1,0:T(8,128)(2,1)S(1)} %get-tuple-element.81), channel_id=1, source_target_pairs={{0,16},{8,24},{16,0},{24,8},{1,17},{9,25},{17,1},{25,9},{2,18},{10... | collective-permute-start | bytes 245768 | tf_op jit(solution)/shard_map/ppermute | solution.py:64
  (16 other events, 90.0 us)
